TPU v7x, 32 devices: a whole 2x2x4 slice. The times are simulated.
32 devices in a mesh: client: 4 (over x, core), shard: 8 (over z, y).
Axes of the slice: x: 2, y: 2, z: 4, core: 2. Of those that a mesh axis runs over, the one named last changes fastest.
Arguments:
- token_ids: int32 [4, 8, 512], P('client', 'shard'), may hold values from 0 to 50303
- lengths: int32 [4, 8], P('client', 'shard'), may hold values from 1 to 512, as said below
- picked: int32 [4, 8, 128], P('client', 'shard'), may hold values from 0 to 510
- joining: int32 [4], replicated, may hold values from 0 to 1, as said below
- embedding: float32 [50304, 768], P(('client', 'shard')), may hold values from -0.4375 to 0.4375
- embedding_first: float32 [50304, 768], P(('client', 'shard')), may hold values from -1.5258789e-05 to 1.5258789e-05
- embedding_second: float32 [50304, 768], P(('client', 'shard')), may hold values from 6.679406e-13 to 1.0687049e-11
- position_table: float32 [1024, 768], P(('client', 'shard')), may hold values from -0.75 to 0.75
- position_first: float32 [1024, 768], P(('client', 'shard')), may hold values from -1.5258789e-05 to 1.5258789e-05
- position_second: float32 [1024, 768], P(('client', 'shard')), may hold values from 6.679406e-13 to 1.0687049e-11
- shared_wide: float32 [768, 6144], P(('client', 'shard')), may hold values from -0.21875 to 0.21875
- shared_wide_first: float32 [768, 6144], P(('client', 'shard')), may hold values from -1.5258789e-05 to 1.5258789e-05
- shared_wide_second: float32 [768, 6144], P(('client', 'shard')), may hold values from 6.679406e-13 to 1.0687049e-11
- shared_down: float32 [3072, 768], P(('client', 'shard')), may hold values from -0.109375 to 0.109375
- shared_down_first: float32 [3072, 768], P(('client', 'shard')), may hold values from -1.5258789e-05 to 1.5258789e-05
- shared_down_second: float32 [3072, 768], P(('client', 'shard')), may hold values from 6.679406e-13 to 1.0687049e-11
- shared_vectors: float32 [10752], P(('client', 'shard'))
- shared_vectors_first: float32 [10752], P(('client', 'shard')), may hold values from -6.1035156e-05 to 6.1035156e-05
- shared_vectors_second: float32 [10752], P(('client', 'shard')), may hold values from 1.0687049e-11 to 1.7099279e-10
- private_wide: float32 [4, 768, 6144], P('client', 'shard'), may hold values from -0.21875 to 0.21875
- private_wide_first: float32 [4, 768, 6144], P('client', 'shard'), may hold values from -1.5258789e-05 to 1.5258789e-05
- private_wide_second: float32 [4, 768, 6144], P('client', 'shard'), may hold values from 6.679406e-13 to 1.0687049e-11
- private_down: float32 [4, 3072, 768], P('client', 'shard'), may hold values from -0.109375 to 0.109375
- private_down_first: float32 [4, 3072, 768], P('client', 'shard'), may hold values from -1.5258789e-05 to 1.5258789e-05
- private_down_second: float32 [4, 3072, 768], P('client', 'shard'), may hold values from 6.679406e-13 to 1.0687049e-11
- private_vectors: float32 [4, 9216], P('client', 'shard')
- private_vectors_first: float32 [4, 9216], P('client', 'shard'), may hold values from -6.1035156e-05 to 6.1035156e-05
- private_vectors_second: float32 [4, 9216], P('client', 'shard'), may hold values from 1.0687049e-11 to 1.7099279e-10
Outputs:
- new_embedding: float32 [50304, 768], P(('client', 'shard'))
- new_embedding_first: float32 [50304, 768], P(('client', 'shard'))
- new_embedding_second: float32 [50304, 768], P(('client', 'shard'))
- new_position: float32 [1024, 768], P(('client', 'shard'))
- new_position_first: float32 [1024, 768], P(('client', 'shard'))
- new_position_second: float32 [1024, 768], P(('client', 'shard'))
- new_shared_wide: float32 [768, 6144], P(('client', 'shard'))
- new_shared_wide_first: float32 [768, 6144], P(('client', 'shard'))
- new_shared_wide_second: float32 [768, 6144], P(('client', 'shard'))
- new_shared_down: float32 [3072, 768], P(('client', 'shard'))
- new_shared_down_first: float32 [3072, 768], P(('client', 'shard'))
- new_shared_down_second: float32 [3072, 768], P(('client', 'shard'))
- new_shared_vectors: float32 [10752], P(('client', 'shard'))
- new_shared_vectors_first: float32 [10752], P(('client', 'shard'))
- new_shared_vectors_second: float32 [10752], P(('client', 'shard'))
- new_private_wide: float32 [4, 768, 6144], P('client', 'shard')
- new_private_wide_first: float32 [4, 768, 6144], P('client', 'shard')
- new_private_wide_second: float32 [4, 768, 6144], P('client', 'shard')
- new_private_down: float32 [4, 3072, 768], P('client', 'shard')
- new_private_down_first: float32 [4, 3072, 768], P('client', 'shard')
- new_private_down_second: float32 [4, 3072, 768], P('client', 'shard')
- new_private_vectors: float32 [4, 9216], P('client', 'shard')
- new_private_vectors_first: float32 [4, 9216], P('client', 'shard')
- new_private_vectors_second: float32 [4, 9216], P('client', 'shard')
- client_sums: float32 [4], P('client')
- client_counts: float32 [4], P('client')
- grad_norm: float32 [], replicated
Inputs may be any that keep to these rules, and one draw needn't show every extreme that they name: `lengths`: in every client some sequence has all 512 slots live. `joining`: at least two clients take part and at least one does not.
All inputs are finite; a program needn't handle non-finite values.
Results may differ from a plain program's by a relative error of at most 0.018.
Values may be sent and summed in bfloat16 or wider, within the bound.
No kernel may reach another device: no remote copies, remote signals or barrier semaphores. Data moves between devices by JAX's collectives and lax.ppermute only.
A program may use at most 448 MiB of HBM per device.

v0:
```python
import jax
import jax.numpy as jnp
from jax import lax
from jax.sharding import PartitionSpec as P

HD = 64
D = 768
FF = 3072
NPOS = 1024
STEP = 5


SCALE = 0.125
CLIP_NORM = 0.01
RATE_MATRIX = 0.03
RATE_VECTOR = 0.5
DECAY = 0.01
EPSILON = 1e-08


def merged(x, axis, join):
    gathered = jax.tree.map(
        lambda a, kind: lax.all_gather(a.astype(kind), axis),
        x,
        (jnp.bfloat16, jnp.bfloat16, jnp.bfloat16),
    )

    def take(source):
        return jax.tree.map(
            lambda a, own: lax.dynamic_index_in_dim(a, source, 0, False).astype(own.dtype),
            gathered,
            x,
        )

    return lax.fori_loop(
        1, lax.axis_size(axis), lambda source, state: join(state, take(source)), take(0)
    )


def dot_plain(former, latter):
    return jnp.dot(former, latter, preferred_element_type=jnp.float32)


def dot_inner(former, latter):
    return lax.dot_general(
        former, latter, (((0,), (0,)), ((), ())), preferred_element_type=jnp.float32
    )


def dot_outer(former, latter):
    return lax.dot_general(
        former, latter, (((1,), (1,)), ((), ())), preferred_element_type=jnp.float32
    )


def layer_norm(values, scales, shifts):
    centre = values - jnp.mean(values, -1, keepdims=True)
    spread = jnp.mean(centre * centre, -1, keepdims=True)
    return centre * lax.rsqrt(spread + 1e-05) * scales + shifts


def gelu_tanh(values):
    return jax.nn.gelu(values, approximate=True)


def split_vectors(vectors, breadth, hidden):
    starts = [
        0,
        breadth,
        2 * breadth,
        3 * breadth,
        4 * breadth,
        5 * breadth,
        6 * breadth,
        7 * breadth,
        7 * breadth + hidden,
        8 * breadth + hidden,
    ]
    return [vectors[starts[position] : starts[position + 1]] for position in range(9)]


def causal_mask(seq_len, live_len):
    rows_at = lax.broadcasted_iota(jnp.int32, (seq_len, seq_len), 0)
    cols_at = lax.broadcasted_iota(jnp.int32, (seq_len, seq_len), 1)
    return (cols_at <= rows_at) & (cols_at < live_len)


def masked_scores(block_qkv, seq_len, live_len):
    scores = (
        jnp.einsum(
            "qhd,khd->hqk", block_qkv[:, 0], block_qkv[:, 1], preferred_element_type=jnp.float32
        )
        * SCALE
    )
    return jnp.where(causal_mask(seq_len, live_len)[None], scores, -1e30)


def attend(joined, lengths):
    sequences = lengths.shape[0]
    breadth = joined.shape[1] // 3
    seq_len = joined.shape[0] // sequences
    blocks = joined.reshape(sequences, seq_len, 3, breadth // HD, HD)

    def single(operands):
        block_qkv, live_len = operands
        scores = masked_scores(block_qkv, seq_len, live_len)
        highest = jnp.max(scores, -1, keepdims=True)
        exponent = jnp.exp(scores - highest)
        totals = jnp.sum(exponent, -1, keepdims=True)
        probs_b = (exponent / totals).astype(jnp.bfloat16)
        mixed_out = jnp.einsum(
            "hqk,khd->qhd", probs_b, block_qkv[:, 2], preferred_element_type=jnp.float32
        )
        return (
            mixed_out.astype(jnp.bfloat16).reshape(seq_len, breadth),
            (highest + jnp.log(totals))[..., 0],
        )

    mixed_out, log_totals = lax.map(single, (blocks, lengths))
    return (mixed_out.reshape(-1, breadth), log_totals)


def attend_back(joined, log_totals, grad_mixed, lengths):
    sequences = lengths.shape[0]
    breadth = joined.shape[1] // 3
    seq_len = joined.shape[0] // sequences
    head_count = breadth // HD
    blocks = joined.reshape(sequences, seq_len, 3, head_count, HD)
    grad_blocks = grad_mixed.reshape(sequences, seq_len, head_count, HD)

    def single(operands):
        block_qkv, log_total, grad_out, live_len = operands
        scores = masked_scores(block_qkv, seq_len, live_len)
        probs = jnp.exp(scores - log_total[..., None])
        probs_b = probs.astype(jnp.bfloat16)
        grad_values = jnp.einsum(
            "hqk,qhd->khd", probs_b, grad_out, preferred_element_type=jnp.float32
        )
        grad_probs = jnp.einsum(
            "qhd,khd->hqk", grad_out, block_qkv[:, 2], preferred_element_type=jnp.float32
        )
        inner = jnp.sum(grad_probs * probs, -1, keepdims=True)
        grad_scores = (probs * (grad_probs - inner)).astype(jnp.bfloat16)
        grad_queries = (
            jnp.einsum(
                "hqk,khd->qhd", grad_scores, block_qkv[:, 1], preferred_element_type=jnp.float32
            )
            * SCALE
        )
        grad_keys = (
            jnp.einsum(
                "hqk,qhd->khd", grad_scores, block_qkv[:, 0], preferred_element_type=jnp.float32
            )
            * SCALE
        )
        stacked = jnp.stack([grad_queries, grad_keys, grad_values], 1).astype(jnp.bfloat16)
        return stacked.reshape(seq_len, 3 * breadth)

    return lax.map(single, (blocks, log_totals, grad_blocks, lengths)).reshape(-1, 3 * breadth)


def layer_forward(inputs, wide, down, vectors, lengths):
    breadth = inputs.shape[1]
    parts = split_vectors(vectors.astype(jnp.float32), breadth, down.shape[0])
    normed = layer_norm(inputs, parts[0], parts[1]).astype(jnp.bfloat16)
    shift_qkv = jnp.concatenate([parts[2], jnp.zeros_like(parts[2]), parts[3]])
    joined = (dot_plain(normed, wide[:, : 3 * breadth]) + shift_qkv).astype(jnp.bfloat16)
    mixed_out, log_totals = attend(joined, lengths)
    middle = inputs + (dot_plain(mixed_out, wide[:, 3 * breadth : 4 * breadth]) + parts[4])
    normed_two = layer_norm(middle, parts[5], parts[6]).astype(jnp.bfloat16)
    pre_act = dot_plain(normed_two, wide[:, 4 * breadth :]) + parts[7]
    activ = gelu_tanh(pre_act).astype(jnp.bfloat16)
    output = middle + (dot_plain(activ, down) + parts[8])
    return (
        output,
        (inputs, normed, joined, mixed_out, log_totals, middle, normed_two, pre_act, activ),
    )


def layer_backward(grad_out, saved, wide, down, vectors, lengths):
    inputs, normed, joined, mixed_out, log_totals, middle, normed_two, pre_act, activ = saved
    breadth = inputs.shape[1]
    parts = split_vectors(vectors.astype(jnp.float32), breadth, down.shape[0])
    grad_y = grad_out.astype(jnp.bfloat16)
    grad_down = dot_inner(activ, grad_y)
    grad_act = dot_outer(grad_y, down)
    grad_pre = jax.vjp(gelu_tanh, pre_act)[1](grad_act)[0].astype(jnp.bfloat16)
    grad_fc = dot_inner(normed_two, grad_pre)
    grad_norm_two = dot_outer(grad_pre, wide[:, 4 * breadth :])
    grad_mid_norm, grad_scale_two, grad_shift_two = jax.vjp(layer_norm, middle, parts[5], parts[6])[
        1
    ](grad_norm_two)
    grad_mid = grad_out + grad_mid_norm
    grad_branch = grad_mid.astype(jnp.bfloat16)
    grad_proj = dot_inner(mixed_out, grad_branch)
    grad_mixed = dot_outer(grad_branch, wide[:, 3 * breadth : 4 * breadth]).astype(jnp.bfloat16)
    grad_joined = attend_back(joined, log_totals, grad_mixed, lengths)
    grad_qkv = dot_inner(normed, grad_joined)
    grad_normed = dot_outer(grad_joined, wide[:, : 3 * breadth])
    grad_in_norm, grad_scale_one, grad_shift_one = jax.vjp(layer_norm, inputs, parts[0], parts[1])[
        1
    ](grad_normed)
    joined_sums = jnp.sum(grad_joined.astype(jnp.float32), 0)
    grad_vectors = jnp.concatenate(
        [
            grad_scale_one,
            grad_shift_one,
            joined_sums[:breadth],
            joined_sums[2 * breadth :],
            jnp.sum(grad_branch.astype(jnp.float32), 0),
            grad_scale_two,
            grad_shift_two,
            jnp.sum(grad_pre.astype(jnp.float32), 0),
            jnp.sum(grad_y.astype(jnp.float32), 0),
        ]
    )
    grad_wide = jnp.concatenate([grad_qkv, grad_proj, grad_fc], 1)
    return (grad_mid + grad_in_norm, grad_wide, grad_down, grad_vectors)


def adamw(weight, first, second, gradient, rate, decay):
    first_new = 0.5 * first + 0.5 * gradient
    second_new = 0.5 * second + 0.5 * gradient * gradient
    first_hat = first_new / (1.0 - 0.5**STEP)
    second_hat = second_new / (1.0 - 0.5**STEP)
    weight_new = weight - rate * (first_hat / (jnp.sqrt(second_hat) + EPSILON) + decay * weight)
    return (weight_new, first_new, second_new)


def combine_parts(former, latter):
    top = jnp.maximum(former[0], latter[0])
    total = former[1] * jnp.exp(former[0] - top) + latter[1] * jnp.exp(latter[0] - top)
    return (top, total, former[2] + latter[2])


def per_device(
    token_ids,
    lengths,
    picked,
    joining,
    embedding,
    embedding_first,
    embedding_second,
    position_table,
    position_first,
    position_second,
    shared_wide,
    shared_wide_first,
    shared_wide_second,
    shared_down,
    shared_down_first,
    shared_down_second,
    shared_vectors,
    shared_vectors_first,
    shared_vectors_second,
    private_wide,
    private_wide_first,
    private_wide_second,
    private_down,
    private_down_first,
    private_down_second,
    private_vectors,
    private_vectors_first,
    private_vectors_second,
):
    table_b, posit_b, wide_s, down_s, vect_s = (
        lax.all_gather(embedding.astype(jnp.bfloat16), ("client", "shard"), axis=0, tiled=True),
        lax.all_gather(
            position_table.astype(jnp.bfloat16), ("client", "shard"), axis=0, tiled=True
        ),
        lax.all_gather(shared_wide.astype(jnp.bfloat16), ("client", "shard"), axis=0, tiled=True),
        lax.all_gather(shared_down.astype(jnp.bfloat16), ("client", "shard"), axis=0, tiled=True),
        lax.all_gather(
            shared_vectors.astype(jnp.bfloat16), ("client", "shard"), axis=0, tiled=True
        ),
    )
    wide_p, down_p, vect_p = (
        lax.all_gather(private_wide.astype(jnp.bfloat16), "shard", axis=1, tiled=True),
        lax.all_gather(private_down.astype(jnp.bfloat16), "shard", axis=1, tiled=True),
        lax.all_gather(private_vectors.astype(jnp.bfloat16), "shard", axis=1, tiled=True),
    )
    wide_p, down_p, vect_p = (wide_p[0], down_p[0], vect_p[0])
    ids_group, picks_group, lens_group = (
        lax.all_gather(token_ids, "shard", axis=1, tiled=True),
        lax.all_gather(picked, "shard", axis=1, tiled=True),
        lax.all_gather(lengths, "shard", axis=1, tiled=True),
    )
    ids_group, picks_group, lens_group = (ids_group[0], picks_group[0], lens_group[0])
    clients = lax.axis_size("client")
    shards = lax.axis_size("shard")
    own_client = lax.axis_index("client")
    device_at = own_client * shards + lax.axis_index("shard")
    joined_total = jnp.sum(joining).astype(jnp.float32)
    count_sum = jnp.sum((picks_group < lens_group[:, None] - 1).astype(jnp.float32))
    sequences = lengths.shape[1]
    seq_len = token_ids.shape[2]
    id_rows = token_ids[0].reshape(-1)
    seq_lengths = lengths[0]
    inputs = jnp.take(table_b, id_rows, axis=0).astype(jnp.float32)
    inputs = inputs + jnp.tile(posit_b[:seq_len].astype(jnp.float32), (sequences, 1))
    first_out, first_saved = layer_forward(inputs, wide_p, down_p, vect_p, seq_lengths)
    second_out, second_saved = layer_forward(first_out, wide_s, down_s, vect_s, seq_lengths)
    final_scale = vect_s[8 * D + FF : 9 * D + FF].astype(jnp.float32)
    final_shift = vect_s[9 * D + FF : 10 * D + FF].astype(jnp.float32)
    row_index = (jnp.arange(sequences, dtype=jnp.int32)[:, None] * seq_len + picked[0]).reshape(-1)
    own_rows = row_index.shape[0]
    live = (picked[0] < seq_lengths[:, None] - 1).reshape(-1)
    targets = jnp.take(id_rows, row_index + 1)
    final_in = jnp.take(second_out, row_index, axis=0)
    final_b = layer_norm(final_in, final_scale, final_shift).astype(jnp.bfloat16)
    scored_all = lax.all_gather(final_b, ("client", "shard"), axis=0, tiled=True)
    targets_all, live_ints = (
        lax.all_gather(targets, ("client", "shard"), axis=0, tiled=True),
        lax.all_gather(live.astype(jnp.int32), ("client", "shard"), axis=0, tiled=True),
    )
    live_all = live_ints > 0
    counts_all = jnp.sum(live_ints.reshape(clients, -1).astype(jnp.float32), 1)
    share_all = joining.astype(jnp.float32) / (joined_total * counts_all)
    table_own = embedding.astype(jnp.bfloat16)
    slice_rows = table_own.shape[0]
    weight_all = jnp.where(
        live_all,
        jnp.broadcast_to(share_all[:, None], (clients, live_all.shape[0] // clients)).reshape(-1),
        0.0,
    )
    logits_own = dot_outer(scored_all, table_own)
    local_target = targets_all - device_at * slice_rows
    vocab_at = lax.broadcasted_iota(jnp.int32, logits_own.shape, 1)
    hit = vocab_at == local_target[:, None]
    part_max = jnp.max(logits_own, -1)
    part_sum = jnp.sum(jnp.exp(logits_own - part_max[:, None]), -1)
    part_target = jnp.sum(jnp.where(hit, logits_own, 0.0), -1)
    top, total, target_all = merged(
        (part_max, part_sum, part_target), ("client", "shard"), combine_parts
    )
    log_all = top + jnp.log(total)
    terms_all = jnp.where(live_all, log_all - target_all, 0.0)
    row_terms = lax.dynamic_slice_in_dim(terms_all, device_at * own_rows, own_rows, 0)
    grad_logits_own = (
        weight_all[:, None] * jnp.exp(logits_own - log_all[:, None])
        - jnp.where(hit, weight_all[:, None], 0.0)
    ).astype(jnp.bfloat16)
    head_table = dot_inner(grad_logits_own, scored_all)
    grad_final_b = lax.psum_scatter(
        dot_plain(grad_logits_own, table_own), ("client", "shard"), scatter_dimension=0, tiled=True
    )
    grad_final_in, grad_fscale, grad_fshift = jax.vjp(
        layer_norm, final_in, final_scale, final_shift
    )[1](grad_final_b)
    grad_second = jnp.zeros_like(second_out).at[row_index].add(grad_final_in)
    grad_first, grad_wide_s, grad_down_s, grad_vect_s = layer_backward(
        grad_second, second_saved, wide_s, down_s, vect_s, seq_lengths
    )
    grad_inputs, grad_wide_p, grad_down_p, grad_vect_p = layer_backward(
        grad_first, first_saved, wide_p, down_p, vect_p, seq_lengths
    )
    grad_vect_s = jnp.concatenate([grad_vect_s, grad_fscale, grad_fshift])
    position_sum = jnp.sum(grad_inputs.reshape(sequences, seq_len, -1), 0)
    grad_position = jnp.zeros((NPOS, D), jnp.float32).at[:seq_len].set(position_sum)
    gathered_grads = lax.all_gather(
        grad_inputs.astype(jnp.bfloat16), "shard", axis=0, tiled=True
    ).astype(grad_inputs.dtype)
    group_ids = ids_group.reshape(-1)
    owner = group_ids // slice_rows
    keep = owner % shards == lax.axis_index("shard")
    slots = jnp.where(
        keep, owner // shards * slice_rows + group_ids % slice_rows, clients * slice_rows
    )
    buffer = (
        jnp.zeros((clients * slice_rows, D), jnp.float32).at[slots].add(gathered_grads, mode="drop")
    )
    grad_table = head_table + lax.psum_scatter(
        buffer.astype(jnp.bfloat16), "client", scatter_dimension=0, tiled=True
    ).astype(jnp.float32)
    grad_wide_sh, grad_down_sh, grad_vect_sh, grad_posit_sh = (
        lax.psum_scatter(grad_wide_s, ("client", "shard"), scatter_dimension=0, tiled=True),
        lax.psum_scatter(grad_down_s, ("client", "shard"), scatter_dimension=0, tiled=True),
        lax.psum_scatter(grad_vect_s, ("client", "shard"), scatter_dimension=0, tiled=True),
        lax.psum_scatter(grad_position, ("client", "shard"), scatter_dimension=0, tiled=True),
    )
    grad_wide_ph, grad_down_ph, grad_vect_ph = (
        lax.psum_scatter(
            grad_wide_p[None].astype(jnp.bfloat16), "shard", scatter_dimension=1, tiled=True
        ).astype(jnp.float32),
        lax.psum_scatter(
            grad_down_p[None].astype(jnp.bfloat16), "shard", scatter_dimension=1, tiled=True
        ).astype(jnp.float32),
        lax.psum_scatter(
            grad_vect_p[None].astype(jnp.bfloat16), "shard", scatter_dimension=1, tiled=True
        ).astype(jnp.float32),
    )
    all_grads = [
        grad_table,
        grad_posit_sh,
        grad_wide_sh,
        grad_down_sh,
        grad_vect_sh,
        grad_wide_ph,
        grad_down_ph,
        grad_vect_ph,
    ]
    squares = jnp.zeros((), jnp.float32)
    for gradient in all_grads:
        squares = squares + jnp.sum(gradient * gradient)
    client_slot = lax.broadcasted_iota(jnp.int32, (clients,), 0) == own_client
    loss_vector = jnp.where(client_slot, jnp.sum(row_terms), 0.0)
    squares_all, loss_all = lax.psum((squares, loss_vector), ("client", "shard"))
    grad_norm = jnp.sqrt(squares_all)
    loss_sum = jnp.sum(jnp.where(client_slot, loss_all, 0.0))
    factor = jnp.minimum(1.0, CLIP_NORM / grad_norm)
    g_table, g_posit, g_wide_s, g_down_s, g_vect_s, g_wide_p, g_down_p, g_vect_p = [
        member * factor for member in all_grads
    ]
    emb_new, emb_first, emb_second = adamw(
        embedding, embedding_first, embedding_second, g_table, RATE_MATRIX, DECAY
    )
    pos_new, pos_first, pos_second = adamw(
        position_table, position_first, position_second, g_posit, RATE_MATRIX, DECAY
    )
    sw_new, sw_first, sw_second = adamw(
        shared_wide, shared_wide_first, shared_wide_second, g_wide_s, RATE_MATRIX, DECAY
    )
    sd_new, sd_first, sd_second = adamw(
        shared_down, shared_down_first, shared_down_second, g_down_s, RATE_MATRIX, DECAY
    )
    sv_new, sv_first, sv_second = adamw(
        shared_vectors, shared_vectors_first, shared_vectors_second, g_vect_s, RATE_VECTOR, 0.0
    )
    pw_new, pw_first, pw_second = adamw(
        private_wide, private_wide_first, private_wide_second, g_wide_p, RATE_MATRIX, DECAY
    )
    pd_new, pd_first, pd_second = adamw(
        private_down, private_down_first, private_down_second, g_down_p, RATE_MATRIX, DECAY
    )
    pv_new, pv_first, pv_second = adamw(
        private_vectors, private_vectors_first, private_vectors_second, g_vect_p, RATE_VECTOR, 0.0
    )
    return (
        emb_new,
        emb_first,
        emb_second,
        pos_new,
        pos_first,
        pos_second,
        sw_new,
        sw_first,
        sw_second,
        sd_new,
        sd_first,
        sd_second,
        sv_new,
        sv_first,
        sv_second,
        pw_new,
        pw_first,
        pw_second,
        pd_new,
        pd_first,
        pd_second,
        pv_new,
        pv_first,
        pv_second,
        loss_sum.reshape(1),
        count_sum.reshape(1),
        grad_norm,
    )


def solution(mesh):
    in_specs = (
        P("client", "shard", None),
        P("client", "shard"),
        P("client", "shard", None),
        P(),
        P(("client", "shard"), None),
        P(("client", "shard"), None),
        P(("client", "shard"), None),
        P(("client", "shard"), None),
        P(("client", "shard"), None),
        P(("client", "shard"), None),
        P(("client", "shard"), None),
        P(("client", "shard"), None),
        P(("client", "shard"), None),
        P(("client", "shard"), None),
        P(("client", "shard"), None),
        P(("client", "shard"), None),
        P(("client", "shard")),
        P(("client", "shard")),
        P(("client", "shard")),
        P("client", "shard", None),
        P("client", "shard", None),
        P("client", "shard", None),
        P("client", "shard", None),
        P("client", "shard", None),
        P("client", "shard", None),
        P("client", "shard"),
        P("client", "shard"),
        P("client", "shard"),
    )
    out_specs = (
        P(("client", "shard"), None),
        P(("client", "shard"), None),
        P(("client", "shard"), None),
        P(("client", "shard"), None),
        P(("client", "shard"), None),
        P(("client", "shard"), None),
        P(("client", "shard"), None),
        P(("client", "shard"), None),
        P(("client", "shard"), None),
        P(("client", "shard"), None),
        P(("client", "shard"), None),
        P(("client", "shard"), None),
        P(("client", "shard")),
        P(("client", "shard")),
        P(("client", "shard")),
        P("client", "shard", None),
        P("client", "shard", None),
        P("client", "shard", None),
        P("client", "shard", None),
        P("client", "shard", None),
        P("client", "shard", None),
        P("client", "shard"),
        P("client", "shard"),
        P("client", "shard"),
        P("client"),
        P("client"),
        P(),
    )
    return jax.shard_map(
        per_device, mesh=mesh, in_specs=in_specs, out_specs=out_specs, check_vma=False
    )
```

profile of v0, /device:TPU:0, one launch (start us, length us, event | category | flops | bytes accessed | tf_op | source)
XLA Modules:
  0.0 2556.7 jit_solution(5016990910735138742)
XLA Ops:
  17.0 32.7 %all_gather.60 = bf16[1,9216]{1,0:T(2,128)(2,1)S(1)} all-gather(bf16[1,1152]{1,0:T(2,128)(2,1)S(1)} %convert_element_type.350), channel_id=1, replica_groups=mesh['client'=4,'shard'=8] {'shard'}, dimensions={1}, use_global_device_ids=true | all-gather | bytes 20736 | tf_op jit(solution)/shard_map/all_gather | solution.py:280
  50.1 42.5 %all-reduce.1 = bf16[10752]{0:T(1024)(128)(2,1)S(1)} all-reduce(bf16[10752]{0:T(1024)(128)(2,1)S(1)} %dynamic-update-slice.3), channel_id=1, replica_groups=mesh['client'=4,'shard'=8] {'client','shard'}, use_global_device_ids=true, to_apply=%add.1 | all-reduce | flops 10752 | bytes 43008
  97.0 324.6 %all-gather.29.cloned.1.call-done = bf16[32,1572,768]{2,1,0:T(8,128)(2,1)} async-done(((bf16[1,1572,768]{2,1,0:T(8,128)(2,1)}), bf16[32,1572,768]{2,1,0:T(8,128)(2,1)}) %all-gather.29.cloned.1.call-update) | async-done | bytes 77266960 | tf_op jit(solution)/shard_map/all_gather | solution.py:267
  421.6 88.7 %reshape.930 = bf16[50304,768]{1,0:T(8,128)(2,1)} reshape(bf16[32,1572,768]{2,1,0:T(8,128)(2,1)} %all-gather.29.cloned.1.call-done) | data formatting | bytes 154533888
  518.4 99.7 %all-gather.17.cloned.1.call-done = bf16[1,768,6144]{2,1,0:T(8,128)(2,1)} async-done(((bf16[1,96,6144]{2,1,0:T(8,128)(2,1)}), bf16[1,768,6144]{2,1,0:T(8,128)(2,1)}) %all-gather.17.cloned.1.call-update) | async-done | bytes 9437200 | tf_op jit(solution)/shard_map/all_gather | solution.py:278
  647.6 51.2 %all-gather.19.cloned.1.call-done = bf16[1,3072,768]{2,1,0:T(8,128)(2,1)} async-done(((bf16[1,384,768]{2,1,0:T(8,128)(2,1)}), bf16[1,3072,768]{2,1,0:T(8,128)(2,1)}) %all-gather.19.cloned.1.call-update) | async-done | bytes 4718608 | tf_op jit(solution)/shard_map/all_gather | solution.py:279
  707.9 74.5 %all-gather.21.cloned.1.call-done = bf16[768,6144]{1,0:T(8,128)(2,1)} async-done(((bf16[24,6144]{1,0:T(8,128)(2,1)}), bf16[768,6144]{1,0:T(8,128)(2,1)}) %all-gather.21.cloned.1.call-update) | async-done | bytes 9437200 | tf_op jit(solution)/shard_map/all_gather | solution.py:271
  812.5 35.5 %all-gather.23.cloned.1.call-done = bf16[3072,768]{1,0:T(8,128)(2,1)} async-done(((bf16[96,768]{1,0:T(8,128)(2,1)}), bf16[3072,768]{1,0:T(8,128)(2,1)}) %all-gather.23.cloned.1.call-update) | async-done | bytes 4718608 | tf_op jit(solution)/shard_map/all_gather | solution.py:272
  863.0 66.2 %all-gather.3 = s32[32,1,128]{2,1,0:T(1,128)S(1)} all-gather(s32[1,1,128]{2,1,0:T(1,128)S(1)} %copy-done.152), channel_id=1, replica_groups=mesh['client'=4,'shard'=8] {'client','shard'}, dimensions={0}, use_global_device_ids=true | all-gather | bytes 16896 | tf_op jit(solution)/shard_map/all_gather | solution.py:314
  931.0 63.0 %all-gather.5 = s32[32,1,128]{2,1,0:T(1,128)S(1)} all-gather(s32[1,1,128]{2,1,0:T(1,128)S(1)} %fusion.107), channel_id=1, replica_groups=mesh['client'=4,'shard'=8] {'client','shard'}, dimensions={0}, use_global_device_ids=true | all-gather | bytes 16896 | tf_op jit(solution)/shard_map/all_gather | solution.py:313
  994.7 18.4 fusion.156
  1013.1 11.9 select_reduce_fusion
  1025.0 67.1 %all-gather.2 = bf16[131072]{0:T(1024)(128)(2,1)S(1)} all-gather(bf16[4096]{0:T(1024)(128)(2,1)S(1)} %get-tuple-element.286), channel_id=4, replica_groups=mesh['client'=4,'shard'=8] {'client','shard'}, dimensions={0}, use_global_device_ids=true | all-gather | bytes 270336 | tf_op jit(solution)/shard_map/all_gather | solution.py:23
  1093.0 64.7 %all-gather.1 = bf16[131072]{0:T(1024)(128)(2,1)S(1)} all-gather(bf16[4096]{0:T(1024)(128)(2,1)S(1)} %get-tuple-element.287), channel_id=3, replica_groups=mesh['client'=4,'shard'=8] {'client','shard'}, dimensions={0}, use_global_device_ids=true | all-gather | bytes 270336 | tf_op jit(solution)/shard_map/all_gather | solution.py:23
  1158.6 67.1 %all-gather = bf16[131072]{0:T(1024)(128)(2,1)S(1)} all-gather(bf16[4096]{0:T(1024)(128)(2,1)S(1)} %convert_element_type.375), channel_id=2, replica_groups=mesh['client'=4,'shard'=8] {'client','shard'}, dimensions={0}, use_global_device_ids=true | all-gather | bytes 270336 | tf_op jit(solution)/shard_map/all_gather | solution.py:23
  1226.4 56.9 %while.13 = (s32[]{:T(128)}, f32[4096]{0:T(1024)S(1)}, f32[4096]{0:T(1024)S(1)}, f32[4096]{0:T(1024)S(1)}, bf16[32,4096]{1,0:T(8,128)(2,1)}, /*index=5*/bf16[32,...) while((s32[]{:T(128)}, f32[4096]{0:T(1024)S(1)}, f32[4096]{0:T(1024)S(1)}, ...), condition=%wide.region_20.21_spmd, body=%wide.region_19.20_spmd.sunk | while | flops 40965 | bytes 221335 | solution.py:35
  1283.4 23.8 fusion.125
  1307.3 153.0 %reduce-scatter.12.cloned.1.call-done = f32[128,768]{1,0:T(8,128)} async-done(((f32[4096,768]{1,0:T(8,128)}), f32[128,768]{1,0:T(8,128)}) %reduce-scatter.12.cloned.1.call-update) | async-done | bytes 393232 | tf_op jit(solution)/shard_map/reduce_scatter | solution.py:344
  1654.3 18.3 all_gather.73
  1672.6 26.0 %all_gather.71 = s32[1,8,512]{2,0,1:T(1,128)S(1)} all-gather(s32[1,1,512]{2,0,1:T(1,128)S(1)} %bitcast.202), channel_id=1, replica_groups=mesh['client'=4,'shard'=8] {'shard'}, dimensions={1}, use_global_device_ids=true | all-gather | bytes 18432 | tf_op jit(solution)/shard_map/all_gather | solution.py:284
  1701.3 38.8 %all-reduce.4 = f32[10752]{0:T(1024)S(1)} all-reduce(f32[10752]{0:T(1024)S(1)} %constant_dynamic-update-slice_fusion.18), channel_id=10, replica_groups=mesh['client'=4,'shard'=8] {'client','shard'}, use_global_device_ids=true, to_apply=%region_54.55.clone | all-reduce | flops 10752 | bytes 86016
  1742.5 13.3 reduce-scatter.14.cloned.1.call-done
  1757.4 99.4 %all-gather.27.cloned.1.call-done = bf16[4096,768]{1,0:T(8,128)(2,1)} async-done(((bf16[512,768]{1,0:T(8,128)(2,1)}), bf16[4096,768]{1,0:T(8,128)(2,1)}) %all-gather.27.cloned.1.call-update) | async-done | bytes 6291472 | tf_op jit(solution)/shard_map/all_gather | solution.py:360
  1856.8 36.1 %scatter_custom_fusion.1 = f32[6288,768]{1,0:T(8,128)} fusion(s32[4096]{0:T(1024)S(1)} %bitcast.237, bf16[4096,768]{1,0:T(8,128)(2,1)} %all-gather.27.cloned.1.call-done, f32[]{:T(128)} %constant.332.clone.1), kind=kCustom, calls=%fused_computation.14 | custom fusion | flops 6291456 | bytes 25608196 | tf_op jit(solution)/shard_map/scatter-add | solution.py:370
  1892.9 11.4 convert_element_type.406
  1904.3 85.5 %fusion = bf16[1576,768]{1,0:T(8,128)(2,1)S(1)} fusion(bf16[6288,768]{1,0:T(8,128)(2,1)} %convert_element_type.406), kind=kCustom, calls=%all-reduce-scatter | all-reduce-scatter fusion | flops 4841473 | bytes 12079616
  2004.1 23.8 multiply_reduce_fusion.2
  2029.2 67.9 %reduce-scatter.18.cloned.1.call-done = f32[96,768]{1,0:T(8,128)} async-done(((f32[3072,768]{1,0:T(8,128)}), f32[96,768]{1,0:T(8,128)}) %reduce-scatter.18.cloned.1.call-update) | async-done | bytes 294928 | tf_op jit(solution)/shard_map/reduce_scatter | solution.py:377
  2098.8 164.4 %reduce-scatter.20.cloned.1.call-done = bf16[1,96,6144]{2,1,0:T(8,128)(2,1)} async-done(((bf16[1,768,6144]{2,1,0:T(8,128)(2,1)}), bf16[1,96,6144]{2,1,0:T(8,128)(2,1)}) %reduce-scatter.20.cloned.1.call-update) | async-done | bytes 1179664 | tf_op jit(solution)/shard_map/reduce_scatter | solution.py:382
  2265.6 209.6 %reduce-scatter.16.cloned.1.call-done = f32[24,6144]{1,0:T(8,128)} async-done(((f32[768,6144]{1,0:T(8,128)}), f32[24,6144]{1,0:T(8,128)}) %reduce-scatter.16.cloned.1.call-update) | async-done | bytes 589840 | tf_op jit(solution)/shard_map/reduce_scatter | solution.py:376
  2481.7 39.3 %all-reduce.6 = (f32[]{:T(128)}, f32[4]{0:T(128)S(1)}) all-reduce(f32[]{:T(128)S(6)} %add.704, f32[4]{0:T(128)S(1)} %compare_select_fusion.12), channel_id=1, replica_groups=mesh['client'=4,'shard'=8] {'client','shard'}, use_global_device_ids=true, to_apply=%region_70.71 | all-reduce | flops 5 | bytes 40 | tf_op jit(solution)/shard_map/psum | solution.py:407
  2523.7 12.7 multiply_subtract_fusion
  (717 shorter events, 398.4 us)
Async XLA Ops:
  7.2 414.4 %all-gather.29.cloned.1.call-start = ((), (), s32[]{:S(2)}) async-start(), calls=%async_computation.20 | async-start | bytes 79884288 | tf_op jit(solution)/shard_map/all_gather | solution.py:267
  11.5 503.2 %all-gather.15.cloned.1.call-start = ((), (), s32[]{:S(2)}) async-start(), calls=%async_computation.7 | async-start | bytes 1622016 | tf_op jit(solution)/shard_map/all_gather | solution.py:268
  13.1 605.0 %all-gather.17.cloned.1.call-start = ((), (), s32[]{:S(2)}) async-start(), calls=%async_computation.8 | async-start | bytes 10616832 | tf_op jit(solution)/shard_map/all_gather | solution.py:278
  14.4 684.4 %all-gather.19.cloned.1.call-start = ((), (), s32[]{:S(2)}) async-start(), calls=%async_computation.9 | async-start | bytes 5308416 | tf_op jit(solution)/shard_map/all_gather | solution.py:279
  15.4 767.0 %all-gather.21.cloned.1.call-start = ((), (), s32[]{:S(2)}) async-start(), calls=%async_computation.10 | async-start | bytes 9732096 | tf_op jit(solution)/shard_map/all_gather | solution.py:271
  16.2 831.8 %all-gather.23.cloned.1.call-start = ((), (), s32[]{:S(2)}) async-start(), calls=%async_computation.11 | async-start | bytes 4866048 | tf_op jit(solution)/shard_map/all_gather | solution.py:272
  17.0 977.7 %all-gather.25.cloned.1.call-start = ((), (), s32[]{:S(2)}) async-start(), calls=%async_computation.12 | async-start | bytes 6488064 | tf_op jit(solution)/shard_map/all_gather | solution.py:311
  49.8 649.0 %copy-start.105 = (f32[1,3072]{1,0:T(1,128)}, f32[1,3072]{1,0:T(1,128)S(1)}, u32[]{:S(2)}) copy-start(f32[1,3072]{1,0:T(1,128)S(1)} %slice.270) | copy-start | bytes 36868
  93.2 689.2 %copy-start.102 = (f32[768]{0:T(1024)}, f32[768]{0:T(1024)S(1)}, u32[]{:S(2)}) copy-start(f32[768]{0:T(1024)S(1)} %get-tuple-element.388) | copy-start | bytes 9220
  93.2 710.9 %copy-start.99 = (f32[768]{0:T(1024)}, f32[768]{0:T(1024)S(1)}, u32[]{:S(2)}) copy-start(f32[768]{0:T(1024)S(1)} %get-tuple-element.384) | copy-start | bytes 9220
  93.8 543.5 %copy-start.111 = (pred[512]{0:T(512)(128)(4,1)}, pred[512]{0:T(512)(128)(4,1)S(1)}, u32[]{:S(2)}) copy-start(pred[512]{0:T(512)(128)(4,1)S(1)} %compare_and_fusion) | copy-start | bytes 1540
  93.9 524.2 %copy-start.97 = (f32[768]{0:T(1024)}, f32[768]{0:T(1024)S(1)}, u32[]{:S(2)}) copy-start(f32[768]{0:T(1024)S(1)} %get-tuple-element.310) | copy-start | bytes 9220
  94.0 524.2 %copy-start.134 = (f32[768]{0:T(1024)}, f32[768]{0:T(1024)S(1)}, u32[]{:S(2)}) copy-start(f32[768]{0:T(1024)S(1)} %get-tuple-element.309) | copy-start | bytes 9220
  94.0 546.3 %copy-start.94 = (f32[768]{0:T(1024)}, f32[768]{0:T(1024)S(1)}, u32[]{:S(2)}) copy-start(f32[768]{0:T(1024)S(1)} %get-tuple-element.303) | copy-start | bytes 9220
  94.0 546.3 %copy-start.132 = (f32[768]{0:T(1024)}, f32[768]{0:T(1024)S(1)}, u32[]{:S(2)}) copy-start(f32[768]{0:T(1024)S(1)} %get-tuple-element.305) | copy-start | bytes 9220
  96.4 764.3 %copy-start.84 = (pred[128]{0:T(512)(128)(4,1)}, pred[128]{0:T(512)(128)(4,1)S(1)}, u32[]{:S(2)}) copy-start(pred[128]{0:T(512)(128)(4,1)S(1)} %get-tuple-element.399) | copy-start | bytes 388
  861.6 598.7 %reduce-scatter.12.cloned.1.call-start = ((), (), s32[]{:S(2)}) async-start(), calls=%async_computation.13 | async-start | bytes 12976128 | tf_op jit(solution)/shard_map/reduce_scatter | solution.py:344
  1307.2 433.5 %reduce-scatter.24.cloned.1.call-start = ((), (), s32[]{:S(2)}) async-start(), calls=%async_computation.21 | async-start | bytes 2654208
  1580.0 175.9 %reduce-scatter.14.cloned.1.call-start = ((), (), s32[]{:S(2)}) async-start(), calls=%async_computation.15 | async-start | bytes 3244032 | tf_op jit(solution)/shard_map/reduce_scatter | solution.py:379
  1586.2 270.6 %all-gather.27.cloned.1.call-start = ((), (), s32[]{:S(2)}) async-start(), calls=%async_computation.14 | async-start | bytes 7077888 | tf_op jit(solution)/shard_map/all_gather | solution.py:360
  1586.9 404.5 %reduce-scatter.22.cloned.1.call-start = ((), (), s32[]{:S(2)}) async-start(), calls=%async_computation.19 | async-start | bytes 5308416 | tf_op jit(solution)/shard_map/reduce_scatter | solution.py:385
  1595.8 501.4 %reduce-scatter.18.cloned.1.call-start = ((), (), s32[]{:S(2)}) async-start(), calls=%async_computation.17 | async-start | bytes 9732096 | tf_op jit(solution)/shard_map/reduce_scatter | solution.py:377
  1607.4 655.8 %reduce-scatter.20.cloned.1.call-start = ((), (), s32[]{:S(2)}) async-start(), calls=%async_computation.18 | async-start | bytes 10616832 | tf_op jit(solution)/shard_map/reduce_scatter | solution.py:382
  1625.1 850.2 %reduce-scatter.16.cloned.1.call-start = ((), (), s32[]{:S(2)}) async-start(), calls=%async_computation.16 | async-start | bytes 19464192 | tf_op jit(solution)/shard_map/reduce_scatter | solution.py:376
  1989.9 3.5 collective-permute-start
  2004.0 518.3 %copy-start.83 = (f32[1,1152]{1,0:T(1,128)S(1)}, f32[1,1152]{1,0:T(1,128)}, u32[]{:S(2)}) copy-start(f32[1,1152]{1,0:T(1,128)} %param.57) | copy-start | bytes 13828
  2004.0 518.3 %copy-start.128 = (f32[1,1152]{1,0:T(1,128)S(1)}, f32[1,1152]{1,0:T(1,128)}, u32[]{:S(2)}) copy-start(f32[1,1152]{1,0:T(1,128)} %param.58) | copy-start | bytes 13828
  2004.0 518.3 %copy-start.129 = (f32[1,1152]{1,0:T(1,128)S(1)}, f32[1,1152]{1,0:T(1,128)}, u32[]{:S(2)}) copy-start(f32[1,1152]{1,0:T(1,128)} %param.59) | copy-start | bytes 13828
  2004.1 518.9 %copy-start.125 = (f32[336]{0:T(512)S(1)}, f32[336]{0:T(512)}, u32[]{:S(2)}) copy-start(f32[336]{0:T(512)} %param.48) | copy-start | bytes 4036
  2004.1 518.9 %copy-start.145 = (f32[336]{0:T(512)S(1)}, f32[336]{0:T(512)}, u32[]{:S(2)}) copy-start(f32[336]{0:T(512)} %param.49) | copy-start | bytes 4036
  2004.1 518.9 %copy-start.146 = (f32[336]{0:T(512)S(1)}, f32[336]{0:T(512)}, u32[]{:S(2)}) copy-start(f32[336]{0:T(512)} %param.50) | copy-start | bytes 4036
  2004.1 519.6 %copy-start.18 = (bf16[1588,768]{1,0:T(8,128)(2,1)S(1)}, bf16[1588,768]{1,0:T(8,128)(2,1)}, u32[]{:S(2)}) copy-start(bf16[1588,768]{1,0:T(8,128)(2,1)} %concatenate.78) | copy-start | bytes 7317508
  (162 other events, 4577.3 us)
Sparse Core Ops, SparseCore 0:
  11.6 409.9 all-gather.28
  425.1 53.2 all-gather.14
  481.1 136.9 all-gather.16
  620.7 78.0 all-gather.18
  702.2 80.1 all-gather.20
  785.7 62.2 all-gather.22
  861.7 68.3 all-gather.24
  1307.4 152.9 reduce-scatter.11
  1580.1 67.9 reduce-scatter.23
  1654.8 101.0 reduce-scatter.13
  1758.8 97.9 all-gather.26
  1861.3 93.5 reduce-scatter.21
  1961.9 135.2 reduce-scatter.17
  2100.6 162.5 reduce-scatter.19
  2269.4 205.8 reduce-scatter.15
where the time goes:
time: 2570 us; the launch traced here: 2560 us
  waiting for transfers between devices  1290 us (50%)
  blocking collectives  622 us (24%)
  matrix products  242 us (9%)
  other arithmetic  219 us (9%)
  local copies, waits for them, and re-layouts  150 us (6%)
  between operations  25.8 us (1%)
    all_gather x1, waiting for transfers between devices, per_device(): lax.all_gather(embedding.astype(jnp.bfloat16), ('client', 'shard'), axis=...  325 us
    reduce_scatter x1, waiting for transfers between devices, per_device(): lax.psum_scatter(grad_wide_s, ('client', 'shard'), scatter_dimension=0, t...  210 us
    all_gather x3, blocking collectives, merged(): lax.all_gather(a.astype(kind), axis)  199 us
    unnamed x4, blocking collectives  177 us
    reduce_scatter x1, waiting for transfers between devices, per_device(): lax.psum_scatter(grad_wide_p[None].astype(jnp.bfloat16), 'shard', scatter...  164 us
    reduce_scatter x1, waiting for transfers between devices, per_device(): lax.psum_scatter(dot_plain(grad_logits_own, table_own), ('client', 'shard...  153 us
    unnamed x386, local copies, waits for them, and re-layouts  126 us
    all_gather x1, waiting for transfers between devices, per_device(): lax.all_gather(private_wide.astype(jnp.bfloat16), 'shard', axis=1, tiled=...  99.7 us
  transfers between devices with their start and end apart: 16, of which 11 were waited for; matrix products, arithmetic and copies ran while one was open for 16% of the time, Pallas kernels for 0%

commit v1 on v0

v1 whole, which is shorter than its diff:
```python
import jax
import jax.numpy as jnp
from jax import lax
from jax.sharding import Mesh
from jax.sharding import PartitionSpec as P

HD = 64
D = 768
FF = 3072
NPOS = 1024
STEP = 5


SCALE = 0.125
CLIP_NORM = 0.01
RATE_MATRIX = 0.03
RATE_VECTOR = 0.5
DECAY = 0.01
EPSILON = 1e-08
BF = jnp.bfloat16
F32 = jnp.float32


def dot_plain(former, latter):
    return jnp.dot(former, latter, preferred_element_type=jnp.float32)


def dot_inner(former, latter):
    return lax.dot_general(
        former, latter, (((0,), (0,)), ((), ())), preferred_element_type=jnp.float32
    )


def dot_outer(former, latter):
    return lax.dot_general(
        former, latter, (((1,), (1,)), ((), ())), preferred_element_type=jnp.float32
    )


def layer_norm(values, scales, shifts):
    centre = values - jnp.mean(values, -1, keepdims=True)
    spread = jnp.mean(centre * centre, -1, keepdims=True)
    return centre * lax.rsqrt(spread + 1e-05) * scales + shifts


def gelu_tanh(values):
    return jax.nn.gelu(values, approximate=True)


def split_vectors(vectors, breadth, hidden):
    starts = [
        0,
        breadth,
        2 * breadth,
        3 * breadth,
        4 * breadth,
        5 * breadth,
        6 * breadth,
        7 * breadth,
        7 * breadth + hidden,
        8 * breadth + hidden,
    ]
    return [vectors[starts[position] : starts[position + 1]] for position in range(9)]


def causal_mask(seq_len, live_len):
    rows_at = lax.broadcasted_iota(jnp.int32, (seq_len, seq_len), 0)
    cols_at = lax.broadcasted_iota(jnp.int32, (seq_len, seq_len), 1)
    return (cols_at <= rows_at) & (cols_at < live_len)


def masked_scores(block_qkv, seq_len, live_len):
    scores = (
        jnp.einsum(
            "qhd,khd->hqk", block_qkv[:, 0], block_qkv[:, 1], preferred_element_type=jnp.float32
        )
        * SCALE
    )
    return jnp.where(causal_mask(seq_len, live_len)[None], scores, -1e30)


def attend(joined, live_len):
    breadth = joined.shape[1] // 3
    seq_len = joined.shape[0]
    block_qkv = joined.reshape(seq_len, 3, breadth // HD, HD)
    scores = masked_scores(block_qkv, seq_len, live_len)
    highest = jnp.max(scores, -1, keepdims=True)
    exponent = jnp.exp(scores - highest)
    totals = jnp.sum(exponent, -1, keepdims=True)
    probs_b = (exponent / totals).astype(jnp.bfloat16)
    mixed_out = jnp.einsum(
        "hqk,khd->qhd", probs_b, block_qkv[:, 2], preferred_element_type=jnp.float32
    )
    return (
        mixed_out.astype(jnp.bfloat16).reshape(seq_len, breadth),
        (highest + jnp.log(totals))[..., 0],
    )


def attend_back(joined, log_total, grad_mixed, live_len):
    breadth = joined.shape[1] // 3
    seq_len = joined.shape[0]
    head_count = breadth // HD
    block_qkv = joined.reshape(seq_len, 3, head_count, HD)
    grad_out = grad_mixed.reshape(seq_len, head_count, HD)
    scores = masked_scores(block_qkv, seq_len, live_len)
    probs = jnp.exp(scores - log_total[..., None])
    probs_b = probs.astype(jnp.bfloat16)
    grad_values = jnp.einsum("hqk,qhd->khd", probs_b, grad_out, preferred_element_type=jnp.float32)
    grad_probs = jnp.einsum(
        "qhd,khd->hqk", grad_out, block_qkv[:, 2], preferred_element_type=jnp.float32
    )
    inner = jnp.sum(grad_probs * probs, -1, keepdims=True)
    grad_scores = (probs * (grad_probs - inner)).astype(jnp.bfloat16)
    grad_queries = (
        jnp.einsum("hqk,khd->qhd", grad_scores, block_qkv[:, 1], preferred_element_type=jnp.float32)
        * SCALE
    )
    grad_keys = (
        jnp.einsum("hqk,qhd->khd", grad_scores, block_qkv[:, 0], preferred_element_type=jnp.float32)
        * SCALE
    )
    stacked = jnp.stack([grad_queries, grad_keys, grad_values], 1).astype(jnp.bfloat16)
    return stacked.reshape(seq_len, 3 * breadth)


def layer_forward(inputs, weights, vectors, live_len):
    qkvo, fore, down = weights
    breadth = inputs.shape[1]
    parts = split_vectors(vectors, breadth, down.shape[0])
    normed = layer_norm(inputs, parts[0], parts[1]).astype(jnp.bfloat16)
    shift_qkv = jnp.concatenate([parts[2], jnp.zeros_like(parts[2]), parts[3]])
    joined = (dot_plain(normed, qkvo[:, : 3 * breadth]) + shift_qkv).astype(jnp.bfloat16)
    mixed_out, log_totals = attend(joined, live_len)
    middle = inputs + (dot_plain(mixed_out, qkvo[:, 3 * breadth :]) + parts[4])
    normed_two = layer_norm(middle, parts[5], parts[6]).astype(jnp.bfloat16)
    pre_act = dot_plain(normed_two, fore) + parts[7]
    activ = gelu_tanh(pre_act).astype(jnp.bfloat16)
    output = middle + (dot_plain(activ, down) + parts[8])
    return (
        output,
        (inputs, normed, joined, mixed_out, log_totals, middle, normed_two, pre_act, activ),
    )


def layer_backward(grad_out, saved, weights, vectors, live_len):
    inputs, normed, joined, mixed_out, log_totals, middle, normed_two, pre_act, activ = saved
    qkvo, fore, down = weights
    breadth = inputs.shape[1]
    parts = split_vectors(vectors, breadth, down.shape[0])
    grad_y = grad_out.astype(jnp.bfloat16)
    grad_down = dot_inner(activ, grad_y).astype(BF)
    grad_act = dot_outer(grad_y, down)
    grad_pre = jax.vjp(gelu_tanh, pre_act)[1](grad_act)[0].astype(jnp.bfloat16)
    grad_fore = dot_inner(normed_two, grad_pre).astype(BF)
    grad_norm_two = dot_outer(grad_pre, fore)
    grad_mid_norm, grad_scale_two, grad_shift_two = jax.vjp(layer_norm, middle, parts[5], parts[6])[
        1
    ](grad_norm_two)
    grad_mid = grad_out + grad_mid_norm
    grad_branch = grad_mid.astype(jnp.bfloat16)
    grad_proj = dot_inner(mixed_out, grad_branch).astype(BF)
    grad_mixed = dot_outer(grad_branch, qkvo[:, 3 * breadth :]).astype(jnp.bfloat16)
    grad_joined = attend_back(joined, log_totals, grad_mixed, live_len)
    grad_qkv = dot_inner(normed, grad_joined).astype(BF)
    grad_normed = dot_outer(grad_joined, qkvo[:, : 3 * breadth])
    grad_in_norm, grad_scale_one, grad_shift_one = jax.vjp(layer_norm, inputs, parts[0], parts[1])[
        1
    ](grad_normed)
    joined_sums = jnp.sum(grad_joined.astype(jnp.float32), 0)
    grad_vectors = jnp.concatenate(
        [
            grad_scale_one,
            grad_shift_one,
            joined_sums[:breadth],
            joined_sums[2 * breadth :],
            jnp.sum(grad_branch.astype(jnp.float32), 0),
            grad_scale_two,
            grad_shift_two,
            jnp.sum(grad_pre.astype(jnp.float32), 0),
            jnp.sum(grad_y.astype(jnp.float32), 0),
        ]
    )
    grad_qkvo = jnp.concatenate([grad_qkv, grad_proj], 1)
    return (grad_mid + grad_in_norm, (grad_qkvo, grad_fore, grad_down), grad_vectors)


def adamw(weight, first, second, gradient, rate, decay):
    first_new = 0.5 * first + 0.5 * gradient
    second_new = 0.5 * second + 0.5 * gradient * gradient
    first_hat = first_new / (1.0 - 0.5**STEP)
    second_hat = second_new / (1.0 - 0.5**STEP)
    weight_new = weight - rate * (first_hat / (jnp.sqrt(second_hat) + EPSILON) + decay * weight)
    return (weight_new, first_new, second_new)


FLIP = [(0, 1), (1, 0)]


def across(x, name):
    return lax.ppermute(x, name, FLIP)


def gather_bit(x, name, dim):
    other = across(x, name)
    low_side = lax.axis_index(name) == 0
    return jnp.where(
        low_side, jnp.concatenate([x, other], dim), jnp.concatenate([other, x], dim)
    )


def gather_bits(x, names, order):
    x = x.reshape((1,) * len(names) + x.shape)
    for name in order:
        x = gather_bit(x, name, names.index(name))
    x = x.reshape((-1,) + x.shape[len(names) :])
    return x.reshape((x.shape[0] * x.shape[1],) + x.shape[2:])


def reduce_bit(x, name, dim, last=BF):
    side = lax.axis_index(name)
    keep = lax.dynamic_index_in_dim(x, side, dim, True)
    other = across(lax.dynamic_index_in_dim(x, 1 - side, dim, True), name)
    return (keep.astype(F32) + other.astype(F32)).astype(last)


def reduce_bits(x, names, order):
    shape = x.shape
    x = x.reshape((2,) * len(names) + (shape[0] // 2 ** len(names),) + shape[1:])
    for name in order:
        x = reduce_bit(x, name, names.index(name), F32 if name == order[-1] else BF)
    return x.reshape((-1,) + shape[1:])


def sum_bits(x, names):
    for name in names:
        x = x + across(x, name)
    return x


def per_device(
    shard_names,
    token_ids,
    lengths,
    picked,
    joining,
    embedding,
    embedding_first,
    embedding_second,
    position_table,
    position_first,
    position_second,
    shared_wide,
    shared_wide_first,
    shared_wide_second,
    shared_down,
    shared_down_first,
    shared_down_second,
    shared_vectors,
    shared_vectors_first,
    shared_vectors_second,
    private_wide,
    private_wide_first,
    private_wide_second,
    private_down,
    private_down_first,
    private_down_second,
    private_vectors,
    private_vectors_first,
    private_vectors_second,
):
    half, rest = shard_names[0], shard_names[1:]
    every = ("pair", "core") + shard_names
    crew = ("core",) + rest
    shards = 2 ** len(shard_names)
    clients = 4
    count = clients * shards
    at_pair, at_core, at_half = (lax.axis_index(n) for n in ("pair", "core", half))
    device_at = lax.axis_index(every)
    shard_at = lax.axis_index(shard_names)
    swap_pairs = []
    block = shards // 2
    for pair in range(clients // 2):
        for spot in range(block):
            former = ((pair * 2 + 0) * 2 + 1) * block + spot
            latter = ((pair * 2 + 1) * 2 + 0) * block + spot
            swap_pairs += [(former, latter), (latter, former)]

    def swap(x):
        return jnp.where(at_core == at_half, x, lax.ppermute(x, every, swap_pairs))

    seq_len = token_ids.shape[2]
    picks = picked.shape[2]
    slice_rows = embedding.shape[0]

    wide_b = private_wide[0].astype(BF)
    down_b = private_down[0].astype(BF)
    there, back = crew[1:] + ("core",), crew[:0:-1] + ("core",)
    cut = 4 * D
    weights_p = (
        gather_bits(swap(wide_b[:, :cut]), crew, there),
        gather_bits(swap(wide_b[:, cut:]), crew, back),
        gather_bits(swap(down_b), crew, there),
    )
    shared_b = shared_wide.astype(BF)
    spread = shard_names + ("pair", "core")
    weights_s = (
        gather_bits(shared_b[:, :cut], every, spread),
        gather_bits(shared_b[:, cut:], every, spread),
        gather_bits(shared_down.astype(BF), every, spread),
    )
    posit_b = gather_bits(position_table.astype(BF), every, spread)[:seq_len]
    table_own = embedding.astype(BF)
    table_four = gather_bits(table_own, ("pair", "core"), ("pair", "core"))

    ids = token_ids[0, 0]
    same = ids[:, None] == ids[None, :]
    at_row = lax.broadcasted_iota(jnp.int32, (seq_len, seq_len), 0)
    at_col = lax.broadcasted_iota(jnp.int32, (seq_len, seq_len), 1)
    first_at = jnp.min(jnp.where(same, at_col, seq_len), 1)
    is_first = first_at == jnp.arange(seq_len, dtype=jnp.int32)
    owners = ids // slice_rows
    slot = jnp.sum(
        (
            (owners[:, None] == owners[None, :]) & is_first[None, :] & (at_col < first_at[:, None])
        ).astype(jnp.int32),
        1,
    )

    vect_own = [shared_vectors, private_vectors[0]]
    pieces = [
        ids.astype(F32),
        slot.astype(F32),
        is_first.astype(F32),
        picked[0, 0].astype(F32),
        lengths[0].astype(F32),
    ] + [v.astype(BF).astype(F32) for v in vect_own]
    starts = [0]
    for piece in pieces:
        starts.append(starts[-1] + piece.shape[0])
    message = jnp.concatenate(pieces)
    message = jnp.pad(message, (0, -message.shape[0] % 1024)).reshape(1, -1, 128)
    board = lax.all_to_all(
        jnp.broadcast_to(message, (count,) + message.shape[1:]), every, 0, 0, tiled=True
    ).reshape(count, -1)

    def posted(place):
        return board[:, starts[place] : starts[place + 1]]

    def hosted(x):
        x = x.reshape((clients // 2, 2, 2, block) + x.shape[1:])
        return jnp.swapaxes(x, 1, 2).reshape((count,) + x.shape[4:])

    all_ids, all_slots, all_first, all_picks, all_lens = [
        hosted(posted(place).astype(jnp.int32)) for place in range(5)
    ]
    vect_s = posted(5).reshape(-1)
    vect_p = lax.dynamic_index_in_dim(
        posted(6).reshape(clients, -1), 2 * at_pair + at_half, 0, False
    )

    all_live = all_picks < all_lens - 1
    live_counts = jnp.sum(all_live.astype(F32), 1).reshape(clients // 2, 2, 2, block)
    counts_all = jnp.sum(live_counts, (1, 3)).reshape(-1)
    joining_f = joining.astype(F32)
    share_all = joining_f / (jnp.sum(joining_f) * counts_all)

    my_ids = lax.dynamic_index_in_dim(all_ids, device_at, 0, False)
    my_slots = lax.dynamic_index_in_dim(all_slots, device_at, 0, False)
    my_picks = lax.dynamic_index_in_dim(all_picks, device_at, 0, False)
    my_len = lax.dynamic_index_in_dim(all_lens, device_at, 0, False)[0]
    my_owners = my_ids // slice_rows

    room = max(16, 1024 // count)
    rounds = jnp.max(all_slots) // room + 1
    in_slice = all_ids - device_at * slice_rows
    wanted = (all_first > 0) & (in_slice >= 0) & (in_slice < slice_rows)

    def asked(turn):
        spots = turn * room + jnp.arange(room, dtype=jnp.int32)
        hits = wanted[:, None, :] & (all_slots[:, None, :] == spots[None, :, None])
        return jnp.sum(jnp.where(hits, in_slice[:, None, :], 0), 2).reshape(-1)

    def fetch(turn, rows):
        sent = jnp.take(table_own, asked(turn), axis=0, mode="clip")
        got = lax.all_to_all(sent, every, 0, 0, tiled=True)
        spot = my_slots - turn * room
        here = (spot >= 0) & (spot < room)
        found = jnp.take(got, jnp.where(here, my_owners * room + spot, 0), axis=0, mode="clip")
        return jnp.where(here[:, None], found, rows)

    rows = fetch(0, jnp.zeros((seq_len, D), BF))
    rows = lax.fori_loop(1, rounds, fetch, rows)
    inputs = rows.astype(F32) + posit_b.astype(F32)

    first_out, first_saved = layer_forward(inputs, weights_p, vect_p, my_len)
    second_out, second_saved = layer_forward(first_out, weights_s, vect_s[: 8 * D + FF], my_len)

    final_scale = vect_s[8 * D + FF : 9 * D + FF]
    final_shift = vect_s[9 * D + FF : 10 * D + FF]
    final_in = jnp.take(second_out, my_picks, axis=0, mode="clip")
    final_b = layer_norm(final_in, final_scale, final_shift).astype(BF)
    target_rows = jnp.take(rows, my_picks + 1, axis=0, mode="clip").astype(F32)

    scored = gather_bits(final_b, shard_names, shard_names)

    def group(x):
        x = x.reshape((clients, shards) + x.shape[1:])
        return lax.dynamic_index_in_dim(x, 2 * at_pair + at_core, 0, False)

    group_ids, group_picks, group_live = group(all_ids), group(all_picks), group(all_live)
    seq_at = lax.broadcasted_iota(jnp.int32, (shards, picks, seq_len), 2)
    targets = jnp.sum(
        jnp.where(seq_at == group_picks[:, :, None] + 1, group_ids[:, None, :], 0), 2
    ).reshape(-1)
    host_clients = 2 * at_pair + jnp.arange(shards, dtype=jnp.int32) // block
    weight = jnp.where(group_live, jnp.take(share_all, host_clients)[:, None], 0.0).reshape(-1)
    target_owner = targets // slice_rows
    local_target = jnp.where(
        target_owner % shards == shard_at,
        target_owner // shards * slice_rows + targets % slice_rows,
        -1,
    )
    logits = dot_outer(scored, table_four)
    hit = lax.broadcasted_iota(jnp.int32, logits.shape, 1) == local_target[:, None]
    part_max = jnp.max(logits, -1)
    exponent = jnp.exp(logits - part_max[:, None])
    part_sum = jnp.sum(exponent, -1)
    part_target = jnp.sum(jnp.where(hit, logits, 0.0), -1)
    pulled = dot_plain(exponent.astype(BF), table_four)
    top, total, target_logit = part_max, part_sum, part_target
    for name in shard_names:
        stats = across(jnp.stack([top, total, target_logit]), name)
        higher = jnp.maximum(top, stats[0])
        total = total * jnp.exp(top - higher) + stats[1] * jnp.exp(stats[0] - higher)
        top, target_logit = higher, target_logit + stats[2]
    log_all = top + jnp.log(total)
    pulled = (pulled * (weight * jnp.exp(part_max - log_all))[:, None]).astype(BF)
    pulled_own = reduce_bits(pulled, shard_names, shard_names[::-1])

    def own_rows(x):
        return lax.dynamic_slice_in_dim(x, shard_at * picks, picks, 0)

    own_weight = own_rows(weight)
    grad_final_b = pulled_own - own_weight[:, None] * target_rows
    own_live = lax.dynamic_index_in_dim(group_live, shard_at, 0, False)
    own_terms = jnp.sum(jnp.where(own_live, own_rows(log_all - target_logit), 0.0))
    grad_logits = (
        weight[:, None] * jnp.exp(logits - log_all[:, None])
        - jnp.where(hit, weight[:, None], 0.0)
    ).astype(BF)
    head_part = dot_inner(grad_logits, scored).astype(BF)
    head_own = reduce_bits(head_part, ("pair", "core"), ("core", "pair"))

    grad_final_in, grad_fscale, grad_fshift = jax.vjp(
        layer_norm, final_in, final_scale, final_shift
    )[1](grad_final_b)
    grad_second = jnp.zeros_like(second_out).at[my_picks].add(grad_final_in)
    grad_first, grads_s, grad_vect_s = layer_backward(
        grad_second, second_saved, weights_s, vect_s[: 8 * D + FF], my_len
    )
    gather_back = ("core", "pair") + shard_names[::-1]
    g_qkvo_s, g_fore_s, g_down_s = [reduce_bits(g, every, gather_back) for g in grads_s]
    grad_inputs, grads_p, grad_vect_p = layer_backward(
        grad_first, first_saved, weights_p, vect_p, my_len
    )
    g_qkvo_p, g_fore_p, g_down_p = [
        swap(reduce_bits(g, crew, order).astype(BF)).astype(F32)
        for g, order in zip(grads_p, (there[::-1], back[::-1], there[::-1]))
    ]

    vector_s = jnp.concatenate([grad_vect_s, grad_fscale, grad_fshift]).reshape(count, -1)
    to_client = jnp.arange(clients, dtype=jnp.int32) == 2 * at_pair + at_half
    vector_p = jnp.where(
        to_client[:, None, None], grad_vect_p.reshape(1, shards, -1), 0.0
    ).reshape(count, -1)
    width_s, width_p = vector_s.shape[1], vector_p.shape[1]
    packet = jnp.concatenate([vector_s, vector_p], 1)
    packet = jnp.pad(packet, ((0, 0), (0, -packet.shape[1] % 1024)))
    landed = lax.all_to_all(packet.reshape(count, -1, 128), every, 0, 0, tiled=True)
    landed = jnp.sum(landed.reshape(count, -1), 0)
    grad_vect_sh = landed[:width_s]
    grad_vect_ph = landed[width_s : width_s + width_p]

    posit_names = ("core",) + shard_names
    grad_posit = reduce_bits(grad_inputs.astype(BF), posit_names, posit_names)
    grad_posit = grad_posit + across(grad_posit.astype(BF), "pair").astype(F32)
    grad_posit = jnp.where(at_pair == 0, grad_posit, 0.0)

    grad_rows = grad_inputs.astype(BF)

    def give(turn, total_rows):
        spot = my_slots - turn * room
        here = (spot >= 0) & (spot < room)
        place = jnp.where(here, my_owners * room + spot, -1)
        chosen = lax.broadcasted_iota(jnp.int32, (count * room, seq_len), 0) == place[None, :]
        sent = dot_plain(chosen.astype(BF), grad_rows).astype(BF)
        got = lax.all_to_all(sent, every, 0, 0, tiled=True)
        landing = lax.broadcasted_iota(
            jnp.int32, (slice_rows, count * room), 0
        ) == asked(turn)[None, :]
        return total_rows + dot_plain(landing.astype(BF), got)

    grad_table = give(0, head_own)
    grad_table = lax.fori_loop(1, rounds, give, grad_table)

    all_grads = [
        grad_table,
        grad_posit,
        jnp.concatenate([g_qkvo_s, g_fore_s], 1),
        g_down_s,
        grad_vect_sh,
        jnp.concatenate([g_qkvo_p, g_fore_p], 1)[None],
        g_down_p[None],
        grad_vect_ph[None],
    ]
    squares = jnp.zeros((), jnp.float32)
    for gradient in all_grads:
        squares = squares + jnp.sum(gradient * gradient)
    client_at = jnp.arange(clients, dtype=jnp.int32)
    loss_vector = jnp.where(client_at == 2 * at_pair + at_half, own_terms, 0.0)
    figures = jnp.pad(jnp.concatenate([squares[None], loss_vector]), (0, 127 - clients))
    figures = sum_bits(figures, every)
    grad_norm = jnp.sqrt(figures[0])
    own_client = client_at == 2 * at_pair + at_core
    loss_sum = jnp.sum(jnp.where(own_client, figures[1 : 1 + clients], 0.0))
    count_sum = jnp.sum(jnp.where(own_client, counts_all, 0.0))
    factor = jnp.minimum(1.0, CLIP_NORM / grad_norm)
    g_table, g_posit, g_wide_s, g_down_s, g_vect_s, g_wide_p, g_down_p, g_vect_p = [
        member * factor for member in all_grads
    ]
    results = []
    for state, gradient, rate, decay in (
        ((embedding, embedding_first, embedding_second), g_table, RATE_MATRIX, DECAY),
        ((position_table, position_first, position_second), g_posit, RATE_MATRIX, DECAY),
        ((shared_wide, shared_wide_first, shared_wide_second), g_wide_s, RATE_MATRIX, DECAY),
        ((shared_down, shared_down_first, shared_down_second), g_down_s, RATE_MATRIX, DECAY),
        ((shared_vectors, shared_vectors_first, shared_vectors_second), g_vect_s, RATE_VECTOR, 0.0),
        ((private_wide, private_wide_first, private_wide_second), g_wide_p, RATE_MATRIX, DECAY),
        ((private_down, private_down_first, private_down_second), g_down_p, RATE_MATRIX, DECAY),
        (
            (private_vectors, private_vectors_first, private_vectors_second),
            g_vect_p,
            RATE_VECTOR,
            0.0,
        ),
    ):
        results += adamw(*state, gradient, rate, decay)
    return (*results, loss_sum.reshape(1), count_sum.reshape(1), grad_norm)


def solution(mesh):
    clients, shards = mesh.shape["client"], mesh.shape["shard"]
    depth = shards.bit_length() - 1
    if clients != 4 or shards != 2**depth:
        raise ValueError("mesh sizes")
    shard_names = tuple("s%d" % place for place in range(depth))
    fine = Mesh(
        mesh.devices.reshape((clients // 2, 2) + (2,) * depth), ("pair", "core") + shard_names
    )
    client, shard, both = ("pair", "core"), shard_names, ("pair", "core") + shard_names
    table, block, vector, lot = P(both, None), P(client, shard, None), P(both), P(client, shard)
    in_specs = (
        (block, lot, block, P())
        + (table,) * 12
        + (vector,) * 3
        + (block,) * 6
        + (lot,) * 3
    )
    out_specs = (
        (table,) * 12 + (vector,) * 3 + (block,) * 6 + (lot,) * 3 + (P(client), P(client), P())
    )

    def run(*arrays):
        return per_device(shard_names, *arrays)

    return jax.shard_map(
        run, mesh=fine, in_specs=in_specs, out_specs=out_specs, check_vma=False
    )
```

time: 2570 us -> 1110 us (0.43)
  waiting for transfers between devices: 1290 us -> 322 us
  blocking collectives: 622 us -> 0 us
  starting transfers between devices: 2.84 us -> 104 us
  other arithmetic: 219 us -> 260 us
    all_gather x8 -> x0, waiting for transfers between devices: 685 us -> none  [the longest x1 325 us: per_device(): lax.all_gather(embedding.astype(jnp.bfloat16), ('client', 'shard'), axis=...]
    reduce_scatter x6 -> x0, waiting for transfers between devices: 608 us -> none  [the longest x1 210 us: per_device(): lax.psum_scatter(grad_wide_s, ('client', 'shard'), scatter_dimension=0, t...]
    all_gather x8 -> x0, blocking collectives: 405 us -> none  [the longest x3 199 us: merged(): lax.all_gather(a.astype(kind), axis)]
    ppermute x0 -> x82, waiting for transfers between devices: none -> 304 us  [the longest x76 304 us: across(): return lax.ppermute(x, name, FLIP)]
    unnamed x4 -> x0, blocking collectives: 177 us -> none
    unnamed x386 -> x510, local copies, waits for them, and re-layouts: 126 us -> 25.8 us
    select_n x5 -> x44, other arithmetic: 1.98 us -> 89.1 us  [the longest x34 85.3 us: gather_bit(): jnp.where(low_side, jnp.concatenate([x, other], dim), jnp.concatenate([ot...]
    ppermute x0 -> x82, starting transfers between devices: none -> 86.1 us  [the longest x76 79.9 us: across(): return lax.ppermute(x, name, FLIP)]
  transfers between devices with their start and end apart: 16 -> 86, of which waited for: 11 -> 40; matrix products, arithmetic and copies ran while one was open for 16% -> 48% of each run, Pallas kernels for 0% -> 0%
where the time goes in v1:
time: 1110 us; the launch traced here: 1100 us
  waiting for transfers between devices  322 us (29%)
  other arithmetic  260 us (23%)
  matrix products  225 us (20%)
  local copies, waits for them, and re-layouts  172 us (15%)
  starting transfers between devices  104 us (9%)
  between operations  15 us (1%)
    ppermute x76, waiting for transfers between devices, across(): return lax.ppermute(x, name, FLIP)  304 us
    select_n x34, other arithmetic, gather_bit(): jnp.where(low_side, jnp.concatenate([x, other], dim), jnp.concatenate([ot...  85.3 us
    ppermute x76, starting transfers between devices, across(): return lax.ppermute(x, name, FLIP)  79.9 us
    dot_general x11, matrix products, dot_plain(): return jnp.dot(former, latter, preferred_element_type=jnp.float32)  58.8 us
    dot_general x9, matrix products, dot_inner(): lax.dot_general(former, latter, (((0,), (0,)), ((), ())), preferred_eleme...  58 us
    dot_general x9, matrix products, dot_outer(): lax.dot_general(former, latter, (((1,), (1,)), ((), ())), preferred_eleme...  56 us
    dynamic_slice x34, local copies, waits for them, and re-layouts, reduce_bit(): other = across(lax.dynamic_index_in_dim(x, 1 - side, dim, True), name)  55.5 us
    select_n x3, local copies, waits for them, and re-layouts, gather_bit(): jnp.where(low_side, jnp.concatenate([x, other], dim), jnp.concatenate([ot...  43.8 us
  transfers between devices with their start and end apart: 86, of which 40 were waited for; matrix products, arithmetic and copies ran while one was open for 48% of the time, Pallas kernels for 0%

profile of v1, /device:TPU:0, one launch (start us, length us, event | category | flops | bytes accessed | tf_op | source)
XLA Modules:
  0.0 1098.3 jit_solution(6294799726650714883)
XLA Ops:
  51.4 9.8 collective-permute-done.18
  63.2 10.6 collective-permute-done.23
  90.2 18.3 %collective-permute-done.3 = bf16[1,1,2,2,2,32,768]{6,5,4,3,2,1,0:T(8,128)(2,1)} collective-permute-done((bf16[1,1,2,2,2,32,768]{6,5,4,3,2,1,0:T(8,128)(2,1)}, bf16[1,1,2,2,2,32,768]{6,5,4,3,2,1,0:T(8,128)(2,1)}, u32[]{:S(2)}, u32[]{:S(2)}) %collective-permute-start.3) | collective-permute-done | bytes 393248 | tf_op jit(solution)/shard_map/ppermute | solution.py:201
  186.0 30.4 %collective-permute-done.20 = bf16[1,1,2,2,2,24,3072]{6,5,4,3,2,1,0:T(8,128)(2,1)} collective-permute-done((bf16[1,1,2,2,2,24,3072]{6,5,4,3,2,1,0:T(8,128)(2,1)}, bf16[1,1,2,2,2,24,3072]{6,5,4,3,2,1,0:T(8,128)(2,1)}, u32[]{:S(2)}, u32[]{:S(2)}) %collective-permute-start.20) | collective-permute-done | bytes 1179680 | tf_op jit(solution)/shard_map/ppermute | solution.py:201
  219.7 21.9 %collective-permute-done.25 = bf16[1,1,2,2,2,24,3072]{6,5,4,3,2,1,0:T(8,128)(2,1)} collective-permute-done((bf16[1,1,2,2,2,24,3072]{6,5,4,3,2,1,0:T(8,128)(2,1)}, bf16[1,1,2,2,2,24,3072]{6,5,4,3,2,1,0:T(8,128)(2,1)}, u32[]{:S(2)}, u32[]{:S(2)}) %collective-permute-start.25) | collective-permute-done | bytes 1179680 | tf_op jit(solution)/shard_map/ppermute | solution.py:201
  256.6 31.9 %copy.295 = bf16[2,1,1572,768]{3,0,2,1:T(2,128)(2,1)} copy(bf16[2,1,1572,768]{3,2,1,0:T(8,128)(2,1)S(1)} %maximum_select_fusion.1) | data formatting | bytes 9658368 | tf_op jit(solution)/shard_map/jit(_where)/select_n | solution.py:207
  405.1 10.1 collective-permute-done.32
  416.4 9.4 collective-permute-done.33
  428.7 16.1 %collective-permute-done.34 = bf16[2,2,1,128,768]{4,3,2,1,0:T(8,128)(2,1)} collective-permute-done((bf16[2,2,1,128,768]{4,3,2,1,0:T(8,128)(2,1)S(1)}, bf16[2,2,1,128,768]{4,3,2,1,0:T(8,128)(2,1)}, u32[]{:S(2)}, u32[]{:S(2)}) %collective-permute-start.34) | collective-permute-done | bytes 786464 | tf_op jit(solution)/shard_map/ppermute | solution.py:201
  457.0 11.0 %select_n.1446 = bf16[6288,768]{1,0:T(8,128)(2,1)} reshape(bf16[2,2,1572,768]{3,2,1,0:T(8,128)(2,1)} %maximum_select_fusion) | data formatting | bytes 19316736 | tf_op jit(solution)/shard_map/jit(_where)/select_n | solution.py:207
  468.0 18.2 %fusion.246 = (f32[1024]{0:T(1024)S(1)}, f32[1024,6288]{0,1:T(8,128)}) fusion(bf16[1024,768]{1,0:T(8,128)(2,1)} %bitcast.613, bf16[6288,768]{1,0:T(8,128)(2,1)} %select_n.1446), kind=kOutput, calls=%fused_computation.673 | convolution fusion | flops 9896606720 | bytes 36990976 | tf_op jit(solution)/shard_map/dot_general | solution.py:35
  486.2 11.9 %fusion.7 = (f32[1024]{0:T(1024)S(1)}, f32[1024]{0:T(1024)S(1)}) fusion(f32[1024,6288]{0,1:T(8,128)} %get-tuple-element.336, f32[1024]{0:T(1024)S(1)} %get-tuple-element.335, s32[1024]{0:T(1024)S(1)} %fusion.140), kind=kLoop, calls=%fused_computation.31 | loop fusion | flops 32192512 | bytes 25772032 | tf_op jit(solution)/shard_map/reduce_sum | solution.py:428
  510.7 18.6 %multiply_convert_fusion.4 = bf16[1024,768]{1,0:T(8,128)(2,1)S(1)} fusion(bf16[6288,768]{1,0:T(8,128)(2,1)} %select_n.1446, f32[1024,6288]{0,1:T(8,128)} %get-tuple-element.336, f32[1024]{0:T(1024)S(1)} %get-tuple-element.335, f32[1024]{0:T(1024)S(1)} %get-tuple-element.317), kind=kOutput, calls=%fused_computation.128 | convolution fusion | flops 9904619520 | bytes 36995072 | tf_op jit(solution)/shard_map/dot_general | solution.py:25
  535.3 10.2 collective-permute-done.42
  548.3 21.9 %fusion.16 = bf16[6288,768]{1,0:T(8,128)(2,1)} fusion(bf16[1024,768]{1,0:T(8,128)(2,1)} %bitcast.614, f32[1024,6288]{0,1:T(8,128)} %get-tuple-element.336, f32[1024]{0:T(1024)S(1)} %get-tuple-element.223, s32[1024]{0:T(1024)S(1)} %fusion.140, f32[1024]{0:T(1024)S(1)} %get-tuple-element.318), kind=kOutput, calls=%fused_computation.51 | convolution fusion | flops 9933631488 | bytes 36999168 | tf_op jit(solution)/shard_map/dot_general | solution.py:29
  570.3 11.0 reshape.5404
  587.1 31.9 %copy.298 = bf16[2,1,1572,768]{3,0,2,1:T(2,128)(2,1)} copy(bf16[2,1,1572,768]{3,2,1,0:T(8,128)(2,1)S(1)} %constant_dynamic-slice_fusion.34) | data formatting | bytes 9658368 | tf_op jit(solution)/shard_map/jit(dynamic_index_in_dim)/dynamic_slice | solution.py:223
  624.0 10.1 convert_reduce_fusion.1
  634.1 8.9 convolution_convert_fusion.3
  667.3 9.7 multiply_reduce_fusion.1
  677.0 7.4 multiply_convert_fusion.1
  698.4 9.1 convert_reduce_fusion
  735.2 9.7 multiply_reduce_fusion
  744.8 7.4 multiply_convert_fusion
  792.8 9.4 collective-permute-done.46
  855.7 17.8 %all-to-all-done.4 = bf16[32,32,768]{2,1,0:T(8,128)(2,1)} async-done(((bf16[32,32,768]{2,1,0:T(8,128)(2,1)}), bf16[32,32,768]{2,1,0:T(8,128)(2,1)}, u32[]{:S(2)}, u32[]{:S(2)}) %all-to-all-start.4) | async-done | bytes 1572896 | tf_op jit(solution)/shard_map/all_to_all | solution.py:498
  897.7 23.3 %collective-permute-done.51 = bf16[1,1,2,2,2,24,3072]{6,5,4,3,2,1,0:T(8,128)(2,1)} collective-permute-done((bf16[1,1,2,2,2,24,3072]{6,5,4,3,2,1,0:T(8,128)(2,1)}, bf16[1,1,2,2,2,24,3072]{6,5,4,3,2,1,0:T(8,128)(2,1)}, u32[]{:S(2)}, u32[]{:S(2)}) %collective-permute-start.51) | collective-permute-done | bytes 1179680 | tf_op jit(solution)/shard_map/ppermute | solution.py:201
  927.9 10.5 collective-permute-done.57
  969.1 8.9 collective-permute-done.53
  981.7 39.7 %collective-permute-done.59 = bf16[1,1,1,1,1,24,3072]{6,5,4,3,2,1,0:T(8,128)(2,1)S(1)} collective-permute-done((bf16[1,1,1,1,1,24,3072]{6,5,4,3,2,1,0:T(8,128)(2,1)S(1)}, bf16[1,1,1,1,1,24,3072]{6,5,4,3,2,1,0:T(8,128)(2,1)S(1)}, u32[]{:S(2)}, u32[]{:S(2)}) %collective-permute-start.59) | collective-permute-done | bytes 147488 | tf_op jit(solution)/shard_map/ppermute | solution.py:201
  1021.5 7.4 collective-permute-done.54
  1082.1 9.3 multiply_subtract_fusion
  (1036 shorter events, 601.7 us)
Async XLA Ops:
  13.2 75.5 %collective-permute-start.13 = (bf16[384,768]{1,0:T(8,128)(2,1)}, bf16[384,768]{1,0:T(8,128)(2,1)}, u32[]{:S(2)}, u32[]{:S(2)}) collective-permute-start(bf16[384,768]{1,0:T(8,128)(2,1)} %convert_bitcast_fusion.1), channel_id=1, source_target_pairs={{4,8},{8,4},{5,9},{9,5},{6,10},{10,6},{7,11},{11,7},{20,24},{24,20... | collective-permute-start | bytes 1769480 | tf_op jit(solution)/shard_map/ppermute | solution.py:290
  27.9 56.4 %collective-permute-start.9 = (bf16[96,3072]{1,0:T(8,128)(2,1)}, bf16[96,3072]{1,0:T(8,128)(2,1)}, u32[]{:S(2)}, u32[]{:S(2)}) collective-permute-start(bf16[96,3072]{1,0:T(8,128)(2,1)} %slice.326), channel_id=1, source_target_pairs={{4,8},{8,4},{5,9},{9,5},{6,10},{10,6},{7,11},{11,7},{20,24},{24,20... | collective-permute-start | bytes 1769480 | tf_op jit(solution)/shard_map/ppermute | solution.py:290
  40.8 212.2 %collective-permute-start.35 = (bf16[1,1,1572,768]{3,2,1,0:T(8,128)(2,1)}, bf16[1,1,1572,768]{3,2,1,0:T(8,128)(2,1)}, u32[]{:S(2)}, u32[]{:S(2)}) collective-permute-start(bf16[1,1,1572,768]{3,2,1,0:T(8,128)(2,1)} %convert_bitcast_fusion.7), channel_id=1, source_target_pairs={{0,16},{16,0},{1,17},{17,1},{2,18},{18,2},{3,19},{19,3},{4,20},{20... | collective-permute-start | bytes 7243784 | tf_op jit(solution)/shard_map/ppermute | solution.py:201
  75.4 61.0 %collective-permute-start.24 = (bf16[1,1,2,2,1,24,3072]{6,5,4,3,2,1,0:T(8,128)(2,1)}, bf16[1,1,2,2,1,24,3072]{6,5,4,3,2,1,0:T(8,128)(2,1)S(1)}, u32[]{:S(2)}, u32[]{:S(2)}) collective-permute-start(bf16[1,1,2,2,1,24,3072]{6,5,4,3,2,1,0:T(8,128)(2,1)} %maximum_select_fusion.32), channel_id=1, source_target_pairs={{0,1},{1,0},{2,3},{3,2},{4,5},{5,4},{6,7},{7,6},{8,9},{9,8},{10,11... | collective-permute-start | bytes 1769480 | tf_op jit(solution)/shard_map/ppermute | solution.py:201
  84.3 56.9 %collective-permute-start.29 = (bf16[1,1,2,2,1,96,768]{6,5,4,3,2,1,0:T(8,128)(2,1)}, bf16[1,1,2,2,1,96,768]{6,5,4,3,2,1,0:T(8,128)(2,1)}, u32[]{:S(2)}, u32[]{:S(2)}) collective-permute-start(bf16[1,1,2,2,1,96,768]{6,5,4,3,2,1,0:T(8,128)(2,1)} %maximum_select_fusion.34), channel_id=1, source_target_pairs={{0,1},{1,0},{2,3},{3,2},{4,5},{5,4},{6,7},{7,6},{8,9},{9,8},{10,11... | collective-permute-start | bytes 1769480 | tf_op jit(solution)/shard_map/ppermute | solution.py:201
  88.7 43.9 %collective-permute-start.19 = (bf16[1,1,2,2,1,24,3072]{6,5,4,3,2,1,0:T(8,128)(2,1)}, bf16[1,1,2,2,1,24,3072]{6,5,4,3,2,1,0:T(8,128)(2,1)}, u32[]{:S(2)}, u32[]{:S(2)}) collective-permute-start(bf16[1,1,2,2,1,24,3072]{6,5,4,3,2,1,0:T(8,128)(2,1)} %copy.275), channel_id=1, source_target_pairs={{0,1},{1,0},{2,3},{3,2},{4,5},{5,4},{6,7},{7,6},{8,9},{9,8},{10,11... | collective-permute-start | bytes 1769480 | tf_op jit(solution)/shard_map/ppermute | solution.py:201
  108.4 47.7 %collective-permute-start.14 = (bf16[1,1,1,384,768]{4,3,2,1,0:T(8,128)(2,1)}, bf16[1,1,1,384,768]{4,3,2,1,0:T(8,128)(2,1)}, u32[]{:S(2)}, u32[]{:S(2)}) collective-permute-start(bf16[1,1,1,384,768]{4,3,2,1,0:T(8,128)(2,1)} %get-tuple-element.251), channel_id=1, source_target_pairs={{0,2},{2,0},{1,3},{3,1},{4,6},{6,4},{5,7},{7,5},{8,10},{10,8},{9,1... | collective-permute-start | bytes 1769480 | tf_op jit(solution)/shard_map/ppermute | solution.py:201
  156.2 60.2 %collective-permute-start.20 = (bf16[1,1,2,2,2,24,3072]{6,5,4,3,2,1,0:T(8,128)(2,1)}, bf16[1,1,2,2,2,24,3072]{6,5,4,3,2,1,0:T(8,128)(2,1)}, u32[]{:S(2)}, u32[]{:S(2)}) collective-permute-start(bf16[1,1,2,2,2,24,3072]{6,5,4,3,2,1,0:T(8,128)(2,1)} %maximum_select_fusion.22), channel_id=1, source_target_pairs={{0,16},{16,0},{1,17},{17,1},{2,18},{18,2},{3,19},{19,3},{4,20},{20... | collective-permute-start | bytes 3538952 | tf_op jit(solution)/shard_map/ppermute | solution.py:201
  162.1 79.5 %collective-permute-start.25 = (bf16[1,1,2,2,2,24,3072]{6,5,4,3,2,1,0:T(8,128)(2,1)}, bf16[1,1,2,2,2,24,3072]{6,5,4,3,2,1,0:T(8,128)(2,1)}, u32[]{:S(2)}, u32[]{:S(2)}) collective-permute-start(bf16[1,1,2,2,2,24,3072]{6,5,4,3,2,1,0:T(8,128)(2,1)} %maximum_select_fusion.24), channel_id=1, source_target_pairs={{0,16},{16,0},{1,17},{17,1},{2,18},{18,2},{3,19},{19,3},{4,20},{20... | collective-permute-start | bytes 3538952 | tf_op jit(solution)/shard_map/ppermute | solution.py:201
  167.4 79.8 %collective-permute-start.15 = (bf16[1,2,1,384,768]{4,3,2,1,0:T(8,128)(2,1)}, bf16[1,2,1,384,768]{4,3,2,1,0:T(8,128)(2,1)}, u32[]{:S(2)}, u32[]{:S(2)}) collective-permute-start(bf16[1,2,1,384,768]{4,3,2,1,0:T(8,128)(2,1)} %maximum_select_fusion.20), channel_id=1, source_target_pairs={{0,1},{1,0},{2,3},{3,2},{4,5},{5,4},{6,7},{7,6},{8,9},{9,8},{10,11... | collective-permute-start | bytes 3538952 | tf_op jit(solution)/shard_map/ppermute | solution.py:201
  168.9 122.0 %all-to-all-start.3 = ((bf16[32,32,768]{2,1,0:T(8,128)(2,1)}), bf16[32,32,768]{2,1,0:T(8,128)(2,1)}, u32[]{:S(2)}, u32[]{:S(2)}) async-start(bf16[32,32,768]{2,1,0:T(8,128)(2,1)} %bitcast.537), calls=%async_computation.3 | async-start | bytes 3145728 | tf_op jit(solution)/shard_map/all_to_all | solution.py:386
  178.4 72.3 %collective-permute-start.11 = (bf16[1,1,2,96,3072]{4,3,2,1,0:T(8,128)(2,1)S(1)}, bf16[1,1,2,96,3072]{4,3,2,1,0:T(8,128)(2,1)S(1)}, u32[]{:S(2)}, u32[]{:S(2)}) collective-permute-start(bf16[1,1,2,96,3072]{4,3,2,1,0:T(8,128)(2,1)S(1)} %copy-done.91), channel_id=1, source_target_pairs={{0,2},{2,0},{1,3},{3,1},{4,6},{6,4},{5,7},{7,5},{8,10},{10,8},{9,1... | collective-permute-start | bytes 3538952 | tf_op jit(solution)/shard_map/ppermute | solution.py:201
  216.3 72.2 %collective-permute-start.7 = (bf16[1,2,1,96,3072]{4,3,2,1,0:T(8,128)(2,1)S(1)}, bf16[1,2,1,96,3072]{4,3,2,1,0:T(8,128)(2,1)S(1)}, u32[]{:S(2)}, u32[]{:S(2)}) collective-permute-start(bf16[1,2,1,96,3072]{4,3,2,1,0:T(8,128)(2,1)S(1)} %maximum_select_fusion.16), channel_id=1, source_target_pairs={{0,1},{1,0},{2,3},{3,2},{4,5},{5,4},{6,7},{7,6},{8,9},{9,8},{10,11... | collective-permute-start | bytes 3538952 | tf_op jit(solution)/shard_map/ppermute | solution.py:201
  241.6 59.8 %collective-permute-start.21 = (bf16[2,1,2,2,2,24,3072]{6,5,4,3,2,1,0:T(8,128)(2,1)}, bf16[2,1,2,2,2,24,3072]{6,5,4,3,2,1,0:T(8,128)(2,1)}, u32[]{:S(2)}, u32[]{:S(2)}) collective-permute-start(bf16[2,1,2,2,2,24,3072]{6,5,4,3,2,1,0:T(8,128)(2,1)} %maximum_select_fusion.11), channel_id=1, source_target_pairs={{0,8},{8,0},{1,9},{9,1},{2,10},{10,2},{3,11},{11,3},{4,12},{12,4},... | collective-permute-start | bytes 7077896 | tf_op jit(solution)/shard_map/ppermute | solution.py:201
  247.2 61.4 %collective-permute-start.26 = (bf16[2,1,2,2,2,24,3072]{6,5,4,3,2,1,0:T(8,128)(2,1)}, bf16[2,1,2,2,2,24,3072]{6,5,4,3,2,1,0:T(8,128)(2,1)}, u32[]{:S(2)}, u32[]{:S(2)}) collective-permute-start(bf16[2,1,2,2,2,24,3072]{6,5,4,3,2,1,0:T(8,128)(2,1)} %maximum_select_fusion.12), channel_id=1, source_target_pairs={{0,8},{8,0},{1,9},{9,1},{2,10},{10,2},{3,11},{11,3},{4,12},{12,4},... | collective-permute-start | bytes 7077896 | tf_op jit(solution)/shard_map/ppermute | solution.py:201
  250.7 65.1 %collective-permute-start.31 = (bf16[2,1,2,2,2,96,768]{6,5,4,3,2,1,0:T(8,128)(2,1)}, bf16[2,1,2,2,2,96,768]{6,5,4,3,2,1,0:T(8,128)(2,1)}, u32[]{:S(2)}, u32[]{:S(2)}) collective-permute-start(bf16[2,1,2,2,2,96,768]{6,5,4,3,2,1,0:T(8,128)(2,1)} %maximum_select_fusion.13), channel_id=1, source_target_pairs={{0,8},{8,0},{1,9},{9,1},{2,10},{10,2},{3,11},{11,3},{4,12},{12,4},... | collective-permute-start | bytes 7077896 | tf_op jit(solution)/shard_map/ppermute | solution.py:201
  253.0 69.7 %collective-permute-start.16 = (bf16[1,2,2,384,768]{4,3,2,1,0:T(8,128)(2,1)}, bf16[1,2,2,384,768]{4,3,2,1,0:T(8,128)(2,1)}, u32[]{:S(2)}, u32[]{:S(2)}) collective-permute-start(bf16[1,2,2,384,768]{4,3,2,1,0:T(8,128)(2,1)} %maximum_select_fusion.10), channel_id=1, source_target_pairs={{0,8},{8,0},{1,9},{9,1},{2,10},{10,2},{3,11},{11,3},{4,12},{12,4},... | collective-permute-start | bytes 7077896 | tf_op jit(solution)/shard_map/ppermute | solution.py:201
  308.6 138.9 %collective-permute-start.36 = (bf16[2,1,1572,768]{3,0,2,1:T(2,128)(2,1)}, bf16[2,1,1572,768]{3,0,2,1:T(2,128)(2,1)}, u32[]{:S(2)}, u32[]{:S(2)}) collective-permute-start(bf16[2,1,1572,768]{3,0,2,1:T(2,128)(2,1)} %copy.295), channel_id=1, source_target_pairs={{0,8},{8,0},{1,9},{9,1},{2,10},{10,2},{3,11},{11,3},{4,12},{12,4},... | collective-permute-start | bytes 14487560 | tf_op jit(solution)/shard_map/ppermute | solution.py:201
  619.0 260.5 %collective-permute-start.40 = (bf16[2,1,1572,768]{3,0,2,1:T(2,128)(2,1)}, bf16[2,1,1572,768]{3,0,2,1:T(2,128)(2,1)}, u32[]{:S(2)}, u32[]{:S(2)}) collective-permute-start(bf16[2,1,1572,768]{3,0,2,1:T(2,128)(2,1)} %copy.298), channel_id=1, source_target_pairs={{0,8},{8,0},{1,9},{9,1},{2,10},{10,2},{3,11},{11,3},{4,12},{12,4},... | collective-permute-start | bytes 14487560 | tf_op jit(solution)/shard_map/ppermute | solution.py:201
  767.5 52.6 %collective-permute-start.60 = (bf16[2,1,2,2,2,96,768]{6,5,4,3,2,1,0:T(8,128)(2,1)}, bf16[2,1,2,2,2,96,768]{6,5,4,3,2,1,0:T(8,128)(2,1)}, u32[]{:S(2)}, u32[]{:S(2)}) collective-permute-start(bf16[2,1,2,2,2,96,768]{6,5,4,3,2,1,0:T(8,128)(2,1)} %constant_dynamic-slice_fusion.15), channel_id=1, source_target_pairs={{0,8},{8,0},{1,9},{9,1},{2,10},{10,2},{3,11},{11,3},{4,12},{12,4},... | collective-permute-start | bytes 7077896 | tf_op jit(solution)/shard_map/ppermute | solution.py:201
  768.0 48.0 %collective-permute-start.55 = (bf16[2,1,2,2,2,24,3072]{6,5,4,3,2,1,0:T(8,128)(2,1)}, bf16[2,1,2,2,2,24,3072]{6,5,4,3,2,1,0:T(8,128)(2,1)}, u32[]{:S(2)}, u32[]{:S(2)}) collective-permute-start(bf16[2,1,2,2,2,24,3072]{6,5,4,3,2,1,0:T(8,128)(2,1)} %constant_dynamic-slice_fusion.20), channel_id=1, source_target_pairs={{0,8},{8,0},{1,9},{9,1},{2,10},{10,2},{3,11},{11,3},{4,12},{12,4},... | collective-permute-start | bytes 7077896 | tf_op jit(solution)/shard_map/ppermute | solution.py:201
  775.1 49.4 %collective-permute-start.50 = (bf16[2,1,2,2,2,24,3072]{6,5,4,3,2,1,0:T(8,128)(2,1)}, bf16[2,1,2,2,2,24,3072]{6,5,4,3,2,1,0:T(8,128)(2,1)}, u32[]{:S(2)}, u32[]{:S(2)}) collective-permute-start(bf16[2,1,2,2,2,24,3072]{6,5,4,3,2,1,0:T(8,128)(2,1)} %constant_dynamic-slice_fusion.25), channel_id=1, source_target_pairs={{0,8},{8,0},{1,9},{9,1},{2,10},{10,2},{3,11},{11,3},{4,12},{12,4},... | collective-permute-start | bytes 7077896 | tf_op jit(solution)/shard_map/ppermute | solution.py:201
  824.5 62.1 %collective-permute-start.61 = (bf16[1,1,2,2,2,96,768]{6,5,4,3,2,1,0:T(8,128)(2,1)}, bf16[1,1,2,2,2,96,768]{6,5,4,3,2,1,0:T(8,128)(2,1)}, u32[]{:S(2)}, u32[]{:S(2)}) collective-permute-start(bf16[1,1,2,2,2,96,768]{6,5,4,3,2,1,0:T(8,128)(2,1)} %constant_dynamic-slice_fusion.14), channel_id=1, source_target_pairs={{0,16},{16,0},{1,17},{17,1},{2,18},{18,2},{3,19},{19,3},{4,20},{20... | collective-permute-start | bytes 3538952 | tf_op jit(solution)/shard_map/ppermute | solution.py:201
  834.5 61.2 %collective-permute-start.56 = (bf16[1,1,2,2,2,24,3072]{6,5,4,3,2,1,0:T(8,128)(2,1)}, bf16[1,1,2,2,2,24,3072]{6,5,4,3,2,1,0:T(8,128)(2,1)}, u32[]{:S(2)}, u32[]{:S(2)}) collective-permute-start(bf16[1,1,2,2,2,24,3072]{6,5,4,3,2,1,0:T(8,128)(2,1)} %constant_dynamic-slice_fusion.19), channel_id=1, source_target_pairs={{0,16},{16,0},{1,17},{17,1},{2,18},{18,2},{3,19},{19,3},{4,20},{20... | collective-permute-start | bytes 3538952 | tf_op jit(solution)/shard_map/ppermute | solution.py:201
  843.8 77.3 %collective-permute-start.51 = (bf16[1,1,2,2,2,24,3072]{6,5,4,3,2,1,0:T(8,128)(2,1)}, bf16[1,1,2,2,2,24,3072]{6,5,4,3,2,1,0:T(8,128)(2,1)}, u32[]{:S(2)}, u32[]{:S(2)}) collective-permute-start(bf16[1,1,2,2,2,24,3072]{6,5,4,3,2,1,0:T(8,128)(2,1)} %constant_dynamic-slice_fusion.24), channel_id=1, source_target_pairs={{0,16},{16,0},{1,17},{17,1},{2,18},{18,2},{3,19},{19,3},{4,20},{20... | collective-permute-start | bytes 3538952 | tf_op jit(solution)/shard_map/ppermute | solution.py:201
  879.5 43.5 %collective-permute-start.70 = (bf16[1,1,2,96,3072]{4,3,2,1,0:T(8,128)(2,1)}, bf16[1,1,2,96,3072]{4,3,2,1,0:T(8,128)(2,1)}, u32[]{:S(2)}, u32[]{:S(2)}) collective-permute-start(bf16[1,1,2,96,3072]{4,3,2,1,0:T(8,128)(2,1)} %constant_dynamic-slice_fusion.6), channel_id=1, source_target_pairs={{0,2},{2,0},{1,3},{3,1},{4,6},{6,4},{5,7},{7,5},{8,10},{10,8},{9,1... | collective-permute-start | bytes 3538952 | tf_op jit(solution)/shard_map/ppermute | solution.py:201
  886.6 152.0 %collective-permute-start.41 = (bf16[1,1,1572,768]{3,2,1,0:T(8,128)(2,1)S(1)}, bf16[1,1,1572,768]{3,2,1,0:T(8,128)(2,1)S(1)}, u32[]{:S(2)}, u32[]{:S(2)}) collective-permute-start(bf16[1,1,1572,768]{3,2,1,0:T(8,128)(2,1)S(1)} %constant_dynamic-slice_fusion.33), channel_id=1, source_target_pairs={{0,16},{16,0},{1,17},{17,1},{2,18},{18,2},{3,19},{19,3},{4,20},{20... | collective-permute-start | bytes 7243784 | tf_op jit(solution)/shard_map/ppermute | solution.py:201
  895.7 43.4 %collective-permute-start.62 = (bf16[1,1,2,2,1,96,768]{6,5,4,3,2,1,0:T(8,128)(2,1)S(1)}, bf16[1,1,2,2,1,96,768]{6,5,4,3,2,1,0:T(8,128)(2,1)S(1)}, u32[]{:S(2)}, u32[]{:S(2)}) collective-permute-start(bf16[1,1,2,2,1,96,768]{6,5,4,3,2,1,0:T(8,128)(2,1)S(1)} %constant_dynamic-slice_fusion.13), channel_id=1, source_target_pairs={{0,1},{1,0},{2,3},{3,2},{4,5},{5,4},{6,7},{7,6},{8,9},{9,8},{10,11... | collective-permute-start | bytes 1769480 | tf_op jit(solution)/shard_map/ppermute | solution.py:201
  966.5 70.4 %collective-permute-start.76 = (bf16[384,768]{1,0:T(8,128)(2,1)S(1)}, bf16[384,768]{1,0:T(8,128)(2,1)S(1)}, u32[]{:S(2)}, u32[]{:S(2)}) collective-permute-start(bf16[384,768]{1,0:T(8,128)(2,1)S(1)} %fusion.99), channel_id=1, source_target_pairs={{4,8},{8,4},{5,9},{9,5},{6,10},{10,6},{7,11},{11,7},{20,24},{24,20... | collective-permute-start | bytes 1769480 | tf_op jit(solution)/shard_map/ppermute | solution.py:290
  968.3 67.2 %collective-permute-start.72 = (bf16[96,3072]{1,0:T(8,128)(2,1)S(1)}, bf16[96,3072]{1,0:T(8,128)(2,1)S(1)}, u32[]{:S(2)}, u32[]{:S(2)}) collective-permute-start(bf16[96,3072]{1,0:T(8,128)(2,1)S(1)} %fusion.98), channel_id=1, source_target_pairs={{4,8},{8,4},{5,9},{9,5},{6,10},{10,6},{7,11},{11,7},{20,24},{24,20... | collective-permute-start | bytes 1769480 | tf_op jit(solution)/shard_map/ppermute | solution.py:290
  978.0 57.7 %collective-permute-start.68 = (bf16[96,3072]{1,0:T(8,128)(2,1)S(1)}, bf16[96,3072]{1,0:T(8,128)(2,1)S(1)}, u32[]{:S(2)}, u32[]{:S(2)}) collective-permute-start(bf16[96,3072]{1,0:T(8,128)(2,1)S(1)} %fusion.97), channel_id=1, source_target_pairs={{4,8},{8,4},{5,9},{9,5},{6,10},{10,6},{7,11},{11,7},{20,24},{24,20... | collective-permute-start | bytes 1769480 | tf_op jit(solution)/shard_map/ppermute | solution.py:290
  979.0 42.4 %collective-permute-start.59 = (bf16[1,1,1,1,1,24,3072]{6,5,4,3,2,1,0:T(8,128)(2,1)S(1)}, bf16[1,1,1,1,1,24,3072]{6,5,4,3,2,1,0:T(8,128)(2,1)S(1)}, u32[]{:S(2)}, u32[]{:S(2)}) collective-permute-start(bf16[1,1,1,1,1,24,3072]{6,5,4,3,2,1,0:T(8,128)(2,1)S(1)} %constant_dynamic-slice_fusion.16), channel_id=1, source_target_pairs={{0,4},{4,0},{1,5},{5,1},{2,6},{6,2},{3,7},{7,3},{8,12},{12,8},{9,1... | collective-permute-start | bytes 442376 | tf_op jit(solution)/shard_map/ppermute | solution.py:201
  (299 other events, 3385.9 us)

commit v2 on v1

v2 whole, which is shorter than its diff:
```python
import jax
import jax.numpy as jnp
from jax import lax
from jax.experimental import pallas as pl
from jax.experimental.pallas import tpu as pltpu
from jax.sharding import Mesh
from jax.sharding import PartitionSpec as P

HD = 64
D = 768
FF = 3072
NPOS = 1024
STEP = 5


SCALE = 0.125
CLIP_NORM = 0.01
RATE_MATRIX = 0.03
RATE_VECTOR = 0.5
DECAY = 0.01
EPSILON = 1e-08
BF = jnp.bfloat16
F32 = jnp.float32
NT = (((1,), (1,)), ((), ()))
TN = (((0,), (0,)), ((), ()))


def dot_plain(former, latter):
    return jnp.dot(former, latter, preferred_element_type=jnp.float32)


def dot_inner(former, latter):
    return lax.dot_general(
        former, latter, (((0,), (0,)), ((), ())), preferred_element_type=jnp.float32
    )


def dot_outer(former, latter):
    return lax.dot_general(
        former, latter, (((1,), (1,)), ((), ())), preferred_element_type=jnp.float32
    )


def layer_norm(values, scales, shifts):
    centre = values - jnp.mean(values, -1, keepdims=True)
    spread = jnp.mean(centre * centre, -1, keepdims=True)
    return centre * lax.rsqrt(spread + 1e-05) * scales + shifts


def gelu_tanh(values):
    return jax.nn.gelu(values, approximate=True)


def split_vectors(vectors, breadth, hidden):
    starts = [
        0,
        breadth,
        2 * breadth,
        3 * breadth,
        4 * breadth,
        5 * breadth,
        6 * breadth,
        7 * breadth,
        7 * breadth + hidden,
        8 * breadth + hidden,
    ]
    return [vectors[starts[position] : starts[position + 1]] for position in range(9)]


def product(former, latter, form):
    return lax.dot_general(former, latter, form, preferred_element_type=F32)


def write_mask(live_ref, mask_ref):
    keys = lax.broadcasted_iota(jnp.int32, mask_ref.shape, 0)
    queries = lax.broadcasted_iota(jnp.int32, mask_ref.shape, 1)
    allowed = (keys <= queries) & (keys < live_ref[0])
    mask_ref[...] = jnp.where(allowed, 0.0, -1e30)


def attend_kernel(live_ref, q_ref, k_ref, v_ref, out_ref, log_ref, mask_ref):
    @pl.when(pl.program_id(0) == 0)
    def _():
        write_mask(live_ref, mask_ref)

    tokens, width = q_ref.shape
    tile = tokens // 2
    for head in range(width // HD):
        cols = slice(head * HD, (head + 1) * HD)
        queries, keys, values = q_ref[:, cols] * SCALE, k_ref[:, cols], v_ref[:, cols]
        for part in range(2):
            begin, end = part * tile, (part + 1) * tile
            scores = product(keys[:end], queries[begin:end], NT) + mask_ref[:end, begin:end]
            highest = jnp.max(scores, 0, keepdims=True)
            exponent = jnp.exp(scores - highest)
            total = jnp.sum(exponent, 0, keepdims=True)
            probs = (exponent * (1.0 / total)).astype(BF)
            mixed = product(values[:end], probs, TN)
            out_ref[begin:end, cols] = mixed.T.astype(BF)
            log_ref[0, head : head + 1, begin:end] = highest + jnp.log(total)


def attend_back_kernel(live_ref, q_ref, k_ref, v_ref, grad_ref, log_ref, out_ref, mask_ref):
    @pl.when(pl.program_id(0) == 0)
    def _():
        write_mask(live_ref, mask_ref)

    tokens, width = q_ref.shape
    tile = tokens // 2
    breadth = out_ref.shape[1] // 3
    sides = [[], [], []]
    for head in range(width // HD):
        cols = slice(head * HD, (head + 1) * HD)
        queries, keys, values = q_ref[:, cols] * SCALE, k_ref[:, cols], v_ref[:, cols]
        grads = grad_ref[:, cols]
        grad_queries, grad_keys, grad_values = [], [], []
        for part in range(2):
            begin, end = part * tile, (part + 1) * tile
            scores = product(keys[:end], queries[begin:end], NT) + mask_ref[:end, begin:end]
            probs = jnp.exp(scores - log_ref[0, head : head + 1, begin:end])
            grad_out = grads[begin:end]
            grad_values.append(
                jnp.dot(probs.astype(BF), grad_out, preferred_element_type=F32)
            )
            grad_probs = product(values[:end], grad_out, NT)
            inner = jnp.sum(grad_probs * probs, 0, keepdims=True)
            grad_scores = (probs * (grad_probs - inner)).astype(BF)
            grad_keys.append(
                jnp.dot(grad_scores, queries[begin:end], preferred_element_type=F32)
            )
            grad_queries.append(product(keys[:end], grad_scores, TN).T * SCALE)
        for side, parts in ((1, grad_keys), (2, grad_values)):
            sides[side].append(
                jnp.concatenate([parts[0] + parts[1][:tile], parts[1][tile:]], 0)
            )
        sides[0].append(jnp.concatenate(grad_queries, 0))
    place = pl.program_id(0) * width
    for side in range(3):
        start = pl.multiple_of(side * breadth + place, width)
        out_ref[:, pl.ds(start, width)] = jnp.concatenate(sides[side], 1).astype(BF)


def attend(joined, live_len):
    tokens, breadth = joined.shape[0], joined.shape[1] // 3
    width = 2 * HD
    pairs = breadth // width
    parts = [
        pl.BlockSpec((tokens, width), lambda i, n, side=side: (0, side * pairs + i))
        for side in range(3)
    ]
    return pl.pallas_call(
        attend_kernel,
        grid_spec=pltpu.PrefetchScalarGridSpec(
            num_scalar_prefetch=1,
            grid=(pairs,),
            in_specs=parts,
            out_specs=[
                pl.BlockSpec((tokens, width), lambda i, n: (0, i)),
                pl.BlockSpec((1, 2, tokens), lambda i, n: (i, 0, 0)),
            ],
            scratch_shapes=[pltpu.VMEM((tokens, tokens), F32)],
        ),
        out_shape=[
            jax.ShapeDtypeStruct((tokens, breadth), BF),
            jax.ShapeDtypeStruct((pairs, 2, tokens), F32),
        ],
        compiler_params=pltpu.CompilerParams(vmem_limit_bytes=32 << 20),
        cost_estimate=pl.CostEstimate(
            flops=4 * tokens * tokens * breadth,
            bytes_accessed=8 * tokens * breadth,
            transcendentals=tokens * tokens * breadth // HD,
        ),
    )(live_len.reshape(1), joined, joined, joined)


def attend_back(joined, log_total, grad_mixed, live_len):
    tokens, breadth = grad_mixed.shape
    width = 2 * HD
    pairs = breadth // width
    parts = [
        pl.BlockSpec((tokens, width), lambda i, n, side=side: (0, side * pairs + i))
        for side in range(3)
    ]
    return pl.pallas_call(
        attend_back_kernel,
        grid_spec=pltpu.PrefetchScalarGridSpec(
            num_scalar_prefetch=1,
            grid=(pairs,),
            in_specs=parts
            + [
                pl.BlockSpec((tokens, width), lambda i, n: (0, i)),
                pl.BlockSpec((1, 2, tokens), lambda i, n: (i, 0, 0)),
            ],
            out_specs=pl.BlockSpec((tokens, 3 * breadth), lambda i, n: (0, 0)),
            scratch_shapes=[pltpu.VMEM((tokens, tokens), F32)],
        ),
        out_shape=jax.ShapeDtypeStruct((tokens, 3 * breadth), BF),
        compiler_params=pltpu.CompilerParams(vmem_limit_bytes=32 << 20),
        cost_estimate=pl.CostEstimate(
            flops=10 * tokens * tokens * breadth,
            bytes_accessed=14 * tokens * breadth,
            transcendentals=tokens * tokens * breadth // HD,
        ),
    )(live_len.reshape(1), joined, joined, joined, grad_mixed, log_total)


def fence(*arrays):
    return lax.optimization_barrier(arrays)


class Tree:
    def tied(self):
        return [self.held] if self.other is None else [self.held, self.other]

    def retie(self, arrays):
        self.held = arrays[0]
        if self.other is not None:
            self.other = arrays[1]

    def step(self):
        if self.other is None:
            self.send()
        else:
            self.advance()

    def result(self):
        while self.open:
            self.step()
        return self.final()


class Gather(Tree):
    def __init__(self, block, names, order, waits=(), lazy=False):
        self.names, self.order, self.rows, self.waits = names, list(order), block.shape, list(waits)
        self.held = block.reshape((1,) * len(names) + block.shape)
        self.other = None
        if not lazy:
            self.send()

    def send(self):
        self.other = across(self.held, self.order[0])

    def advance(self):
        name = self.order.pop(0)
        dim, low_side = self.names.index(name), lax.axis_index(name) == 0
        self.held = jnp.where(
            low_side,
            jnp.concatenate([self.held, self.other], dim),
            jnp.concatenate([self.other, self.held], dim),
        )
        self.other = None
        if self.order:
            self.send()

    @property
    def open(self):
        return bool(self.order)

    def final(self):
        return self.held.reshape((-1,) + self.rows[1:])


class Reduce(Tree):
    def __init__(self, blocks, names, order, after=None, waits=(), lazy=False):
        self.names, self.order, self.after, self.waits = names, list(order), after, list(waits)
        self.tail = blocks.shape[1:]
        self.held = blocks.reshape((2,) * len(names) + (-1,) + self.tail)
        self.other = None
        if not lazy:
            self.send()

    def send(self):
        if self.order:
            name = self.order[0]
            dim, side = self.names.index(name), lax.axis_index(name)
            self.other = across(lax.dynamic_index_in_dim(self.held, 1 - side, dim, True), name)
            self.held = lax.dynamic_index_in_dim(self.held, side, dim, True)
        else:
            self.held = self.held.astype(BF)
            self.other = self.after[0](self.held)

    def advance(self):
        if self.order:
            self.order.pop(0)
            total = self.held.astype(F32) + self.other.astype(F32)
            self.held = total.astype(BF) if self.order else total
        else:
            self.held = self.after[1](self.held, self.other)
            self.after = None
        self.other = None
        if self.open:
            self.send()

    @property
    def open(self):
        return bool(self.order) or self.after is not None

    def final(self):
        return self.held.astype(F32).reshape((-1,) + self.tail)


class Exchange(Tree):
    def __init__(self, packet, names, waits):
        self.held, self.names, self.waits = packet, names, list(waits)
        self.other, self.open = None, True

    def send(self):
        self.other = lax.all_to_all(self.held, self.names, 0, 0, tiled=True)

    def advance(self):
        self.open = False

    def final(self):
        return self.other


def meet(carry, trees):
    due = []
    for tree in trees:
        if tree.open:
            if tree.waits and tree.waits[0] > 0:
                tree.waits[0] -= 1
            else:
                tree.waits = tree.waits[1:]
                due.append(tree)
    flat, spans = list(carry), []
    for tree in due:
        start = len(flat)
        flat += tree.tied()
        spans.append((start, len(flat)))
    flat = fence(*flat)
    for tree, (start, stop) in zip(due, spans):
        tree.retie(flat[start:stop])
        tree.step()
    return flat[: len(carry)]


def core_half(active, lead, side):
    width = active.shape[1] // (2 * lead)
    if width % 128:
        pieces = [
            active[:, (2 * part + core) * width : (2 * part + core + 1) * width]
            for core in range(2)
            for part in range(lead)
        ]
        active, lead, width = jnp.concatenate(pieces, 1), 1, width * lead
    pieces = [
        lax.dynamic_slice_in_dim(active, (2 * part + side) * width, width, 1)
        for part in range(lead)
    ]
    return pieces[0] if lead == 1 else jnp.concatenate(pieces, 1)


def core_reduce(active, grad, lead):
    side = lax.axis_index("core")
    send = dot_inner(core_half(active, lead, 1 - side), grad).astype(BF)
    other = across(send, "core")
    return (dot_inner(core_half(active, lead, side), grad) + other.astype(F32)).astype(BF)


def settled(weight):
    return weight.result() if isinstance(weight, Tree) else weight


def layer_forward(inputs, weights, vectors, live_len, meets):
    breadth = inputs.shape[1]
    parts = split_vectors(vectors, breadth, vectors.shape[0] - 8 * breadth)
    normed = layer_norm(inputs, parts[0], parts[1]).astype(jnp.bfloat16)
    shift_qkv = jnp.concatenate([parts[2], jnp.zeros_like(parts[2]), parts[3]])
    qkvo = settled(weights[0])
    joined = (dot_plain(normed, qkvo[:, : 3 * breadth]) + shift_qkv).astype(jnp.bfloat16)
    mixed_out, log_totals = attend(joined, live_len)
    (mixed_out,) = meet([mixed_out], meets[0])
    middle = inputs + (dot_plain(mixed_out, qkvo[:, 3 * breadth :]) + parts[4])
    normed_two = layer_norm(middle, parts[5], parts[6]).astype(jnp.bfloat16)
    fore = settled(weights[1])
    pre_act = dot_plain(normed_two, fore) + parts[7]
    activ = gelu_tanh(pre_act).astype(jnp.bfloat16)
    (activ,) = meet([activ], meets[1])
    down = settled(weights[2])
    output = middle + (dot_plain(activ, down) + parts[8])
    return (
        output,
        (inputs, normed, joined, mixed_out, log_totals, middle, normed_two, pre_act, activ),
        (qkvo, fore, down),
    )


def layer_backward(grad_out, saved, weights, vectors, live_len, lead, trees, launch):
    inputs, normed, joined, mixed_out, log_totals, middle, normed_two, pre_act, activ = saved
    qkvo, fore, down = weights
    breadth = inputs.shape[1]
    parts = split_vectors(vectors, breadth, down.shape[0])
    grad_y = grad_out.astype(jnp.bfloat16)
    part_down = core_reduce(activ, grad_y, lead)
    grad_act = dot_outer(grad_y, down)
    grad_pre = jax.vjp(gelu_tanh, pre_act)[1](grad_act)[0].astype(jnp.bfloat16)
    grad_pre, part_down = meet([grad_pre, part_down], trees)
    trees.extend(launch("down", part_down))
    part_fore = core_reduce(normed_two, grad_pre, lead)
    grad_norm_two = dot_outer(grad_pre, fore)
    grad_mid_norm, grad_scale_two, grad_shift_two = jax.vjp(layer_norm, middle, parts[5], parts[6])[
        1
    ](grad_norm_two)
    grad_mid = grad_out + grad_mid_norm
    grad_branch = grad_mid.astype(jnp.bfloat16)
    grad_branch, part_fore = meet([grad_branch, part_fore], trees)
    part_proj = core_reduce(mixed_out, grad_branch, lead)
    grad_mixed = dot_outer(grad_branch, qkvo[:, 3 * breadth :]).astype(jnp.bfloat16)
    grad_mixed, part_proj = meet([grad_mixed, part_proj], trees)
    trees.extend(launch("fore", jnp.concatenate([part_fore, part_proj], 1)))
    grad_joined = attend_back(joined, log_totals, grad_mixed, live_len)
    (grad_joined,) = meet([grad_joined], trees)
    part_qkv = core_reduce(normed, grad_joined, lead)
    grad_normed = dot_outer(grad_joined, qkvo[:, : 3 * breadth])
    grad_in_norm, grad_scale_one, grad_shift_one = jax.vjp(layer_norm, inputs, parts[0], parts[1])[
        1
    ](grad_normed)
    grad_in = grad_mid + grad_in_norm
    grad_in, part_qkv = meet([grad_in, part_qkv], trees)
    joined_sums = jnp.sum(grad_joined.astype(jnp.float32), 0)
    rows = [
        grad_scale_one,
        grad_shift_one,
        joined_sums[:breadth],
        joined_sums[2 * breadth :],
        jnp.sum(grad_branch.astype(jnp.float32), 0),
        grad_scale_two,
        grad_shift_two,
        jnp.sum(grad_pre.astype(jnp.float32), 0),
        jnp.sum(grad_y.astype(jnp.float32), 0),
    ]
    grad_vectors = jnp.concatenate([row.reshape(-1, breadth) for row in rows], 0)
    return (grad_in, grad_vectors, part_qkv)


def adamw(weight, first, second, gradient, rate, decay):
    first_new = 0.5 * first + 0.5 * gradient
    second_new = 0.5 * second + 0.5 * gradient * gradient
    first_hat = first_new / (1.0 - 0.5**STEP)
    second_hat = second_new / (1.0 - 0.5**STEP)
    weight_new = weight - rate * (first_hat / (jnp.sqrt(second_hat) + EPSILON) + decay * weight)
    return (weight_new, first_new, second_new)


FLIP = [(0, 1), (1, 0)]


def across(x, name):
    return lax.ppermute(x, name, FLIP)


def sum_bits(x, names):
    for name in names:
        x = x + across(x, name)
    return x


def per_device(
    shard_names,
    token_ids,
    lengths,
    picked,
    joining,
    embedding,
    embedding_first,
    embedding_second,
    position_table,
    position_first,
    position_second,
    shared_wide,
    shared_wide_first,
    shared_wide_second,
    shared_down,
    shared_down_first,
    shared_down_second,
    shared_vectors,
    shared_vectors_first,
    shared_vectors_second,
    private_wide,
    private_wide_first,
    private_wide_second,
    private_down,
    private_down_first,
    private_down_second,
    private_vectors,
    private_vectors_first,
    private_vectors_second,
):
    half, rest = shard_names[0], shard_names[1:]
    every = ("pair", "core") + shard_names
    crew = ("core",) + rest
    shards = 2 ** len(shard_names)
    clients = 4
    count = clients * shards
    at_pair, at_core, at_half = (lax.axis_index(n) for n in ("pair", "core", half))
    device_at = lax.axis_index(every)
    shard_at = lax.axis_index(shard_names)
    swap_pairs = []
    block = shards // 2
    for pair in range(clients // 2):
        for spot in range(block):
            former = ((pair * 2 + 0) * 2 + 1) * block + spot
            latter = ((pair * 2 + 1) * 2 + 0) * block + spot
            swap_pairs += [(former, latter), (latter, former)]

    seq_len = token_ids.shape[2]
    picks = picked.shape[2]
    slice_rows = embedding.shape[0]

    wide_b = private_wide[0].astype(BF)
    down_b = private_down[0].astype(BF)
    shared_b = shared_wide.astype(BF)
    shared_down_b = shared_down.astype(BF)
    cut = 4 * D

    ids = token_ids[0, 0]
    same = ids[:, None] == ids[None, :]
    at_row = lax.broadcasted_iota(jnp.int32, (seq_len, seq_len), 0)
    at_col = lax.broadcasted_iota(jnp.int32, (seq_len, seq_len), 1)
    first_at = jnp.min(jnp.where(same, at_col, seq_len), 1)
    is_first = first_at == jnp.arange(seq_len, dtype=jnp.int32)
    owners = ids // slice_rows
    slot = jnp.sum(
        (
            (owners[:, None] == owners[None, :]) & is_first[None, :] & (at_col < first_at[:, None])
        ).astype(jnp.int32),
        1,
    )

    vect_own = [shared_vectors, private_vectors[0]]
    pieces = [
        ids.astype(F32),
        slot.astype(F32),
        is_first.astype(F32),
        picked[0, 0].astype(F32),
        lengths[0].astype(F32),
    ] + [v.astype(BF).astype(F32) for v in vect_own]
    starts = [0]
    for piece in pieces:
        starts.append(starts[-1] + piece.shape[0])
    room = max(16, 1024 // count)
    owner_at = jnp.arange(count, dtype=jnp.int32)[:, None, None]
    room_at = jnp.arange(room, dtype=jnp.int32)[None, :, None]
    sought = (owners == owner_at) & (jnp.where(is_first, slot, -1) == room_at)
    sought = jnp.sum(jnp.where(sought, ids - owner_at * slice_rows, 0), 2).astype(F32)
    message = jnp.concatenate(pieces)
    message = jnp.broadcast_to(message, (count,) + message.shape)
    message = jnp.concatenate([message, sought], 1)
    width = message.shape[1]
    message = jnp.pad(message, ((0, 0), (0, -width % 1024))).reshape(count, -1, 128)
    def moved(x):
        return lax.ppermute(x, every, swap_pairs)

    first_moved = moved(wide_b[:, :cut])
    board = lax.all_to_all(message, every, 0, 0, tiled=True).reshape(count, -1)
    posit_b = lax.all_gather(position_table.astype(BF), every, axis=0, tiled=True)[:seq_len]
    posit_names = ("core",) + shard_names
    spread = shard_names + ("pair", "core")
    shared_one = Gather(shared_b[:, :cut], every, spread)
    board, wide_b, down_b, shared_b, shared_down_b = fence(
        board, wide_b, down_b, shared_b, shared_down_b
    )
    (board, first_moved) = meet([board, first_moved], [shared_one])
    stays = at_core == at_half
    there, back = rest + ("core",), rest[::-1] + ("core",)
    private_one = Gather(jnp.where(stays, wide_b[:, :cut], first_moved), crew, there)
    second_moved, third_moved = moved(wide_b[:, cut:]), moved(down_b)

    table_own = embedding.astype(BF)
    pad_rows = -(-slice_rows // 16) * 16
    table_four = Gather(
        jnp.pad(table_own, ((0, pad_rows - slice_rows), (0, 0))),
        ("pair", "core"),
        ("pair", "core"),
        (),
        True,
    )
    filled = jnp.where(
        jnp.arange(clients * pad_rows, dtype=jnp.int32) % pad_rows < slice_rows, 0.0, -jnp.inf
    )

    def posted(place):
        return board[:, starts[place] : starts[place + 1]]

    def hosted(x):
        x = x.reshape((clients // 2, 2, 2, block) + x.shape[1:])
        return jnp.swapaxes(x, 1, 2).reshape((count,) + x.shape[4:])

    all_ids, all_slots, all_first, all_picks, all_lens = [
        hosted(posted(place).astype(jnp.int32)) for place in range(5)
    ]
    vect_s = posted(5).reshape(-1)
    vect_p = lax.dynamic_index_in_dim(
        posted(6).reshape(clients, -1), 2 * at_pair + at_half, 0, False
    )

    all_live = all_picks < all_lens - 1
    live_counts = jnp.sum(all_live.astype(F32), 1).reshape(clients // 2, 2, 2, block)
    counts_all = jnp.sum(live_counts, (1, 3)).reshape(-1)
    joining_f = joining.astype(F32)
    share_all = joining_f / (jnp.sum(joining_f) * counts_all)

    my_ids = lax.dynamic_index_in_dim(all_ids, device_at, 0, False)
    my_slots = lax.dynamic_index_in_dim(all_slots, device_at, 0, False)
    my_picks = lax.dynamic_index_in_dim(all_picks, device_at, 0, False)
    my_len = lax.dynamic_index_in_dim(all_lens, device_at, 0, False)[0]
    my_owners = my_ids // slice_rows

    rounds = jnp.max(all_slots) // room + 1
    in_slice = all_ids - device_at * slice_rows
    wanted = (all_first > 0) & (in_slice >= 0) & (in_slice < slice_rows)

    def asked(turn):
        spots = turn * room + jnp.arange(room, dtype=jnp.int32)
        hits = wanted[:, None, :] & (all_slots[:, None, :] == spots[None, :, None])
        return jnp.sum(jnp.where(hits, in_slice[:, None, :], 0), 2).reshape(-1)

    asked_first = hosted(board[:, width - room : width].astype(jnp.int32)).reshape(-1)

    def land(turn, rows, got):
        spot = my_slots - turn * room
        here = (spot >= 0) & (spot < room)
        found = jnp.take(got, jnp.where(here, my_owners * room + spot, 0), axis=0, mode="clip")
        return jnp.where(here[:, None], found, rows)

    def fetch(turn, rows):
        sent = jnp.take(table_own, asked(turn), axis=0, mode="clip")
        return land(turn, rows, lax.all_to_all(sent, every, 0, 0, tiled=True))

    sent = jnp.take(table_own, asked_first, axis=0, mode="clip")
    (sent,) = meet([sent], [private_one, shared_one])
    got = lax.all_to_all(sent, every, 0, 0, tiled=True)
    shared_two = Gather(shared_b[:, cut:], every, spread)
    shared_three = Gather(shared_down_b, every, spread, (0, 0, 0, 0))
    second_moved, third_moved = meet([second_moved, third_moved], [private_one, shared_one])
    private_two = Gather(jnp.where(stays, wide_b[:, cut:], second_moved), crew, back)
    private_three = Gather(jnp.where(stays, down_b, third_moved), crew, there)
    (got,) = meet([got], [private_two, private_three, shared_two, shared_three])
    rows = land(0, jnp.zeros((seq_len, D), BF), got)
    rows = lax.fori_loop(1, rounds, fetch, rows)
    inputs = rows.astype(F32) + posit_b.astype(F32)

    weights_p = (private_one, private_two, private_three)
    weights_s = (shared_one, shared_two, shared_three)
    first_out, first_saved, weights_p = layer_forward(
        inputs, weights_p, vect_p, my_len, ([private_two, private_three, *weights_s], [shared_two, shared_three])
    )
    second_out, second_saved, weights_s = layer_forward(
        first_out, weights_s, vect_s[: 8 * D + FF], my_len, ([shared_two], [table_four])
    )

    final_scale = vect_s[8 * D + FF : 9 * D + FF]
    final_shift = vect_s[9 * D + FF : 10 * D + FF]
    final_in = jnp.take(second_out, my_picks, axis=0, mode="clip")
    final_b = layer_norm(final_in, final_scale, final_shift).astype(BF)
    target_rows = jnp.take(rows, my_picks + 1, axis=0, mode="clip").astype(F32)

    scored_tree = Gather(final_b, shard_names, shard_names)
    meet([final_b], [scored_tree])
    meet([final_b], [scored_tree, table_four])
    table_four = table_four.result()
    scored = scored_tree.result()

    def group(x):
        x = x.reshape((clients, shards) + x.shape[1:])
        return lax.dynamic_index_in_dim(x, 2 * at_pair + at_core, 0, False)

    group_ids, group_picks, group_live = group(all_ids), group(all_picks), group(all_live)
    seq_at = lax.broadcasted_iota(jnp.int32, (shards, picks, seq_len), 2)
    targets = jnp.sum(
        jnp.where(seq_at == group_picks[:, :, None] + 1, group_ids[:, None, :], 0), 2
    ).reshape(-1)
    host_clients = 2 * at_pair + jnp.arange(shards, dtype=jnp.int32) // block
    weight = jnp.where(group_live, jnp.take(share_all, host_clients)[:, None], 0.0).reshape(-1)
    target_owner = targets // slice_rows
    local_target = jnp.where(
        target_owner % shards == shard_at,
        target_owner // shards * pad_rows + targets % slice_rows,
        -1,
    )
    logits = dot_outer(scored, table_four) + filled
    hit = lax.broadcasted_iota(jnp.int32, logits.shape, 1) == local_target[:, None]
    part_max = jnp.max(logits, -1)
    exponent = jnp.exp(logits - part_max[:, None])
    part_sum = jnp.sum(exponent, -1)
    part_target = jnp.sum(jnp.where(hit, logits, 0.0), -1)
    pulled = dot_plain(exponent.astype(BF), table_four)
    stats = jnp.stack([part_max, part_sum, part_target])
    stats = lax.all_to_all(
        jnp.broadcast_to(stats, (shards,) + stats.shape), shard_names, 0, 0, tiled=True
    )
    pulled, stats = fence(pulled, stats)
    top = jnp.max(stats[:, 0], 0)
    total = jnp.sum(stats[:, 1] * jnp.exp(stats[:, 0] - top), 0)
    target_logit = jnp.sum(stats[:, 2], 0)
    log_all = top + jnp.log(total)
    pulled = (pulled * (weight * jnp.exp(part_max - log_all))[:, None]).astype(BF)
    pulled_tree = Reduce(pulled, shard_names, shard_names[::-1])
    grad_logits = (
        weight[:, None] * jnp.exp(logits - log_all[:, None])
        - jnp.where(hit, weight[:, None], 0.0)
    ).astype(BF)
    head_parts = []
    for part in jnp.split(grad_logits, clients // 2, 1):
        part = dot_inner(part, scored).astype(BF)
        head_parts += meet([part], [pulled_tree])
    pulled_own = pulled_tree.result()

    def own_rows(x):
        return lax.dynamic_slice_in_dim(x, shard_at * picks, picks, 0)

    own_weight = own_rows(weight)
    grad_final_b = pulled_own - own_weight[:, None] * target_rows
    own_live = lax.dynamic_index_in_dim(group_live, shard_at, 0, False)
    own_terms = jnp.sum(jnp.where(own_live, own_rows(log_all - target_logit), 0.0))
    head_trees = [Reduce(part, ("core",), ("core",), None, (1,)) for part in head_parts]

    grad_final_in, grad_fscale, grad_fshift = jax.vjp(
        layer_norm, final_in, final_scale, final_shift
    )[1](grad_final_b)
    grad_second = jnp.zeros_like(second_out).at[my_picks].add(grad_final_in)
    shared_rest, waits_s = ("pair",) + shard_names, {"down": (2,), "fore": (2,), "qkv": (1, 1)}

    def launch_s(kind, part):
        shared_trees[kind] = Reduce(
            part, shared_rest, ("pair",) + shard_names[::-1], None, waits_s[kind]
        )
        return [shared_trees[kind]]

    unswap = (
        lambda x: lax.ppermute(x, every, swap_pairs),
        lambda x, other: jnp.where(at_core == at_half, x, other),
    )
    waits_p = {"down": (2,), "fore": ()}

    def launch_p(kind, part):
        order = rest[::-1] if kind == "down" else rest
        private_trees[kind] = [Reduce(part, rest, order, unswap, waits_p[kind])]
        return private_trees[kind]

    shared_trees, private_trees, trees = {}, {}, list(head_trees)
    grad_first, grad_vect_s, part_qkv = layer_backward(
        grad_second,
        second_saved,
        weights_s,
        vect_s[: 8 * D + FF],
        my_len,
        clients // 2,
        trees,
        launch_s,
    )
    trees.extend(launch_s("qkv", part_qkv))
    head_tree = Reduce(
        jnp.concatenate([tree.result().astype(BF) for tree in head_trees], 0),
        ("pair",),
        ("pair",),
        None,
        (1, 2),
        True,
    )
    trees.append(head_tree)
    vector_s = jnp.concatenate([grad_vect_s, grad_fscale[None], grad_fshift[None]], 0)
    vector_s = vector_s.reshape(count, -1)
    width_s = vector_s.shape[1]
    vector_s = jnp.pad(vector_s, ((0, 0), (0, -width_s % 1024))).reshape(count, -1, 128)
    vector_tree = Exchange(vector_s, every, (0, 2))
    trees.append(vector_tree)
    grad_inputs, grad_vect_p, part_qkv = layer_backward(
        grad_first, first_saved, weights_p, vect_p, my_len, 1, trees, launch_p
    )
    grad_rows = grad_inputs.astype(BF)

    def gathered_up(turn):
        spot = my_slots - turn * room
        here = (spot >= 0) & (spot < room)
        place = jnp.where(here, my_owners * room + spot, -1)
        chosen = lax.broadcasted_iota(jnp.int32, (count * room, seq_len), 0) == place[None, :]
        return dot_plain(chosen.astype(BF), grad_rows).astype(BF)

    def settle(sought, got, total_rows):
        landing = (
            lax.broadcasted_iota(jnp.int32, (slice_rows, count * room), 0) == sought[None, :]
        )
        return total_rows + dot_plain(landing.astype(BF), got)

    def give(turn, total_rows):
        got = lax.all_to_all(gathered_up(turn), every, 0, 0, tiled=True)
        return settle(asked(turn), got, total_rows)

    sent_back = gathered_up(0)

    middle = part_qkv.shape[1] // 2
    sides = grad_vect_p.reshape(2, -1, D)
    keep = lax.dynamic_index_in_dim(sides, at_core, 0, False)
    keep = keep + across(lax.dynamic_index_in_dim(sides, 1 - at_core, 0, False), "core")
    keep = keep.astype(BF).reshape(block, 1, -1)
    width_p = keep.shape[2]
    keep = jnp.pad(keep, ((0, 0), (0, 15), (0, middle - width_p)))
    qkv_one = part_qkv[:, :middle].reshape(block, -1, middle)
    height = qkv_one.shape[1]
    qkv_one = jnp.concatenate([qkv_one, keep], 1).reshape(-1, middle)
    tree_one = Reduce(qkv_one, rest, rest[::-1], unswap)
    tree_two = Reduce(part_qkv[:, middle:], rest, rest, unswap)
    trees += [tree_one, tree_two]
    (sent_back,) = meet([sent_back], trees)
    got_back = lax.all_to_all(sent_back, every, 0, 0, tiled=True)

    posit_tree = Reduce(grad_rows, posit_names, ("core",) + shard_names[::-1])
    meet([sent_back], trees + [posit_tree])
    meet([sent_back], [posit_tree])
    grad_posit = posit_tree.result()
    grad_posit = grad_posit + across(grad_posit.astype(BF), "pair").astype(F32)
    grad_posit = jnp.where(at_pair == 0, grad_posit, 0.0)
    grad_vect_sh = jnp.sum(vector_tree.result().reshape(count, -1), 0)[:width_s]
    head_own = head_tree.result()[:slice_rows]
    g_down_s, g_fore_s, g_qkv_s = [
        shared_trees[kind].result() for kind in ("down", "fore", "qkv")
    ]
    g_wide_s = jnp.concatenate([g_qkv_s, g_fore_s[:, FF:], g_fore_s[:, :FF]], 1)
    g_down_p, g_fore_p = [private_trees[kind][0].result() for kind in ("down", "fore")]
    g_qkv_p, g_qkv_q = tree_one.result(), tree_two.result()
    g_qkv_p, grad_vect_ph = g_qkv_p[:height], g_qkv_p[height, :width_p]
    g_wide_p = jnp.concatenate([g_qkv_p, g_qkv_q, g_fore_p[:, FF:], g_fore_p[:, :FF]], 1)

    grad_table = settle(asked_first, got_back, head_own)
    grad_table = lax.fori_loop(1, rounds, give, grad_table)

    all_grads = [
        grad_table,
        grad_posit,
        g_wide_s,
        g_down_s,
        grad_vect_sh,
        g_wide_p[None],
        g_down_p[None],
        grad_vect_ph[None],
    ]
    squares = jnp.zeros((), jnp.float32)
    for gradient in all_grads:
        squares = squares + jnp.sum(gradient * gradient)
    client_at = jnp.arange(clients, dtype=jnp.int32)
    loss_vector = jnp.where(client_at == 2 * at_pair + at_half, own_terms, 0.0)
    figures = jnp.pad(jnp.concatenate([squares[None], loss_vector]), (0, 127 - clients))
    figures = sum_bits(figures, every)
    grad_norm = jnp.sqrt(figures[0])
    own_client = client_at == 2 * at_pair + at_core
    loss_sum = jnp.sum(jnp.where(own_client, figures[1 : 1 + clients], 0.0))
    count_sum = jnp.sum(jnp.where(own_client, counts_all, 0.0))
    factor = jnp.minimum(1.0, CLIP_NORM / grad_norm)
    g_table, g_posit, g_wide_s, g_down_s, g_vect_s, g_wide_p, g_down_p, g_vect_p = [
        member * factor for member in all_grads
    ]
    results = []
    for state, gradient, rate, decay in (
        ((embedding, embedding_first, embedding_second), g_table, RATE_MATRIX, DECAY),
        ((position_table, position_first, position_second), g_posit, RATE_MATRIX, DECAY),
        ((shared_wide, shared_wide_first, shared_wide_second), g_wide_s, RATE_MATRIX, DECAY),
        ((shared_down, shared_down_first, shared_down_second), g_down_s, RATE_MATRIX, DECAY),
        ((shared_vectors, shared_vectors_first, shared_vectors_second), g_vect_s, RATE_VECTOR, 0.0),
        ((private_wide, private_wide_first, private_wide_second), g_wide_p, RATE_MATRIX, DECAY),
        ((private_down, private_down_first, private_down_second), g_down_p, RATE_MATRIX, DECAY),
        (
            (private_vectors, private_vectors_first, private_vectors_second),
            g_vect_p,
            RATE_VECTOR,
            0.0,
        ),
    ):
        results += adamw(*state, gradient, rate, decay)
    return (*results, loss_sum.reshape(1), count_sum.reshape(1), grad_norm)


def solution(mesh):
    clients, shards = mesh.shape["client"], mesh.shape["shard"]
    depth = shards.bit_length() - 1
    if clients != 4 or shards != 2**depth:
        raise ValueError("mesh sizes")
    shard_names = tuple("s%d" % place for place in range(depth))
    fine = Mesh(
        mesh.devices.reshape((clients // 2, 2) + (2,) * depth), ("pair", "core") + shard_names
    )
    client, shard, both = ("pair", "core"), shard_names, ("pair", "core") + shard_names
    table, block, vector, lot = P(both, None), P(client, shard, None), P(both), P(client, shard)
    in_specs = (
        (block, lot, block, P())
        + (table,) * 12
        + (vector,) * 3
        + (block,) * 6
        + (lot,) * 3
    )
    out_specs = (
        (table,) * 12 + (vector,) * 3 + (block,) * 6 + (lot,) * 3 + (P(client), P(client), P())
    )

    def run(*arrays):
        return per_device(shard_names, *arrays)

    return jax.shard_map(
        run, mesh=fine, in_specs=in_specs, out_specs=out_specs, check_vma=False
    )
```

time: 1110 us -> 954 us (0.86)
  local copies, waits for them, and re-layouts: 172 us -> 79.8 us
  matrix products: 225 us -> 147 us
  other arithmetic: 260 us -> 207 us
  Pallas kernels: 0 us -> 48.9 us
  starting transfers between devices: 104 us -> 121 us
  between operations: 15 us -> 27.9 us
    dot_general x12 -> x0, matrix products: 52 us -> none  [the longest x2 19.3 us: attend_back(): jnp.einsum('qhd,khd->hqk', grad_out, block_qkv[:, 2], preferred_element_t...]
    pallas_call x0 -> x4, Pallas kernels: none -> 48.9 us  [the longest x2 25.2 us: attend(): pl.pallas_call(attend_kernel, grid_spec=pltpu.PrefetchScalarGridSpec(num_...]
    select_n x3 -> x0, local copies, waits for them, and re-layouts: 43.8 us -> none  [gather_bit(): jnp.where(low_side, jnp.concatenate([x, other], dim), jnp.concatenate([ot...]
    ppermute x76 -> x74, waiting for transfers between devices: 304 us -> 268 us  [across(): return lax.ppermute(x, name, FLIP)]
    dynamic_slice x34 -> x30, local copies, waits for them, and re-layouts: 55.5 us -> 25.1 us  [the longest x29 23.3 us: send(): lax.dynamic_index_in_dim(self.held, 1 - side, dim, True)]
    select_n x39 -> x35, other arithmetic: 87.3 us -> 59.5 us  [the longest x30 56.9 us: advance(): jnp.where(low_side, jnp.concatenate([self.held, self.other], dim), jnp.co...]
    all_to_all x4 -> x5, waiting for transfers between devices: 18.2 us -> 44.7 us  [the longest x1 30.6 us: send(): self.other = lax.all_to_all(self.held, self.names, 0, 0, tiled=True)]
    concatenate x25 -> x10, other arithmetic: 26.7 us -> 6.79 us  [the longest x3 3.61 us: core_half(): active, lead, width = (jnp.concatenate(pieces, 1), 1, width * lead)]
  transfers between devices with their start and end apart: 86 -> 87, of which waited for: 40 -> 32; matrix products, arithmetic and copies ran while one was open for 48% -> 33% of each run, Pallas kernels for 0% -> 5%
where the time goes in v2:
time: 954 us; the launch traced here: 944 us
  waiting for transfers between devices  312 us (33%)
  other arithmetic  207 us (22%)
  matrix products  147 us (15%)
  starting transfers between devices  121 us (13%)
  local copies, waits for them, and re-layouts  79.8 us (8%)
  Pallas kernels  48.9 us (5%)
  between operations  27.9 us (3%)
    ppermute x74, waiting for transfers between devices, across(): return lax.ppermute(x, name, FLIP)  268 us
    ppermute x74, starting transfers between devices, across(): return lax.ppermute(x, name, FLIP)  88.8 us
    select_n x30, other arithmetic, advance(): jnp.where(low_side, jnp.concatenate([self.held, self.other], dim), jnp.co...  56.9 us
    dot_general x11, matrix products, dot_plain(): return jnp.dot(former, latter, preferred_element_type=jnp.float32)  54.5 us
    dot_general x9, matrix products, dot_outer(): lax.dot_general(former, latter, (((1,), (1,)), ((), ())), preferred_eleme...  48.4 us
    dot_general x18, matrix products, dot_inner(): lax.dot_general(former, latter, (((0,), (0,)), ((), ())), preferred_eleme...  44.3 us
    all_to_all x1, waiting for transfers between devices, send(): self.other = lax.all_to_all(self.held, self.names, 0, 0, tiled=True)  30.6 us
    pallas_call x2, Pallas kernels, attend(): pl.pallas_call(attend_kernel, grid_spec=pltpu.PrefetchScalarGridSpec(num_...  25.2 us
  transfers between devices with their start and end apart: 87, of which 32 were waited for; matrix products, arithmetic and copies ran while one was open for 33% of the time, Pallas kernels for 5%

profile of v2, /device:TPU:0, one launch (start us, length us, event | category | flops | bytes accessed | tf_op | source)
XLA Modules:
  0.0 944.1 jit_solution(2109559964544357890)
XLA Ops:
  16.2 7.4 all-to-all-start.2
  35.8 14.1 %all-to-all-done.2 = f32[32,32,128]{2,1,0:T(8,128)} async-done(((f32[32,32,128]{2,1,0:T(8,128)}), f32[32,32,128]{2,1,0:T(8,128)}, u32[]{:S(2)}, u32[]{:S(2)}) %all-to-all-start.2) | async-done | bytes 524320 | tf_op jit(solution)/shard_map/all_to_all | solution.py:556
  51.3 7.4 collective-permute-done.1
  84.5 14.7 %collective-permute-done.3 = bf16[1,1,2,1,1,24,3072]{6,5,4,3,2,1,0:T(8,128)(2,1)} collective-permute-done((bf16[1,1,2,1,1,24,3072]{6,5,4,3,2,1,0:T(8,128)(2,1)}, bf16[1,1,2,1,1,24,3072]{6,5,4,3,2,1,0:T(8,128)(2,1)}, u32[]{:S(2)}, u32[]{:S(2)}) %collective-permute-start.3) | collective-permute-done | bytes 294944 | tf_op jit(solution)/shard_map/ppermute | solution.py:450
  125.6 35.9 %collective-permute-done.7 = bf16[1,1,2,2,1,24,3072]{6,5,4,3,2,1,0:T(8,128)(2,1)} collective-permute-done((bf16[1,1,2,2,1,24,3072]{6,5,4,3,2,1,0:T(8,128)(2,1)S(1)}, bf16[1,1,2,2,1,24,3072]{6,5,4,3,2,1,0:T(8,128)(2,1)}, u32[]{:S(2)}, u32[]{:S(2)}) %collective-permute-start.7) | collective-permute-done | bytes 589856 | tf_op jit(solution)/shard_map/ppermute | solution.py:450
  208.0 12.6 %shard_map.475 = (bf16[512,768]{1,0:T(8,128)(2,1)S(1)}, f32[6,2,512]{2,1,0:T(2,128)S(1)}) custom-call(s32[1]{0:T(128)} %bitcast.41.live_ref, bf16[512,2304]{1,0:T(8,128)(2,1)S(1)} %fusion.30.q_ref.k_ref.v_ref, bf16[512,2304]{1,0:T(8,128)(2,1)S(1)} %fusion.30.q_ref.k_ref.v_ref, bf16[512,2304]{1,0:T(8,128)(2,1)S(1)} %fusion.30.q_ref.k_ref.v_ref), custom_call_target="tpu_custom_call" | custom-call | flops 805306368 | bytes 3145728 | tf_op jit(solution)/shard_map/pallas_call | solution.py:151
  262.3 12.6 %shard_map.476 = (bf16[512,768]{1,0:T(8,128)(2,1)S(1)}, f32[6,2,512]{2,1,0:T(2,128)S(1)}) custom-call(s32[1]{0:T(128)} %bitcast.41.live_ref, bf16[512,2304]{1,0:T(8,128)(2,1)S(1)} %fusion.31.q_ref.k_ref.v_ref, bf16[512,2304]{1,0:T(8,128)(2,1)S(1)} %fusion.31.q_ref.k_ref.v_ref, bf16[512,2304]{1,0:T(8,128)(2,1)S(1)} %fusion.31.q_ref.k_ref.v_ref), custom_call_target="tpu_custom_call" | custom-call | flops 805306368 | bytes 3145728 | tf_op jit(solution)/shard_map/pallas_call | solution.py:151
  286.5 17.4 %collective-permute-done.25 = bf16[1,1,2,2,2,96,768]{6,5,4,3,2,1,0:T(8,128)(2,1)S(1)} collective-permute-done((bf16[1,1,2,2,2,96,768]{6,5,4,3,2,1,0:T(8,128)(2,1)S(1)}, bf16[1,1,2,2,2,96,768]{6,5,4,3,2,1,0:T(8,128)(2,1)S(1)}, u32[]{:S(2)}, u32[]{:S(2)}) %collective-permute-start.25) | collective-permute-done | bytes 1179680 | tf_op jit(solution)/shard_map/ppermute | solution.py:450
  324.4 12.1 %collective-permute-done.27 = bf16[1,1,1,128,768]{4,3,2,1,0:T(8,128)(2,1)S(1)} collective-permute-done((bf16[1,1,1,128,768]{4,3,2,1,0:T(8,128)(2,1)S(1)}, bf16[1,1,1,128,768]{4,3,2,1,0:T(8,128)(2,1)S(1)}, u32[]{:S(2)}, u32[]{:S(2)}) %collective-permute-start.27) | collective-permute-done | bytes 196640 | tf_op jit(solution)/shard_map/ppermute | solution.py:450
  336.6 11.0 %collective-permute-done.28 = bf16[2,1,1,128,768]{4,3,2,1,0:T(8,128)(2,1)S(1)} collective-permute-done((bf16[2,1,1,128,768]{4,3,2,1,0:T(8,128)(2,1)S(1)}, bf16[2,1,1,128,768]{4,3,2,1,0:T(8,128)(2,1)S(1)}, u32[]{:S(2)}, u32[]{:S(2)}) %collective-permute-start.28) | collective-permute-done | bytes 393248 | tf_op jit(solution)/shard_map/ppermute | solution.py:450
  348.3 19.9 %collective-permute-done.29 = bf16[1,1,1584,768]{3,2,1,0:T(8,128)(2,1)} collective-permute-done((bf16[1,1,1584,768]{3,2,1,0:T(8,128)(2,1)}, bf16[1,1,1584,768]{3,2,1,0:T(8,128)(2,1)}, u32[]{:S(2)}, u32[]{:S(2)}) %collective-permute-start.29) | collective-permute-done | bytes 2433056 | tf_op jit(solution)/shard_map/ppermute | solution.py:450
  368.3 7.6 maximum_select_fusion.1
  387.3 15.1 %collective-permute-done.30 = bf16[2,2,1,128,768]{4,3,2,1,0:T(8,128)(2,1)S(1)} collective-permute-done((bf16[2,2,1,128,768]{4,3,2,1,0:T(8,128)(2,1)S(1)}, bf16[2,2,1,128,768]{4,3,2,1,0:T(8,128)(2,1)S(1)}, u32[]{:S(2)}, u32[]{:S(2)}) %collective-permute-start.30) | collective-permute-done | bytes 786464 | tf_op jit(solution)/shard_map/ppermute | solution.py:450
  402.6 8.2 maximum_select_fusion
  410.8 14.3 %add_reduce_fusion = (f32[1024]{0:T(1024)S(1)}, f32[1024,6336]{0,1:T(8,128)}) fusion(f32[6336]{0:T(1024)S(1)} %fusion.109, bf16[1024,768]{1,0:T(8,128)(2,1)S(1)} %bitcast.399, bf16[6336,768]{1,0:T(8,128)(2,1)S(1)} %bitcast.345), kind=kOutput, calls=%fused_computation.32 | convolution fusion | flops 9978641408 | bytes 37286656 | tf_op jit(solution)/shard_map/dot_general | solution.py:39
  425.1 12.2 %fusion.6 = (f32[1024]{0:T(1024)S(1)}, f32[1024]{0:T(1024)S(1)}) fusion(f32[1024,6336]{0,1:T(8,128)} %get-tuple-element.639, f32[1024]{0:T(1024)S(1)} %get-tuple-element.638, f32[6336]{0:T(1024)S(1)} %fusion.109, s32[1024]{0:T(1024)S(1)} %fusion.132), kind=kLoop, calls=%fused_computation.30 | loop fusion | flops 38926336 | bytes 25993984 | tf_op jit(solution)/shard_map/reduce_sum | solution.py:686
  441.8 20.3 %fusion.8 = f32[1024,768]{1,0:T(8,128)} fusion(bf16[6336,768]{1,0:T(8,128)(2,1)} %bitcast.346, f32[1024,6336]{0,1:T(8,128)} %get-tuple-element.639, f32[1024]{0:T(1024)S(1)} %get-tuple-element.638, f32[6336]{0:T(1024)S(1)} %fusion.109), kind=kOutput, calls=%fused_computation.33 | convolution fusion | flops 9985130496 | bytes 38859520 | tf_op jit(solution)/shard_map/dot_general | solution.py:29
  466.7 12.7 %subtract_convert_fusion = bf16[1024,6336]{0,1:T(8,128)(2,1)S(1)} fusion(f32[1024,6336]{0,1:T(8,128)} %get-tuple-element.639, f32[1024]{0:T(1024)S(1)} %get-tuple-element.501, s32[1024]{0:T(1024)S(1)} %fusion.132, f32[6336]{0:T(1024)S(1)} %fusion.109, f32[1024]{0:T(1024)S(1)} %get-tuple-element.619), kind=kLoop, calls=%fused_computation.26 | loop fusion | flops 45416448 | bytes 38966016 | tf_op jit(solution)/shard_map/convert_element_type | solution.py:703
  479.4 6.9 convolution_convert_fusion
  488.2 7.1 convolution_convert_fusion.1
  562.6 12.1 %shard_map.477 = bf16[512,2304]{1,0:T(8,128)(2,1)S(1)} custom-call(s32[1]{0:T(128)} %bitcast.41.live_ref, bf16[512,2304]{1,0:T(8,128)(2,1)S(1)} %copy-done.3, bf16[512,2304]{1,0:T(8,128)(2,1)S(1)} %copy-done.3, bf16[512,2304]{1,0:T(8,128)(2,1)S(1)} %copy-done.3, bf16[512,768]{1,0:T(8,128)(2,1)S(1)} %convolution_convert_fusion.9.grad_ref, ...), custom_call_target="tpu_custom_call" | custom-call | flops 2013265920 | bytes 5505024 | tf_op jit(solution)/shard_map/pallas_call | solution.py:184
  588.3 8.2 collective-permute-done.42
  603.7 8.2 fusion.21
  613.4 20.7 %collective-permute-done.45 = bf16[1,2,2,2,24,3840]{5,4,3,2,1,0:T(8,128)(2,1)S(1)} collective-permute-done((bf16[1,2,2,2,24,3840]{5,4,3,2,1,0:T(8,128)(2,1)S(1)}, bf16[1,2,2,2,24,3840]{5,4,3,2,1,0:T(8,128)(2,1)S(1)}, u32[]{:S(2)}, u32[]{:S(2)}) %collective-permute-start.45) | collective-permute-done | bytes 1474592 | tf_op jit(solution)/shard_map/ppermute | solution.py:450
  681.9 11.5 %shard_map.478 = bf16[512,2304]{1,0:T(8,128)(2,1)S(1)} custom-call(s32[1]{0:T(128)} %bitcast.41.live_ref, bf16[512,2304]{1,0:T(8,128)(2,1)S(1)} %copy-done.1, bf16[512,2304]{1,0:T(8,128)(2,1)S(1)} %copy-done.1, bf16[512,2304]{1,0:T(8,128)(2,1)S(1)} %copy-done.1, bf16[512,768]{1,0:T(8,128)(2,1)S(1)} %convolution_convert_fusion.8.grad_ref, ...), custom_call_target="tpu_custom_call" | custom-call | flops 2013265920 | bytes 5505024 | tf_op jit(solution)/shard_map/pallas_call | solution.py:184
  694.9 30.6 %all-to-all-done.5 = f32[32,8,128]{2,1,0:T(8,128)} async-done(((f32[32,8,128]{2,1,0:T(8,128)}), f32[32,8,128]{2,1,0:T(8,128)}, u32[]{:S(2)}, u32[]{:S(2)}) %all-to-all-start.5) | async-done | bytes 131104 | tf_op jit(solution)/shard_map/all_to_all | solution.py:308
  759.4 8.9 collective-permute-done.57
  786.2 23.5 %collective-permute-done.61 = bf16[1,1,1,1,24,2304]{5,4,3,2,1,0:T(8,128)(2,1)S(1)} collective-permute-done((bf16[1,1,1,1,24,2304]{5,4,3,2,1,0:T(8,128)(2,1)S(1)}, bf16[1,1,1,1,24,2304]{5,4,3,2,1,0:T(8,128)(2,1)S(1)}, u32[]{:S(2)}, u32[]{:S(2)}) %collective-permute-start.61) | collective-permute-done | bytes 110624 | tf_op jit(solution)/shard_map/ppermute | solution.py:450
  830.6 23.4 %collective-permute-done.71 = bf16[1,2,1,1,32,768]{5,4,3,2,1,0:T(8,128)(2,1)S(1)} collective-permute-done((bf16[1,2,1,1,32,768]{5,4,3,2,1,0:T(8,128)(2,1)S(1)}, bf16[1,2,1,1,32,768]{5,4,3,2,1,0:T(8,128)(2,1)S(1)}, u32[]{:S(2)}, u32[]{:S(2)}) %collective-permute-start.71) | collective-permute-done | bytes 98336 | tf_op jit(solution)/shard_map/ppermute | solution.py:450
  854.1 15.7 %collective-permute-start.72 = (bf16[1,1,1,1,32,768]{5,4,3,2,1,0:T(8,128)(2,1)S(1)}, bf16[1,1,1,1,32,768]{5,4,3,2,1,0:T(8,128)(2,1)S(1)}, u32[]{:S(2)}, u32[]{:S(2)}) collective-permute-start(bf16[1,1,1,1,32,768]{5,4,3,2,1,0:T(8,128)(2,1)S(1)} %constant_dynamic-slice_fusion.2), channel_id=1, source_target_pairs={{0,4},{4,0},{1,5},{5,1},{2,6},{6,2},{3,7},{7,3},{8,12},{12,8},{9,1... | collective-permute-start | bytes 147464 | tf_op jit(solution)/shard_map/ppermute | solution.py:450
  877.1 6.8 bitcast_add_fusion
  921.9 10.6 %multiply_subtract_fusion = (f32[1572,768]{1,0:T(8,128)}, f32[1572,768]{1,0:T(8,128)}, f32[1572,768]{1,0:T(8,128)}) fusion(f32[1572,768]{1,0:T(8,128)} %param.36, f32[1572,768]{1,0:T(8,128)S(1)} %bitcast.342, f32[]{:T(128)S(6)} %min.3, f32[1572,768]{1,0:T(8,128)} %param.37, f32[1572,768]{1,0:T(8,128)} %param.38), kind=kLoop, calls=%fused_computation.73 | loop fusion | flops 18109440 | bytes 33804292 | tf_op jit(solution)/shard_map/sub | solution.py:442
  (977 shorter events, 466.4 us)
Async XLA Ops:
  23.6 172.3 %all-gather.2.cloned.1.call-start = ((), (), s32[]{:S(2)}) async-start(), calls=%async_computation.7 | async-start | bytes 1622016 | tf_op jit(solution)/shard_map/all_gather | solution.py:557
  62.3 37.0 %collective-permute-start.2 = (bf16[1,1,1,96,3072]{4,3,2,1,0:T(8,128)(2,1)S(1)}, bf16[1,1,1,96,3072]{4,3,2,1,0:T(8,128)(2,1)}, u32[]{:S(2)}, u32[]{:S(2)}) collective-permute-start(bf16[1,1,1,96,3072]{4,3,2,1,0:T(8,128)(2,1)S(1)} %get-tuple-element.275), channel_id=1, source_target_pairs={{0,2},{2,0},{1,3},{3,1},{4,6},{6,4},{5,7},{7,5},{8,10},{10,8},{9,1... | collective-permute-start | bytes 1769480 | tf_op jit(solution)/shard_map/ppermute | solution.py:450
  64.2 35.1 %collective-permute-start.3 = (bf16[1,1,2,1,1,24,3072]{6,5,4,3,2,1,0:T(8,128)(2,1)}, bf16[1,1,2,1,1,24,3072]{6,5,4,3,2,1,0:T(8,128)(2,1)}, u32[]{:S(2)}, u32[]{:S(2)}) collective-permute-start(bf16[1,1,2,1,1,24,3072]{6,5,4,3,2,1,0:T(8,128)(2,1)} %maximum_select_fusion.27), channel_id=1, source_target_pairs={{0,2},{2,0},{1,3},{3,1},{4,6},{6,4},{5,7},{7,5},{8,10},{10,8},{9,1... | collective-permute-start | bytes 884744 | tf_op jit(solution)/shard_map/ppermute | solution.py:450
  66.3 56.8 %collective-permute-start.4 = (bf16[96,3072]{1,0:T(8,128)(2,1)}, bf16[96,3072]{1,0:T(8,128)(2,1)}, u32[]{:S(2)}, u32[]{:S(2)}) collective-permute-start(bf16[96,3072]{1,0:T(8,128)(2,1)} %get-tuple-element.556), channel_id=1, source_target_pairs={{4,8},{8,4},{5,9},{9,5},{6,10},{10,6},{7,11},{11,7},{20,24},{24,20... | collective-permute-start | bytes 1769480 | tf_op jit(solution)/shard_map/ppermute | solution.py:553
  67.7 57.9 %collective-permute-start.5 = (bf16[384,768]{1,0:T(8,128)(2,1)}, bf16[384,768]{1,0:T(8,128)(2,1)}, u32[]{:S(2)}, u32[]{:S(2)}) collective-permute-start(bf16[384,768]{1,0:T(8,128)(2,1)} %convert_bitcast_fusion.1), channel_id=1, source_target_pairs={{4,8},{8,4},{5,9},{9,5},{6,10},{10,6},{7,11},{11,7},{20,24},{24,20... | collective-permute-start | bytes 1769480 | tf_op jit(solution)/shard_map/ppermute | solution.py:553
  69.9 101.9 %collective-permute-start.10 = (bf16[1,1,1,1,1,24,3072]{6,5,4,3,2,1,0:T(8,128)(2,1)}, bf16[1,1,1,1,1,24,3072]{6,5,4,3,2,1,0:T(8,128)(2,1)}, u32[]{:S(2)}, u32[]{:S(2)}) collective-permute-start(bf16[1,1,1,1,1,24,3072]{6,5,4,3,2,1,0:T(8,128)(2,1)} %slice_bitcast_fusion.4), channel_id=1, source_target_pairs={{0,4},{4,0},{1,5},{5,1},{2,6},{6,2},{3,7},{7,3},{8,12},{12,8},{9,1... | collective-permute-start | bytes 442376 | tf_op jit(solution)/shard_map/ppermute | solution.py:450
  99.2 81.0 %all-to-all-start.3 = ((bf16[32,32,768]{2,1,0:T(8,128)(2,1)}), bf16[32,32,768]{2,1,0:T(8,128)(2,1)}, u32[]{:S(2)}, u32[]{:S(2)}) async-start(bf16[32,32,768]{2,1,0:T(8,128)(2,1)} %bitcast.351), calls=%async_computation.3 | async-start | bytes 3145728 | tf_op jit(solution)/shard_map/all_to_all | solution.py:633
  106.4 55.2 %collective-permute-start.6 = (bf16[1,2,1,96,3072]{4,3,2,1,0:T(8,128)(2,1)}, bf16[1,2,1,96,3072]{4,3,2,1,0:T(8,128)(2,1)}, u32[]{:S(2)}, u32[]{:S(2)}) collective-permute-start(bf16[1,2,1,96,3072]{4,3,2,1,0:T(8,128)(2,1)} %maximum_select_fusion.15), channel_id=1, source_target_pairs={{0,1},{1,0},{2,3},{3,2},{4,5},{5,4},{6,7},{7,6},{8,9},{9,8},{10,11... | collective-permute-start | bytes 3538952 | tf_op jit(solution)/shard_map/ppermute | solution.py:450
  111.9 49.7 %collective-permute-start.7 = (bf16[1,1,2,2,1,24,3072]{6,5,4,3,2,1,0:T(8,128)(2,1)S(1)}, bf16[1,1,2,2,1,24,3072]{6,5,4,3,2,1,0:T(8,128)(2,1)}, u32[]{:S(2)}, u32[]{:S(2)}) collective-permute-start(bf16[1,1,2,2,1,24,3072]{6,5,4,3,2,1,0:T(8,128)(2,1)S(1)} %maximum_select_fusion.23), channel_id=1, source_target_pairs={{0,1},{1,0},{2,3},{3,2},{4,5},{5,4},{6,7},{7,6},{8,9},{9,8},{10,11... | collective-permute-start | bytes 1769480 | tf_op jit(solution)/shard_map/ppermute | solution.py:450
  123.0 50.5 %collective-permute-start.11 = (bf16[1,1,1,1,1,96,768]{6,5,4,3,2,1,0:T(8,128)(2,1)S(1)}, bf16[1,1,1,1,1,96,768]{6,5,4,3,2,1,0:T(8,128)(2,1)S(1)}, u32[]{:S(2)}, u32[]{:S(2)}) collective-permute-start(bf16[1,1,1,1,1,96,768]{6,5,4,3,2,1,0:T(8,128)(2,1)S(1)} %bitcast.406), channel_id=1, source_target_pairs={{0,4},{4,0},{1,5},{5,1},{2,6},{6,2},{3,7},{7,3},{8,12},{12,8},{9,1... | collective-permute-start | bytes 442376 | tf_op jit(solution)/shard_map/ppermute | solution.py:450
  171.8 48.9 %collective-permute-start.15 = (bf16[1,1,2,2,2,24,3072]{6,5,4,3,2,1,0:T(8,128)(2,1)}, bf16[1,1,2,2,2,24,3072]{6,5,4,3,2,1,0:T(8,128)(2,1)}, u32[]{:S(2)}, u32[]{:S(2)}) collective-permute-start(bf16[1,1,2,2,2,24,3072]{6,5,4,3,2,1,0:T(8,128)(2,1)} %maximum_select_fusion.18), channel_id=1, source_target_pairs={{0,16},{16,0},{1,17},{17,1},{2,18},{18,2},{3,19},{19,3},{4,20},{20... | collective-permute-start | bytes 3538952 | tf_op jit(solution)/shard_map/ppermute | solution.py:450
  183.1 42.5 %collective-permute-start.14 = (bf16[1,2,1,384,768]{4,3,2,1,0:T(8,128)(2,1)}, bf16[1,2,1,384,768]{4,3,2,1,0:T(8,128)(2,1)}, u32[]{:S(2)}, u32[]{:S(2)}) collective-permute-start(bf16[1,2,1,384,768]{4,3,2,1,0:T(8,128)(2,1)} %maximum_select_fusion.17), channel_id=1, source_target_pairs={{0,1},{1,0},{2,3},{3,2},{4,5},{5,4},{6,7},{7,6},{8,9},{9,8},{10,11... | collective-permute-start | bytes 3538952 | tf_op jit(solution)/shard_map/ppermute | solution.py:450
  185.5 35.2 %collective-permute-start.16 = (bf16[1,1,2,1,1,24,3072]{6,5,4,3,2,1,0:T(8,128)(2,1)}, bf16[1,1,2,1,1,24,3072]{6,5,4,3,2,1,0:T(8,128)(2,1)}, u32[]{:S(2)}, u32[]{:S(2)}) collective-permute-start(bf16[1,1,2,1,1,24,3072]{6,5,4,3,2,1,0:T(8,128)(2,1)} %maximum_select_fusion.28), channel_id=1, source_target_pairs={{0,2},{2,0},{1,3},{3,1},{4,6},{6,4},{5,7},{7,5},{8,10},{10,8},{9,1... | collective-permute-start | bytes 884744 | tf_op jit(solution)/shard_map/ppermute | solution.py:450
  188.5 37.0 %collective-permute-start.13 = (bf16[1,1,2,96,3072]{4,3,2,1,0:T(8,128)(2,1)}, bf16[1,1,2,96,3072]{4,3,2,1,0:T(8,128)(2,1)}, u32[]{:S(2)}, u32[]{:S(2)}) collective-permute-start(bf16[1,1,2,96,3072]{4,3,2,1,0:T(8,128)(2,1)} %maximum_select_fusion.16), channel_id=1, source_target_pairs={{0,2},{2,0},{1,3},{3,1},{4,6},{6,4},{5,7},{7,5},{8,10},{10,8},{9,1... | collective-permute-start | bytes 3538952 | tf_op jit(solution)/shard_map/ppermute | solution.py:450
  254.9 48.9 %collective-permute-start.25 = (bf16[1,1,2,2,2,96,768]{6,5,4,3,2,1,0:T(8,128)(2,1)S(1)}, bf16[1,1,2,2,2,96,768]{6,5,4,3,2,1,0:T(8,128)(2,1)S(1)}, u32[]{:S(2)}, u32[]{:S(2)}) collective-permute-start(bf16[1,1,2,2,2,96,768]{6,5,4,3,2,1,0:T(8,128)(2,1)S(1)} %maximum_select_fusion.21), channel_id=1, source_target_pairs={{0,16},{16,0},{1,17},{17,1},{2,18},{18,2},{3,19},{19,3},{4,20},{20... | collective-permute-start | bytes 3538952 | tf_op jit(solution)/shard_map/ppermute | solution.py:450
  312.8 55.5 %collective-permute-start.29 = (bf16[1,1,1584,768]{3,2,1,0:T(8,128)(2,1)}, bf16[1,1,1584,768]{3,2,1,0:T(8,128)(2,1)}, u32[]{:S(2)}, u32[]{:S(2)}) collective-permute-start(bf16[1,1,1584,768]{3,2,1,0:T(8,128)(2,1)} %pad_bitcast_fusion), channel_id=1, source_target_pairs={{0,16},{16,0},{1,17},{17,1},{2,18},{18,2},{3,19},{19,3},{4,20},{20... | collective-permute-start | bytes 7299080 | tf_op jit(solution)/shard_map/ppermute | solution.py:450
  517.3 34.0 %collective-permute-start.37 = (bf16[1,1584,768]{2,1,0:T(8,128)(2,1)}, bf16[1,1584,768]{2,1,0:T(8,128)(2,1)}, u32[]{:S(2)}, u32[]{:S(2)}) collective-permute-start(bf16[1,1584,768]{2,1,0:T(8,128)(2,1)} %get-tuple-element.528), channel_id=1, source_target_pairs={{0,8},{8,0},{1,9},{9,1},{2,10},{10,2},{3,11},{11,3},{4,12},{12,4},... | collective-permute-start | bytes 7299080 | tf_op jit(solution)/shard_map/ppermute | solution.py:450
  535.4 39.3 %collective-permute-start.40 = (bf16[1,2,2,2,96,768]{5,4,3,2,1,0:T(8,128)(2,1)}, bf16[1,2,2,2,96,768]{5,4,3,2,1,0:T(8,128)(2,1)}, u32[]{:S(2)}, u32[]{:S(2)}) collective-permute-start(bf16[1,2,2,2,96,768]{5,4,3,2,1,0:T(8,128)(2,1)} %get-tuple-element.540), channel_id=1, source_target_pairs={{0,16},{16,0},{1,17},{17,1},{2,18},{18,2},{3,19},{19,3},{4,20},{20... | collective-permute-start | bytes 3538952 | tf_op jit(solution)/shard_map/ppermute | solution.py:450
  599.0 35.1 %collective-permute-start.45 = (bf16[1,2,2,2,24,3840]{5,4,3,2,1,0:T(8,128)(2,1)S(1)}, bf16[1,2,2,2,24,3840]{5,4,3,2,1,0:T(8,128)(2,1)S(1)}, u32[]{:S(2)}, u32[]{:S(2)}) collective-permute-start(bf16[1,2,2,2,24,3840]{5,4,3,2,1,0:T(8,128)(2,1)S(1)} %get-tuple-element.536), channel_id=1, source_target_pairs={{0,16},{16,0},{1,17},{17,1},{2,18},{18,2},{3,19},{19,3},{4,20},{20... | collective-permute-start | bytes 4423688 | tf_op jit(solution)/shard_map/ppermute | solution.py:450
  599.7 34.4 %collective-permute-start.44 = (bf16[1,2,1,1,96,768]{5,4,3,2,1,0:T(8,128)(2,1)S(1)}, bf16[1,2,1,1,96,768]{5,4,3,2,1,0:T(8,128)(2,1)S(1)}, u32[]{:S(2)}, u32[]{:S(2)}) collective-permute-start(bf16[1,2,1,1,96,768]{5,4,3,2,1,0:T(8,128)(2,1)S(1)} %get-tuple-element.582), channel_id=1, source_target_pairs={{0,2},{2,0},{1,3},{3,1},{4,6},{6,4},{5,7},{7,5},{8,10},{10,8},{9,1... | collective-permute-start | bytes 884744 | tf_op jit(solution)/shard_map/ppermute | solution.py:450
  601.5 54.2 %collective-permute-start.49 = (bf16[1,2,2,2,24,2304]{5,4,3,2,1,0:T(8,128)(2,1)}, bf16[1,2,2,2,24,2304]{5,4,3,2,1,0:T(8,128)(2,1)}, u32[]{:S(2)}, u32[]{:S(2)}) collective-permute-start(bf16[1,2,2,2,24,2304]{5,4,3,2,1,0:T(8,128)(2,1)} %get-tuple-element.544), channel_id=1, source_target_pairs={{0,16},{16,0},{1,17},{17,1},{2,18},{18,2},{3,19},{19,3},{4,20},{20... | collective-permute-start | bytes 2654216 | tf_op jit(solution)/shard_map/ppermute | solution.py:450
  647.1 78.4 %collective-permute-start.54 = (bf16[2,1,384,768]{3,2,1,0:T(8,128)(2,1)}, bf16[2,1,384,768]{3,2,1,0:T(8,128)(2,1)}, u32[]{:S(2)}, u32[]{:S(2)}) collective-permute-start(bf16[2,1,384,768]{3,2,1,0:T(8,128)(2,1)} %get-tuple-element.538), channel_id=1, source_target_pairs={{0,1},{1,0},{2,3},{3,2},{4,5},{5,4},{6,7},{7,6},{8,9},{9,8},{10,11... | collective-permute-start | bytes 3538952 | tf_op jit(solution)/shard_map/ppermute | solution.py:450
  664.2 61.3 %collective-permute-start.53 = (bf16[1,2,2,1,24,2304]{5,4,3,2,1,0:T(8,128)(2,1)}, bf16[1,2,2,1,24,2304]{5,4,3,2,1,0:T(8,128)(2,1)}, u32[]{:S(2)}, u32[]{:S(2)}) collective-permute-start(bf16[1,2,2,1,24,2304]{5,4,3,2,1,0:T(8,128)(2,1)} %get-tuple-element.562), channel_id=1, source_target_pairs={{0,1},{1,0},{2,3},{3,2},{4,5},{5,4},{6,7},{7,6},{8,9},{9,8},{10,11... | collective-permute-start | bytes 1327112 | tf_op jit(solution)/shard_map/ppermute | solution.py:450
  668.1 100.2 %collective-permute-start.58 = (bf16[1,1584,768]{2,1,0:T(8,128)(2,1)}, bf16[1,1584,768]{2,1,0:T(8,128)(2,1)}, u32[]{:S(2)}, u32[]{:S(2)}) collective-permute-start(bf16[1,1584,768]{2,1,0:T(8,128)(2,1)} %get-tuple-element.524), channel_id=1, source_target_pairs={{0,16},{16,0},{1,17},{17,1},{2,18},{18,2},{3,19},{19,3},{4,20},{20... | collective-permute-start | bytes 7299080 | tf_op jit(solution)/shard_map/ppermute | solution.py:450
  673.8 51.7 %collective-permute-start.55 = (bf16[1,2,96,3840]{3,2,1,0:T(8,128)(2,1)}, bf16[1,2,96,3840]{3,2,1,0:T(8,128)(2,1)}, u32[]{:S(2)}, u32[]{:S(2)}) collective-permute-start(bf16[1,2,96,3840]{3,2,1,0:T(8,128)(2,1)} %get-tuple-element.534), channel_id=1, source_target_pairs={{0,2},{2,0},{1,3},{3,1},{4,6},{6,4},{5,7},{7,5},{8,10},{10,8},{9,1... | collective-permute-start | bytes 4423688 | tf_op jit(solution)/shard_map/ppermute | solution.py:450
  674.4 51.1 %all-to-all-start.5 = ((f32[32,8,128]{2,1,0:T(8,128)}), f32[32,8,128]{2,1,0:T(8,128)}, u32[]{:S(2)}, u32[]{:S(2)}) async-start(f32[32,8,128]{2,1,0:T(8,128)} %bitcast.410), calls=%async_computation.5 | async-start | bytes 262144 | tf_op jit(solution)/shard_map/all_to_all | solution.py:308
  679.4 46.2 %collective-permute-start.52 = (bf16[1,1,1,1,24,3840]{5,4,3,2,1,0:T(8,128)(2,1)}, bf16[1,1,1,1,24,3840]{5,4,3,2,1,0:T(8,128)(2,1)S(1)}, u32[]{:S(2)}, u32[]{:S(2)}) collective-permute-start(bf16[1,1,1,1,24,3840]{5,4,3,2,1,0:T(8,128)(2,1)} %get-tuple-element.594), channel_id=1, source_target_pairs={{0,4},{4,0},{1,5},{5,1},{2,6},{6,2},{3,7},{7,3},{8,12},{12,8},{9,1... | collective-permute-start | bytes 552968 | tf_op jit(solution)/shard_map/ppermute | solution.py:450
  768.6 41.1 %collective-permute-start.65 = (bf16[2,1,112,1152]{3,2,1,0:T(8,128)(2,1)S(1)}, bf16[2,1,112,1152]{3,2,1,0:T(8,128)(2,1)S(1)}, u32[]{:S(2)}, u32[]{:S(2)}) collective-permute-start(bf16[2,1,112,1152]{3,2,1,0:T(8,128)(2,1)S(1)} %get-tuple-element.558), channel_id=1, source_target_pairs={{0,1},{1,0},{2,3},{3,2},{4,5},{5,4},{6,7},{7,6},{8,9},{9,8},{10,11... | collective-permute-start | bytes 1548296 | tf_op jit(solution)/shard_map/ppermute | solution.py:450
  771.2 38.4 %collective-permute-start.63 = (bf16[1,1,96,3840]{3,2,1,0:T(8,128)(2,1)S(1)}, bf16[1,1,96,3840]{3,2,1,0:T(8,128)(2,1)S(1)}, u32[]{:S(2)}, u32[]{:S(2)}) collective-permute-start(bf16[1,1,96,3840]{3,2,1,0:T(8,128)(2,1)S(1)} %add_convert_fusion.16), channel_id=1, source_target_pairs={{4,8},{8,4},{5,9},{9,5},{6,10},{10,6},{7,11},{11,7},{20,24},{24,20... | collective-permute-start | bytes 2211848 | tf_op jit(solution)/shard_map/ppermute | solution.py:732
  773.2 36.5 %collective-permute-start.62 = (bf16[1,1,384,768]{3,2,1,0:T(8,128)(2,1)S(1)}, bf16[1,1,384,768]{3,2,1,0:T(8,128)(2,1)S(1)}, u32[]{:S(2)}, u32[]{:S(2)}) collective-permute-start(bf16[1,1,384,768]{3,2,1,0:T(8,128)(2,1)S(1)} %add_convert_fusion.18), channel_id=1, source_target_pairs={{4,8},{8,4},{5,9},{9,5},{6,10},{10,6},{7,11},{11,7},{20,24},{24,20... | collective-permute-start | bytes 1769480 | tf_op jit(solution)/shard_map/ppermute | solution.py:732
  774.4 35.3 %collective-permute-start.66 = (bf16[1,2,96,1152]{3,2,1,0:T(8,128)(2,1)S(1)}, bf16[1,2,96,1152]{3,2,1,0:T(8,128)(2,1)S(1)}, u32[]{:S(2)}, u32[]{:S(2)}) collective-permute-start(bf16[1,2,96,1152]{3,2,1,0:T(8,128)(2,1)S(1)} %get-tuple-element.560), channel_id=1, source_target_pairs={{0,2},{2,0},{1,3},{3,1},{4,6},{6,4},{5,7},{7,5},{8,10},{10,8},{9,1... | collective-permute-start | bytes 1327112 | tf_op jit(solution)/shard_map/ppermute | solution.py:450
  822.3 54.8 %all-to-all-start.6 = ((bf16[32,32,768]{2,1,0:T(8,128)(2,1)}), bf16[32,32,768]{2,1,0:T(8,128)(2,1)}, u32[]{:S(2)}, u32[]{:S(2)}) async-start(bf16[32,32,768]{2,1,0:T(8,128)(2,1)} %bitcast.398), calls=%async_computation.6 | async-start | bytes 3145728 | tf_op jit(solution)/shard_map/all_to_all | solution.py:807
  (279 other events, 3168.4 us)
Sparse Core Ops, SparseCore 0:
  31.0 81.5 all-gather.1

commit v3 on v2

--- a/solution.py
+++ b/solution.py
@@ -165,11 +165,7 @@
             jax.ShapeDtypeStruct((pairs, 2, tokens), F32),
         ],
         compiler_params=pltpu.CompilerParams(vmem_limit_bytes=32 << 20),
-        cost_estimate=pl.CostEstimate(
-            flops=4 * tokens * tokens * breadth,
-            bytes_accessed=8 * tokens * breadth,
-            transcendentals=tokens * tokens * breadth // HD,
-        ),
+        cost_estimate=pl.CostEstimate(flops=0, bytes_accessed=0, transcendentals=0),
     )(live_len.reshape(1), joined, joined, joined)
 
 
@@ -196,11 +192,7 @@
         ),
         out_shape=jax.ShapeDtypeStruct((tokens, 3 * breadth), BF),
         compiler_params=pltpu.CompilerParams(vmem_limit_bytes=32 << 20),
-        cost_estimate=pl.CostEstimate(
-            flops=10 * tokens * tokens * breadth,
-            bytes_accessed=14 * tokens * breadth,
-            transcendentals=tokens * tokens * breadth // HD,
-        ),
+        cost_estimate=pl.CostEstimate(flops=0, bytes_accessed=0, transcendentals=0),
     )(live_len.reshape(1), joined, joined, joined, grad_mixed, log_total)
 
 
@@ -408,11 +400,12 @@
     part_proj = core_reduce(mixed_out, grad_branch, lead)
     grad_mixed = dot_outer(grad_branch, qkvo[:, 3 * breadth :]).astype(jnp.bfloat16)
     grad_mixed, part_proj = meet([grad_mixed, part_proj], trees)
-    trees.extend(launch("fore", jnp.concatenate([part_fore, part_proj], 1)))
+    trees.extend(launch("fore", (part_fore, part_proj)))
     grad_joined = attend_back(joined, log_totals, grad_mixed, live_len)
     (grad_joined,) = meet([grad_joined], trees)
     part_qkv = core_reduce(normed, grad_joined, lead)
     grad_normed = dot_outer(grad_joined, qkvo[:, : 3 * breadth])
+    (grad_normed,) = meet([grad_normed], trees if lead == 1 else [])
     grad_in_norm, grad_scale_one, grad_shift_one = jax.vjp(layer_norm, inputs, parts[0], parts[1])[
         1
     ](grad_normed)
@@ -448,12 +441,6 @@
 
 def across(x, name):
     return lax.ppermute(x, name, FLIP)
-
-
-def sum_bits(x, names):
-    for name in names:
-        x = x + across(x, name)
-    return x
 
 
 def per_device(
@@ -549,10 +536,17 @@
     message = jnp.concatenate([message, sought], 1)
     width = message.shape[1]
     message = jnp.pad(message, ((0, 0), (0, -width % 1024))).reshape(count, -1, 128)
+    first_moved = lax.ppermute(wide_b[:, :cut], every, swap_pairs)
+    table_own = embedding.astype(BF)
+    pad_rows = -(-slice_rows // 16) * 16
+    table_four = Gather(
+        jnp.pad(table_own, ((0, pad_rows - slice_rows), (0, 0))),
+        ("pair", "core"),
+        ("pair", "core"),
+    )
     def moved(x):
         return lax.ppermute(x, every, swap_pairs)
 
-    first_moved = moved(wide_b[:, :cut])
     board = lax.all_to_all(message, every, 0, 0, tiled=True).reshape(count, -1)
     posit_b = lax.all_gather(position_table.astype(BF), every, axis=0, tiled=True)[:seq_len]
     posit_names = ("core",) + shard_names
@@ -564,18 +558,9 @@
     (board, first_moved) = meet([board, first_moved], [shared_one])
     stays = at_core == at_half
     there, back = rest + ("core",), rest[::-1] + ("core",)
-    private_one = Gather(jnp.where(stays, wide_b[:, :cut], first_moved), crew, there)
+    private_one = Gather(jnp.where(stays, wide_b[:, :cut], first_moved), crew, back)
     second_moved, third_moved = moved(wide_b[:, cut:]), moved(down_b)
 
-    table_own = embedding.astype(BF)
-    pad_rows = -(-slice_rows // 16) * 16
-    table_four = Gather(
-        jnp.pad(table_own, ((0, pad_rows - slice_rows), (0, 0))),
-        ("pair", "core"),
-        ("pair", "core"),
-        (),
-        True,
-    )
     filled = jnp.where(
         jnp.arange(clients * pad_rows, dtype=jnp.int32) % pad_rows < slice_rows, 0.0, -jnp.inf
     )
@@ -629,14 +614,16 @@
         return land(turn, rows, lax.all_to_all(sent, every, 0, 0, tiled=True))
 
     sent = jnp.take(table_own, asked_first, axis=0, mode="clip")
-    (sent,) = meet([sent], [private_one, shared_one])
     got = lax.all_to_all(sent, every, 0, 0, tiled=True)
     shared_two = Gather(shared_b[:, cut:], every, spread)
-    shared_three = Gather(shared_down_b, every, spread, (0, 0, 0, 0))
+    shared_three = Gather(shared_down_b, every, spread)
     second_moved, third_moved = meet([second_moved, third_moved], [private_one, shared_one])
     private_two = Gather(jnp.where(stays, wide_b[:, cut:], second_moved), crew, back)
     private_three = Gather(jnp.where(stays, down_b, third_moved), crew, there)
-    (got,) = meet([got], [private_two, private_three, shared_two, shared_three])
+    meet([], [shared_one])
+    meet([], [private_one, private_two, private_three, shared_two, shared_three])
+    meet([], [shared_two, shared_three])
+    (got,) = meet([got], [table_four])
     rows = land(0, jnp.zeros((seq_len, D), BF), got)
     rows = lax.fori_loop(1, rounds, fetch, rows)
     inputs = rows.astype(F32) + posit_b.astype(F32)
@@ -644,10 +631,10 @@
     weights_p = (private_one, private_two, private_three)
     weights_s = (shared_one, shared_two, shared_three)
     first_out, first_saved, weights_p = layer_forward(
-        inputs, weights_p, vect_p, my_len, ([private_two, private_three, *weights_s], [shared_two, shared_three])
+        inputs, weights_p, vect_p, my_len, ([private_two, private_three, shared_one, shared_two], [shared_three])
     )
     second_out, second_saved, weights_s = layer_forward(
-        first_out, weights_s, vect_s[: 8 * D + FF], my_len, ([shared_two], [table_four])
+        first_out, weights_s, vect_s[: 8 * D + FF], my_len, ([shared_two], [])
     )
 
     final_scale = vect_s[8 * D + FF : 9 * D + FF]
@@ -658,7 +645,6 @@
 
     scored_tree = Gather(final_b, shard_names, shard_names)
     meet([final_b], [scored_tree])
-    meet([final_b], [scored_tree, table_four])
     table_four = table_four.result()
     scored = scored_tree.result()
 
@@ -685,7 +671,8 @@
     exponent = jnp.exp(logits - part_max[:, None])
     part_sum = jnp.sum(exponent, -1)
     part_target = jnp.sum(jnp.where(hit, logits, 0.0), -1)
-    pulled = dot_plain(exponent.astype(BF), table_four)
+    exponent, part_sum, part_target = fence(exponent.astype(BF), part_sum, part_target)
+    pulled = dot_plain(exponent, table_four)
     stats = jnp.stack([part_max, part_sum, part_target])
     stats = lax.all_to_all(
         jnp.broadcast_to(stats, (shards,) + stats.shape), shard_names, 0, 0, tiled=True
@@ -698,7 +685,7 @@
     pulled = (pulled * (weight * jnp.exp(part_max - log_all))[:, None]).astype(BF)
     pulled_tree = Reduce(pulled, shard_names, shard_names[::-1])
     grad_logits = (
-        weight[:, None] * jnp.exp(logits - log_all[:, None])
+        exponent.astype(F32) * (weight * jnp.exp(part_max - log_all))[:, None]
         - jnp.where(hit, weight[:, None], 0.0)
     ).astype(BF)
     head_parts = []
@@ -720,11 +707,17 @@
         layer_norm, final_in, final_scale, final_shift
     )[1](grad_final_b)
     grad_second = jnp.zeros_like(second_out).at[my_picks].add(grad_final_in)
-    shared_rest, waits_s = ("pair",) + shard_names, {"down": (2,), "fore": (2,), "qkv": (1, 1)}
+    shared_rest = ("pair",) + shard_names
 
     def launch_s(kind, part):
+        if kind == "fore":
+            shared_trees[kind] = part
+            return []
+        if kind == "qkv":
+            part = jnp.concatenate([part, *shared_trees["fore"][::-1]], 1)
+        waits = (2,) if kind == "down" else (3, 1)
         shared_trees[kind] = Reduce(
-            part, shared_rest, ("pair",) + shard_names[::-1], None, waits_s[kind]
+            part, shared_rest, ("pair",) + shard_names[::-1], None, waits
         )
         return [shared_trees[kind]]
 
@@ -732,10 +725,12 @@
         lambda x: lax.ppermute(x, every, swap_pairs),
         lambda x, other: jnp.where(at_core == at_half, x, other),
     )
-    waits_p = {"down": (2,), "fore": ()}
+    waits_p = {"down": (2,), "fore": (1,)}
 
     def launch_p(kind, part):
         order = rest[::-1] if kind == "down" else rest
+        if kind == "fore":
+            part = jnp.concatenate(part, 1)
         private_trees[kind] = [Reduce(part, rest, order, unswap, waits_p[kind])]
         return private_trees[kind]
 
@@ -756,7 +751,7 @@
         ("pair",),
         ("pair",),
         None,
-        (1, 2),
+        (3, 2),
         True,
     )
     trees.append(head_tree)
@@ -803,27 +798,25 @@
     tree_one = Reduce(qkv_one, rest, rest[::-1], unswap)
     tree_two = Reduce(part_qkv[:, middle:], rest, rest, unswap)
     trees += [tree_one, tree_two]
-    (sent_back,) = meet([sent_back], trees)
     got_back = lax.all_to_all(sent_back, every, 0, 0, tiled=True)
 
     posit_tree = Reduce(grad_rows, posit_names, ("core",) + shard_names[::-1])
-    meet([sent_back], trees + [posit_tree])
-    meet([sent_back], [posit_tree])
+    posit_tree.step()
+    (got_back,) = meet([got_back], trees + [posit_tree])
+    meet([], [tree_one, tree_two, posit_tree])
+    grad_table = settle(asked_first, got_back, 0.0)
     grad_posit = posit_tree.result()
     grad_posit = grad_posit + across(grad_posit.astype(BF), "pair").astype(F32)
     grad_posit = jnp.where(at_pair == 0, grad_posit, 0.0)
     grad_vect_sh = jnp.sum(vector_tree.result().reshape(count, -1), 0)[:width_s]
     head_own = head_tree.result()[:slice_rows]
-    g_down_s, g_fore_s, g_qkv_s = [
-        shared_trees[kind].result() for kind in ("down", "fore", "qkv")
-    ]
-    g_wide_s = jnp.concatenate([g_qkv_s, g_fore_s[:, FF:], g_fore_s[:, :FF]], 1)
+    g_down_s, g_wide_s = shared_trees["down"].result(), shared_trees["qkv"].result()
     g_down_p, g_fore_p = [private_trees[kind][0].result() for kind in ("down", "fore")]
     g_qkv_p, g_qkv_q = tree_one.result(), tree_two.result()
     g_qkv_p, grad_vect_ph = g_qkv_p[:height], g_qkv_p[height, :width_p]
     g_wide_p = jnp.concatenate([g_qkv_p, g_qkv_q, g_fore_p[:, FF:], g_fore_p[:, :FF]], 1)
 
-    grad_table = settle(asked_first, got_back, head_own)
+    grad_table = grad_table + head_own
     grad_table = lax.fori_loop(1, rounds, give, grad_table)
 
     all_grads = [
@@ -841,8 +834,10 @@
         squares = squares + jnp.sum(gradient * gradient)
     client_at = jnp.arange(clients, dtype=jnp.int32)
     loss_vector = jnp.where(client_at == 2 * at_pair + at_half, own_terms, 0.0)
-    figures = jnp.pad(jnp.concatenate([squares[None], loss_vector]), (0, 127 - clients))
-    figures = sum_bits(figures, every)
+    figures = jnp.concatenate([squares[None], loss_vector])
+    figures = jnp.pad(figures, (0, 127 - clients)).reshape(1, 1, 128)
+    figures = jnp.broadcast_to(figures, (count, 1, 128))
+    figures = jnp.sum(lax.all_to_all(figures, every, 0, 0, tiled=True)[:, 0], 0)
     grad_norm = jnp.sqrt(figures[0])
     own_client = client_at == 2 * at_pair + at_core
     loss_sum = jnp.sum(jnp.where(own_client, figures[1 : 1 + clients], 0.0))

time: 954 us -> 844 us (0.88)
  waiting for transfers between devices: 312 us -> 164 us
  starting transfers between devices: 121 us -> 141 us
  other arithmetic: 207 us -> 220 us
    ppermute x74 -> x65, waiting for transfers between devices: 268 us -> 155 us  [across(): return lax.ppermute(x, name, FLIP)]
    all_to_all x1, waiting for transfers between devices: 30.6 us -> 0.99 us  [send(): self.other = lax.all_to_all(self.held, self.names, 0, 0, tiled=True)]
    all_to_all x1, starting transfers between devices: 4.66 us -> 18.2 us  [per_device(): got = lax.all_to_all(sent, every, 0, 0, tiled=True)]
    dynamic_slice x29 -> x25, local copies, waits for them, and re-layouts: 23.3 us -> 27.2 us  [send(): lax.dynamic_index_in_dim(self.held, 1 - side, dim, True)]
    ppermute x74 -> x65, starting transfers between devices: 88.8 us -> 91.9 us  [across(): return lax.ppermute(x, name, FLIP)]
    unnamed x453 -> x405, local copies, waits for them, and re-layouts: 20.4 us -> 18.7 us
  transfers between devices with their start and end apart: 87 -> 78, of which waited for: 32 -> 17; matrix products, arithmetic and copies ran while one was open for 33% -> 42% of each run, Pallas kernels for 5% -> 6%
where the time goes in v3:
time: 844 us; the launch traced here: 833 us
  other arithmetic  220 us (26%)
  waiting for transfers between devices  164 us (19%)
  matrix products  144 us (17%)
  starting transfers between devices  141 us (17%)
  local copies, waits for them, and re-layouts  78.6 us (9%)
  Pallas kernels  48.6 us (6%)
  between operations  27.6 us (3%)
  blocking collectives  8.81 us (1%)
    ppermute x65, waiting for transfers between devices, across(): return lax.ppermute(x, name, FLIP)  155 us
    ppermute x65, starting transfers between devices, across(): return lax.ppermute(x, name, FLIP)  91.9 us
    select_n x30, other arithmetic, advance(): jnp.where(low_side, jnp.concatenate([self.held, self.other], dim), jnp.co...  65.7 us
    dot_general x11, matrix products, dot_plain(): return jnp.dot(former, latter, preferred_element_type=jnp.float32)  51.4 us
    dot_general x18, matrix products, dot_inner(): lax.dot_general(former, latter, (((0,), (0,)), ((), ())), preferred_eleme...  46.9 us
    dot_general x9, matrix products, dot_outer(): lax.dot_general(former, latter, (((1,), (1,)), ((), ())), preferred_eleme...  45.3 us
    dynamic_slice x25, local copies, waits for them, and re-layouts, send(): lax.dynamic_index_in_dim(self.held, 1 - side, dim, True)  27.2 us
    pallas_call x2, Pallas kernels, attend(): pl.pallas_call(attend_kernel, grid_spec=pltpu.PrefetchScalarGridSpec(num_...  25.2 us
  transfers between devices with their start and end apart: 78, of which 17 were waited for; matrix products, arithmetic and copies ran while one was open for 42% of the time, Pallas kernels for 6%

profile of v3, /device:TPU:0, one launch (start us, length us, event | category | flops | bytes accessed | tf_op | source)
XLA Modules:
  0.0 833.0 jit_solution(3751571447062014987)
XLA Ops:
  39.1 8.0 all-to-all-done.2
  88.5 18.2 %all-to-all-start.3 = ((bf16[32,32,768]{2,1,0:T(8,128)(2,1)}), bf16[32,32,768]{2,1,0:T(8,128)(2,1)}, u32[]{:S(2)}, u32[]{:S(2)}) async-start(bf16[32,32,768]{2,1,0:T(8,128)(2,1)} %bitcast.358), calls=%async_computation.3 | async-start | bytes 3145728 | tf_op jit(solution)/shard_map/all_to_all | solution.py:617
  119.6 8.8 %collective-permute-start.11 = (bf16[1,1,1,1,1,96,768]{6,5,4,3,2,1,0:T(8,128)(2,1)S(1)}, bf16[1,1,1,1,1,96,768]{6,5,4,3,2,1,0:T(8,128)(2,1)S(1)}, u32[]{:S(2)}, u32[]{:S(2)}) collective-permute-start(bf16[1,1,1,1,1,96,768]{6,5,4,3,2,1,0:T(8,128)(2,1)S(1)} %bitcast.421), channel_id=1, source_target_pairs={{0,4},{4,0},{1,5},{5,1},{2,6},{6,2},{3,7},{7,3},{8,12},{12,8},{9,1... | collective-permute-start | bytes 442376 | tf_op jit(solution)/shard_map/ppermute | solution.py:443
  130.8 14.2 %collective-permute-done.11 = bf16[1,1,1,1,1,96,768]{6,5,4,3,2,1,0:T(8,128)(2,1)S(1)} collective-permute-done((bf16[1,1,1,1,1,96,768]{6,5,4,3,2,1,0:T(8,128)(2,1)S(1)}, bf16[1,1,1,1,1,96,768]{6,5,4,3,2,1,0:T(8,128)(2,1)S(1)}, u32[]{:S(2)}, u32[]{:S(2)}) %collective-permute-start.11) | collective-permute-done | bytes 147488 | tf_op jit(solution)/shard_map/ppermute | solution.py:443
  151.2 8.2 collective-permute-start.18
  198.7 12.6 %shard_map.475 = (bf16[512,768]{1,0:T(8,128)(2,1)S(1)}, f32[6,2,512]{2,1,0:T(2,128)S(1)}) custom-call(s32[1]{0:T(128)} %bitcast.32.live_ref, bf16[512,2304]{1,0:T(8,128)(2,1)S(1)} %fusion.26.q_ref.k_ref.v_ref, bf16[512,2304]{1,0:T(8,128)(2,1)S(1)} %fusion.26.q_ref.k_ref.v_ref, bf16[512,2304]{1,0:T(8,128)(2,1)S(1)} %fusion.26.q_ref.k_ref.v_ref), custom_call_target="tpu_custom_call" | custom-call | tf_op jit(solution)/shard_map/pallas_call | solution.py:151
  240.8 12.6 %shard_map.476 = (bf16[512,768]{1,0:T(8,128)(2,1)S(1)}, f32[6,2,512]{2,1,0:T(2,128)S(1)}) custom-call(s32[1]{0:T(128)} %bitcast.32.live_ref, bf16[512,2304]{1,0:T(8,128)(2,1)S(1)} %fusion.27.q_ref.k_ref.v_ref, bf16[512,2304]{1,0:T(8,128)(2,1)S(1)} %fusion.27.q_ref.k_ref.v_ref, bf16[512,2304]{1,0:T(8,128)(2,1)S(1)} %fusion.27.q_ref.k_ref.v_ref), custom_call_target="tpu_custom_call" | custom-call | tf_op jit(solution)/shard_map/pallas_call | solution.py:151
  257.7 7.3 maximum_select_fusion.1
  270.4 12.8 %collective-permute-done.26 = bf16[1,1,2,2,2,96,768]{6,5,4,3,2,1,0:T(8,128)(2,1)} collective-permute-done((bf16[1,1,2,2,2,96,768]{6,5,4,3,2,1,0:T(8,128)(2,1)}, bf16[1,1,2,2,2,96,768]{6,5,4,3,2,1,0:T(8,128)(2,1)}, u32[]{:S(2)}, u32[]{:S(2)}) %collective-permute-start.26) | collective-permute-done | bytes 1179680 | tf_op jit(solution)/shard_map/ppermute | solution.py:443
  306.1 11.3 %collective-permute-done.28 = bf16[1,1,1,128,768]{4,3,2,1,0:T(8,128)(2,1)S(1)} collective-permute-done((bf16[1,1,1,128,768]{4,3,2,1,0:T(8,128)(2,1)S(1)}, bf16[1,1,1,128,768]{4,3,2,1,0:T(8,128)(2,1)S(1)}, u32[]{:S(2)}, u32[]{:S(2)}) %collective-permute-start.28) | collective-permute-done | bytes 196640 | tf_op jit(solution)/shard_map/ppermute | solution.py:443
  319.9 8.5 %collective-permute-done.29 = bf16[2,1,1,128,768]{4,3,2,1,0:T(8,128)(2,1)S(1)} collective-permute-done((bf16[2,1,1,128,768]{4,3,2,1,0:T(8,128)(2,1)S(1)}, bf16[2,1,1,128,768]{4,3,2,1,0:T(8,128)(2,1)S(1)}, u32[]{:S(2)}, u32[]{:S(2)}) %collective-permute-start.29) | collective-permute-done | bytes 393248 | tf_op jit(solution)/shard_map/ppermute | solution.py:443
  329.6 8.0 maximum_select_fusion
  337.6 9.4 %collective-permute-done.30 = bf16[2,2,1,128,768]{4,3,2,1,0:T(8,128)(2,1)S(1)} collective-permute-done((bf16[2,2,1,128,768]{4,3,2,1,0:T(8,128)(2,1)S(1)}, bf16[2,2,1,128,768]{4,3,2,1,0:T(8,128)(2,1)S(1)}, u32[]{:S(2)}, u32[]{:S(2)}) %collective-permute-start.30) | collective-permute-done | bytes 786464 | tf_op jit(solution)/shard_map/ppermute | solution.py:443
  347.3 14.2 %add_reduce_fusion = (f32[1024]{0:T(1024)S(1)}, f32[1024,6336]{0,1:T(8,128)}) fusion(f32[6336]{0:T(1024)S(1)} %copy-done.117, bf16[1024,768]{1,0:T(8,128)(2,1)S(1)} %bitcast.410, bf16[6336,768]{1,0:T(8,128)(2,1)S(1)} %bitcast.353), kind=kOutput, calls=%fused_computation.32 | convolution fusion | flops 9978641408 | bytes 37286656 | tf_op jit(solution)/shard_map/dot_general | solution.py:39
  361.5 16.6 %select_reduce_fusion.2 = (f32[1024]{0:T(1024)S(1)}, f32[1024]{0:T(1024)S(1)}, bf16[1024,6336]{0,1:T(8,128)(2,1)}) fusion(f32[1024,6336]{0,1:T(8,128)} %get-tuple-element.607, s32[1024]{0:T(1024)S(1)} %copy-done.129, f32[6336]{0:T(1024)S(1)} %copy-done.117, f32[1024]{0:T(1024)S(1)} %get-tuple-element.606), kind=kLoop, calls=%fused_computation.27 | loop fusion | flops 45414400 | bytes 38970112 | tf_op jit(solution)/shard_map/reduce_sum | solution.py:673
  383.4 17.4 %fusion.194 = f32[1024,768]{1,0:T(8,128)} fusion(bf16[1024,6336]{0,1:T(8,128)(2,1)} %get-tuple-element.310, bf16[6336,768]{1,0:T(8,128)(2,1)} %bitcast.354), kind=kOutput, calls=%fused_computation.583 | convolution fusion | flops 9965666304 | bytes 25853952 | tf_op jit(solution)/shard_map/dot_general | solution.py:29
  406.1 9.3 %subtract_convert_fusion = bf16[1024,6336]{0,1:T(8,128)(2,1)S(1)} fusion(bf16[1024,6336]{0,1:T(8,128)(2,1)} %get-tuple-element.310, f32[1024]{0:T(1024)S(1)} %get-tuple-element.587, f32[1024]{0:T(1024)S(1)} %get-tuple-element.586, s32[1024]{0:T(1024)S(1)} %copy-done.129), kind=kLoop, calls=%fused_computation.26 | loop fusion | flops 38928384 | bytes 25964544 | tf_op jit(solution)/shard_map/convert_element_type | solution.py:690
  415.5 6.9 convolution_convert_fusion
  424.2 7.1 convolution_convert_fusion.1
  455.8 6.5 fusion.24
  494.7 11.9 %shard_map.477 = bf16[512,2304]{1,0:T(8,128)(2,1)S(1)} custom-call(s32[1]{0:T(128)} %bitcast.32.live_ref, bf16[512,2304]{1,0:T(8,128)(2,1)S(1)} %copy-done.3, bf16[512,2304]{1,0:T(8,128)(2,1)S(1)} %copy-done.3, bf16[512,2304]{1,0:T(8,128)(2,1)S(1)} %copy-done.3, bf16[512,768]{1,0:T(8,128)(2,1)S(1)} %convolution_convert_fusion.9.grad_ref, ...), custom_call_target="tpu_custom_call" | custom-call | tf_op jit(solution)/shard_map/pallas_call | solution.py:180
  523.4 9.3 %collective-permute-done.42 = bf16[1,2,2,1,96,768]{5,4,3,2,1,0:T(8,128)(2,1)S(1)} collective-permute-done((bf16[1,2,2,1,96,768]{5,4,3,2,1,0:T(8,128)(2,1)S(1)}, bf16[1,2,2,1,96,768]{5,4,3,2,1,0:T(8,128)(2,1)S(1)}, u32[]{:S(2)}, u32[]{:S(2)}) %collective-permute-start.42) | collective-permute-done | bytes 589856 | tf_op jit(solution)/shard_map/ppermute | solution.py:443
  540.6 8.3 fusion.17
  582.9 11.5 %shard_map.478 = bf16[512,2304]{1,0:T(8,128)(2,1)S(1)} custom-call(s32[1]{0:T(128)} %bitcast.32.live_ref, bf16[512,2304]{1,0:T(8,128)(2,1)S(1)} %copy-done.1, bf16[512,2304]{1,0:T(8,128)(2,1)S(1)} %copy-done.1, bf16[512,2304]{1,0:T(8,128)(2,1)S(1)} %copy-done.1, bf16[512,768]{1,0:T(8,128)(2,1)S(1)} %convolution_convert_fusion.8.grad_ref, ...), custom_call_target="tpu_custom_call" | custom-call | tf_op jit(solution)/shard_map/pallas_call | solution.py:180
  615.6 12.9 %collective-permute-done.50 = bf16[1,1,384,768]{3,2,1,0:T(8,128)(2,1)S(1)} collective-permute-done((bf16[1,1,384,768]{3,2,1,0:T(8,128)(2,1)}, bf16[1,1,384,768]{3,2,1,0:T(8,128)(2,1)S(1)}, u32[]{:S(2)}, u32[]{:S(2)}) %collective-permute-start.50) | collective-permute-done | bytes 589856 | tf_op jit(solution)/shard_map/ppermute | solution.py:443
  652.5 8.5 %collective-permute-start.62 = (bf16[1,2,2,2,32,768]{5,4,3,2,1,0:T(8,128)(2,1)}, bf16[1,2,2,2,32,768]{5,4,3,2,1,0:T(8,128)(2,1)}, u32[]{:S(2)}, u32[]{:S(2)}) collective-permute-start(bf16[1,2,2,2,32,768]{5,4,3,2,1,0:T(8,128)(2,1)} %constant_dynamic-slice_fusion.12), channel_id=1, source_target_pairs={{0,8},{8,0},{1,9},{9,1},{2,10},{10,2},{3,11},{11,3},{4,12},{12,4},... | collective-permute-start | bytes 1179656 | tf_op jit(solution)/shard_map/ppermute | solution.py:443
  683.7 45.5 %collective-permute-done.61 = bf16[1,2,96,1152]{3,2,1,0:T(8,128)(2,1)S(1)} collective-permute-done((bf16[1,2,96,1152]{3,2,1,0:T(8,128)(2,1)S(1)}, bf16[1,2,96,1152]{3,2,1,0:T(8,128)(2,1)S(1)}, u32[]{:S(2)}, u32[]{:S(2)}) %collective-permute-start.61) | collective-permute-done | bytes 442400 | tf_op jit(solution)/shard_map/ppermute | solution.py:443
  739.3 6.5 bitcast_add_fusion
  761.3 15.9 %collective-permute-done.67 = bf16[1,1,1,1,32,768]{5,4,3,2,1,0:T(8,128)(2,1)S(1)} collective-permute-done((bf16[1,1,1,1,32,768]{5,4,3,2,1,0:T(8,128)(2,1)S(1)}, bf16[1,1,1,1,32,768]{5,4,3,2,1,0:T(8,128)(2,1)S(1)}, u32[]{:S(2)}, u32[]{:S(2)}) %collective-permute-start.67) | collective-permute-done | bytes 49184 | tf_op jit(solution)/shard_map/ppermute | solution.py:443
  791.1 8.8 %all_to_all.68 = f32[32,1,128]{2,1,0:T(1,128)S(1)} all-to-all(f32[32,1,128]{2,1,0:T(1,128)S(1)} %broadcast_in_dim.311), channel_id=1, replica_groups=mesh['pair'=2,'core'=2,'s0'=2,'s1'=2,'s2'=2] {'pair','core','s0','s1','s2'}, dimensions={0} | all-to-all | bytes 32768 | tf_op jit(solution)/shard_map/all_to_all | solution.py:840
  802.5 6.9 multiply_subtract_fusion.1
  811.2 8.6 %multiply_subtract_fusion = (f32[1572,768]{1,0:T(8,128)}, f32[1572,768]{1,0:T(8,128)}, f32[1572,768]{1,0:T(8,128)}) fusion(f32[1572,768]{1,0:T(8,128)S(1)} %bitcast.348, f32[1572,768]{1,0:T(8,128)S(1)} %bitcast.350, f32[]{:T(128)S(6)} %min.3, f32[1572,768]{1,0:T(8,128)S(1)} %bitcast.368, f32[1572,768]{1,0:T(8,128)} %param.38), kind=kLoop, calls=%fused_computation.70 | loop fusion | flops 18109440 | bytes 33804292 | tf_op jit(solution)/shard_map/sub | solution.py:435
  (902 shorter events, 432.9 us)
Async XLA Ops:
  9.1 38.3 %collective-permute-start.1 = (bf16[1,1,1,1,1,24,3072]{6,5,4,3,2,1,0:T(8,128)(2,1)}, bf16[1,1,1,1,1,24,3072]{6,5,4,3,2,1,0:T(8,128)(2,1)}, u32[]{:S(2)}, u32[]{:S(2)}) collective-permute-start(bf16[1,1,1,1,1,24,3072]{6,5,4,3,2,1,0:T(8,128)(2,1)} %slice_bitcast_fusion.3), channel_id=1, source_target_pairs={{0,4},{4,0},{1,5},{5,1},{2,6},{6,2},{3,7},{7,3},{8,12},{12,8},{9,1... | collective-permute-start | bytes 442376 | tf_op jit(solution)/shard_map/ppermute | solution.py:443
  16.9 30.6 %collective-permute-start = (bf16[96,3072]{1,0:T(8,128)(2,1)}, bf16[96,3072]{1,0:T(8,128)(2,1)}, u32[]{:S(2)}, u32[]{:S(2)}) collective-permute-start(bf16[96,3072]{1,0:T(8,128)(2,1)} %slice.336), channel_id=1, source_target_pairs={{4,8},{8,4},{5,9},{9,5},{6,10},{10,6},{7,11},{11,7},{20,24},{24,20... | collective-permute-start | bytes 1769480 | tf_op jit(solution)/shard_map/ppermute | solution.py:539
  30.2 156.7 %all-gather.2.cloned.1.call-start = ((), (), s32[]{:S(2)}) async-start(), calls=%async_computation.8 | async-start | bytes 1622016 | tf_op jit(solution)/shard_map/all_gather | solution.py:551
  31.8 147.7 %collective-permute-start.2 = (bf16[1,1,1584,768]{3,2,1,0:T(8,128)(2,1)}, bf16[1,1,1584,768]{3,2,1,0:T(8,128)(2,1)}, u32[]{:S(2)}, u32[]{:S(2)}) collective-permute-start(bf16[1,1,1584,768]{3,2,1,0:T(8,128)(2,1)} %pad_bitcast_fusion), channel_id=1, source_target_pairs={{0,16},{16,0},{1,17},{17,1},{2,18},{18,2},{3,19},{19,3},{4,20},{20... | collective-permute-start | bytes 7299080 | tf_op jit(solution)/shard_map/ppermute | solution.py:443
  76.0 43.5 %collective-permute-start.10 = (bf16[1,1,1,1,1,24,3072]{6,5,4,3,2,1,0:T(8,128)(2,1)}, bf16[1,1,1,1,1,24,3072]{6,5,4,3,2,1,0:T(8,128)(2,1)}, u32[]{:S(2)}, u32[]{:S(2)}) collective-permute-start(bf16[1,1,1,1,1,24,3072]{6,5,4,3,2,1,0:T(8,128)(2,1)} %slice_bitcast_fusion.4), channel_id=1, source_target_pairs={{0,4},{4,0},{1,5},{5,1},{2,6},{6,2},{3,7},{7,3},{8,12},{12,8},{9,1... | collective-permute-start | bytes 442376 | tf_op jit(solution)/shard_map/ppermute | solution.py:443
  84.1 67.1 %collective-permute-start.7 = (bf16[1,1,2,96,3072]{4,3,2,1,0:T(8,128)(2,1)}, bf16[1,1,2,96,3072]{4,3,2,1,0:T(8,128)(2,1)}, u32[]{:S(2)}, u32[]{:S(2)}) collective-permute-start(bf16[1,1,2,96,3072]{4,3,2,1,0:T(8,128)(2,1)} %maximum_select_fusion.15), channel_id=1, source_target_pairs={{0,2},{2,0},{1,3},{3,1},{4,6},{6,4},{5,7},{7,5},{8,10},{10,8},{9,1... | collective-permute-start | bytes 3538952 | tf_op jit(solution)/shard_map/ppermute | solution.py:443
  85.6 65.6 %collective-permute-start.9 = (bf16[1,1,1,384,768]{4,3,2,1,0:T(8,128)(2,1)}, bf16[1,1,1,384,768]{4,3,2,1,0:T(8,128)(2,1)}, u32[]{:S(2)}, u32[]{:S(2)}) collective-permute-start(bf16[1,1,1,384,768]{4,3,2,1,0:T(8,128)(2,1)} %select_bitcast_fusion), channel_id=1, source_target_pairs={{0,2},{2,0},{1,3},{3,1},{4,6},{6,4},{5,7},{7,5},{8,10},{10,8},{9,1... | collective-permute-start | bytes 1769480 | tf_op jit(solution)/shard_map/ppermute | solution.py:443
  88.5 92.4 %all-to-all-start.3 = ((bf16[32,32,768]{2,1,0:T(8,128)(2,1)}), bf16[32,32,768]{2,1,0:T(8,128)(2,1)}, u32[]{:S(2)}, u32[]{:S(2)}) async-start(bf16[32,32,768]{2,1,0:T(8,128)(2,1)} %bitcast.358), calls=%async_computation.3 | async-start | bytes 3145728 | tf_op jit(solution)/shard_map/all_to_all | solution.py:617
  108.6 42.5 %collective-permute-start.8 = (bf16[1,1,1,96,3072]{4,3,2,1,0:T(8,128)(2,1)}, bf16[1,1,1,96,3072]{4,3,2,1,0:T(8,128)(2,1)}, u32[]{:S(2)}, u32[]{:S(2)}) collective-permute-start(bf16[1,1,1,96,3072]{4,3,2,1,0:T(8,128)(2,1)} %select_bitcast_fusion.1), channel_id=1, source_target_pairs={{0,1},{1,0},{2,3},{3,2},{4,5},{5,4},{6,7},{7,6},{8,9},{9,8},{10,11... | collective-permute-start | bytes 1769480 | tf_op jit(solution)/shard_map/ppermute | solution.py:443
  145.0 66.3 %collective-permute-start.16 = (bf16[1,1,2,2,2,24,3072]{6,5,4,3,2,1,0:T(8,128)(2,1)}, bf16[1,1,2,2,2,24,3072]{6,5,4,3,2,1,0:T(8,128)(2,1)}, u32[]{:S(2)}, u32[]{:S(2)}) collective-permute-start(bf16[1,1,2,2,2,24,3072]{6,5,4,3,2,1,0:T(8,128)(2,1)} %maximum_select_fusion.18), channel_id=1, source_target_pairs={{0,16},{16,0},{1,17},{17,1},{2,18},{18,2},{3,19},{19,3},{4,20},{20... | collective-permute-start | bytes 3538952 | tf_op jit(solution)/shard_map/ppermute | solution.py:443
  163.4 47.9 %collective-permute-start.14 = (bf16[1,2,1,384,768]{4,3,2,1,0:T(8,128)(2,1)}, bf16[1,2,1,384,768]{4,3,2,1,0:T(8,128)(2,1)}, u32[]{:S(2)}, u32[]{:S(2)}) collective-permute-start(bf16[1,2,1,384,768]{4,3,2,1,0:T(8,128)(2,1)} %maximum_select_fusion.17), channel_id=1, source_target_pairs={{0,1},{1,0},{2,3},{3,2},{4,5},{5,4},{6,7},{7,6},{8,9},{9,8},{10,11... | collective-permute-start | bytes 3538952 | tf_op jit(solution)/shard_map/ppermute | solution.py:443
  172.4 39.0 %collective-permute-start.13 = (bf16[1,1,2,96,3072]{4,3,2,1,0:T(8,128)(2,1)}, bf16[1,1,2,96,3072]{4,3,2,1,0:T(8,128)(2,1)}, u32[]{:S(2)}, u32[]{:S(2)}) collective-permute-start(bf16[1,1,2,96,3072]{4,3,2,1,0:T(8,128)(2,1)} %maximum_select_fusion.16), channel_id=1, source_target_pairs={{0,2},{2,0},{1,3},{3,1},{4,6},{6,4},{5,7},{7,5},{8,10},{10,8},{9,1... | collective-permute-start | bytes 3538952 | tf_op jit(solution)/shard_map/ppermute | solution.py:443
  179.5 31.8 %collective-permute-start.19 = (bf16[1,1,2,2,1,24,3072]{6,5,4,3,2,1,0:T(8,128)(2,1)}, bf16[1,1,2,2,1,24,3072]{6,5,4,3,2,1,0:T(8,128)(2,1)}, u32[]{:S(2)}, u32[]{:S(2)}) collective-permute-start(bf16[1,1,2,2,1,24,3072]{6,5,4,3,2,1,0:T(8,128)(2,1)} %maximum_select_fusion.24), channel_id=1, source_target_pairs={{0,1},{1,0},{2,3},{3,2},{4,5},{5,4},{6,7},{7,6},{8,9},{9,8},{10,11... | collective-permute-start | bytes 1769480 | tf_op jit(solution)/shard_map/ppermute | solution.py:443
  191.4 41.0 %collective-permute-start.21 = (bf16[1,1,2,2,1,96,768]{6,5,3,2,4,1,0:T(8,128)(2,1)S(1)}, bf16[1,1,2,2,1,96,768]{6,5,3,2,4,1,0:T(8,128)(2,1)S(1)}, u32[]{:S(2)}, u32[]{:S(2)}) collective-permute-start(bf16[1,1,2,2,1,96,768]{6,5,3,2,4,1,0:T(8,128)(2,1)S(1)} %copy-done.106), channel_id=1, source_target_pairs={{0,1},{1,0},{2,3},{3,2},{4,5},{5,4},{6,7},{7,6},{8,9},{9,8},{10,11... | collective-permute-start | bytes 1769480 | tf_op jit(solution)/shard_map/ppermute | solution.py:443
  216.6 36.8 %collective-permute-start.24 = (bf16[1,1,2,2,2,24,3072]{6,5,4,3,2,1,0:T(8,128)(2,1)S(1)}, bf16[1,1,2,2,2,24,3072]{6,5,4,3,2,1,0:T(8,128)(2,1)S(1)}, u32[]{:S(2)}, u32[]{:S(2)}) collective-permute-start(bf16[1,1,2,2,2,24,3072]{6,5,4,3,2,1,0:T(8,128)(2,1)S(1)} %maximum_select_fusion.19), channel_id=1, source_target_pairs={{0,16},{16,0},{1,17},{17,1},{2,18},{18,2},{3,19},{19,3},{4,20},{20... | collective-permute-start | bytes 3538952 | tf_op jit(solution)/shard_map/ppermute | solution.py:443
  264.9 64.6 %collective-permute-start.31 = (bf16[2,1,1584,768]{3,2,1,0:T(8,128)(2,1)}, bf16[2,1,1584,768]{3,2,1,0:T(8,128)(2,1)}, u32[]{:S(2)}, u32[]{:S(2)}) collective-permute-start(bf16[2,1,1584,768]{3,2,1,0:T(8,128)(2,1)} %maximum_select_fusion.1), channel_id=1, source_target_pairs={{0,8},{8,0},{1,9},{9,1},{2,10},{10,2},{3,11},{11,3},{4,12},{12,4},... | collective-permute-start | bytes 14598152 | tf_op jit(solution)/shard_map/ppermute | solution.py:443
  450.7 32.8 %collective-permute-start.37 = (bf16[1,1584,768]{2,1,0:T(8,128)(2,1)}, bf16[1,1584,768]{2,1,0:T(8,128)(2,1)}, u32[]{:S(2)}, u32[]{:S(2)}) collective-permute-start(bf16[1,1584,768]{2,1,0:T(8,128)(2,1)} %get-tuple-element.505), channel_id=1, source_target_pairs={{0,8},{8,0},{1,9},{9,1},{2,10},{10,2},{3,11},{11,3},{4,12},{12,4},... | collective-permute-start | bytes 7299080 | tf_op jit(solution)/shard_map/ppermute | solution.py:443
  468.7 37.9 %collective-permute-start.40 = (bf16[1,2,2,2,96,768]{5,4,3,2,1,0:T(8,128)(2,1)}, bf16[1,2,2,2,96,768]{5,4,3,2,1,0:T(8,128)(2,1)}, u32[]{:S(2)}, u32[]{:S(2)}) collective-permute-start(bf16[1,2,2,2,96,768]{5,4,3,2,1,0:T(8,128)(2,1)} %get-tuple-element.519), channel_id=1, source_target_pairs={{0,16},{16,0},{1,17},{17,1},{2,18},{18,2},{3,19},{19,3},{4,20},{20... | collective-permute-start | bytes 3538952 | tf_op jit(solution)/shard_map/ppermute | solution.py:443
  539.5 55.0 %collective-permute-start.48 = (bf16[1,2,2,2,24,6144]{5,4,3,2,1,0:T(8,128)(2,1)}, bf16[1,2,2,2,24,6144]{5,4,3,2,1,0:T(8,128)(2,1)}, u32[]{:S(2)}, u32[]{:S(2)}) collective-permute-start(bf16[1,2,2,2,24,6144]{5,4,3,2,1,0:T(8,128)(2,1)} %get-tuple-element.507), channel_id=1, source_target_pairs={{0,16},{16,0},{1,17},{17,1},{2,18},{18,2},{3,19},{19,3},{4,20},{20... | collective-permute-start | bytes 7077896 | tf_op jit(solution)/shard_map/ppermute | solution.py:443
  565.5 30.0 %collective-permute-start.49 = (bf16[2,1,384,768]{3,2,1,0:T(8,128)(2,1)}, bf16[2,1,384,768]{3,2,1,0:T(8,128)(2,1)}, u32[]{:S(2)}, u32[]{:S(2)}) collective-permute-start(bf16[2,1,384,768]{3,2,1,0:T(8,128)(2,1)} %get-tuple-element.517), channel_id=1, source_target_pairs={{0,1},{1,0},{2,3},{3,2},{4,5},{5,4},{6,7},{7,6},{8,9},{9,8},{10,11... | collective-permute-start | bytes 3538952 | tf_op jit(solution)/shard_map/ppermute | solution.py:443
  581.0 47.4 %collective-permute-start.51 = (bf16[1,2,96,3840]{3,2,1,0:T(8,128)(2,1)}, bf16[1,2,96,3840]{3,2,1,0:T(8,128)(2,1)}, u32[]{:S(2)}, u32[]{:S(2)}) collective-permute-start(bf16[1,2,96,3840]{3,2,1,0:T(8,128)(2,1)} %get-tuple-element.513), channel_id=1, source_target_pairs={{0,2},{2,0},{1,3},{3,1},{4,6},{6,4},{5,7},{7,5},{8,10},{10,8},{9,1... | collective-permute-start | bytes 4423688 | tf_op jit(solution)/shard_map/ppermute | solution.py:443
  598.6 29.8 %collective-permute-start.50 = (bf16[1,1,384,768]{3,2,1,0:T(8,128)(2,1)}, bf16[1,1,384,768]{3,2,1,0:T(8,128)(2,1)S(1)}, u32[]{:S(2)}, u32[]{:S(2)}) collective-permute-start(bf16[1,1,384,768]{3,2,1,0:T(8,128)(2,1)} %get-tuple-element.529), channel_id=1, source_target_pairs={{0,2},{2,0},{1,3},{3,1},{4,6},{6,4},{5,7},{7,5},{8,10},{10,8},{9,1... | collective-permute-start | bytes 1769480 | tf_op jit(solution)/shard_map/ppermute | solution.py:443
  603.8 40.8 %collective-permute-start.53 = (bf16[1,2,2,1,24,6144]{5,4,3,2,1,0:T(8,128)(2,1)}, bf16[1,2,2,1,24,6144]{5,4,3,2,1,0:T(8,128)(2,1)}, u32[]{:S(2)}, u32[]{:S(2)}) collective-permute-start(bf16[1,2,2,1,24,6144]{5,4,3,2,1,0:T(8,128)(2,1)} %get-tuple-element.515), channel_id=1, source_target_pairs={{0,1},{1,0},{2,3},{3,2},{4,5},{5,4},{6,7},{7,6},{8,9},{9,8},{10,11... | collective-permute-start | bytes 3538952 | tf_op jit(solution)/shard_map/ppermute | solution.py:443
  606.7 35.3 %collective-permute-start.52 = (bf16[384,2304]{1,0:T(8,128)(2,1)}, bf16[384,2304]{1,0:T(8,128)(2,1)}, u32[]{:S(2)}, u32[]{:S(2)}) collective-permute-start(bf16[384,2304]{1,0:T(8,128)(2,1)} %convolution_convert_fusion.2), channel_id=1, source_target_pairs={{0,8},{8,0},{1,9},{9,1},{2,10},{10,2},{3,11},{11,3},{4,12},{12,4},... | collective-permute-start | bytes 5308424 | tf_op jit(solution)/shard_map/ppermute | solution.py:443
  609.3 69.9 %collective-permute-start.57 = (bf16[1,1584,768]{2,1,0:T(8,128)(2,1)}, bf16[1,1584,768]{2,1,0:T(8,128)(2,1)}, u32[]{:S(2)}, u32[]{:S(2)}) collective-permute-start(bf16[1,1584,768]{2,1,0:T(8,128)(2,1)} %get-tuple-element.501), channel_id=1, source_target_pairs={{0,16},{16,0},{1,17},{17,1},{2,18},{18,2},{3,19},{19,3},{4,20},{20... | collective-permute-start | bytes 7299080 | tf_op jit(solution)/shard_map/ppermute | solution.py:443
  662.2 67.0 %collective-permute-start.60 = (bf16[2,1,112,1152]{3,2,1,0:T(8,128)(2,1)}, bf16[2,1,112,1152]{3,2,1,0:T(8,128)(2,1)}, u32[]{:S(2)}, u32[]{:S(2)}) collective-permute-start(bf16[2,1,112,1152]{3,2,1,0:T(8,128)(2,1)} %get-tuple-element.535), channel_id=1, source_target_pairs={{0,1},{1,0},{2,3},{3,2},{4,5},{5,4},{6,7},{7,6},{8,9},{9,8},{10,11... | collective-permute-start | bytes 1548296 | tf_op jit(solution)/shard_map/ppermute | solution.py:443
  666.4 62.9 %all-to-all-start.6 = ((bf16[32,32,768]{2,1,0:T(8,128)(2,1)}), bf16[32,32,768]{2,1,0:T(8,128)(2,1)}, u32[]{:S(2)}, u32[]{:S(2)}) async-start(bf16[32,32,768]{2,1,0:T(8,128)(2,1)} %bitcast.409), calls=%async_computation.6 | async-start | bytes 3145728 | tf_op jit(solution)/shard_map/all_to_all | solution.py:801
  672.5 56.8 %collective-permute-start.58 = (bf16[1,1,96,3840]{3,2,1,0:T(8,128)(2,1)S(1)}, bf16[1,1,96,3840]{3,2,1,0:T(8,128)(2,1)}, u32[]{:S(2)}, u32[]{:S(2)}) collective-permute-start(bf16[1,1,96,3840]{3,2,1,0:T(8,128)(2,1)S(1)} %add_convert_fusion.16), channel_id=1, source_target_pairs={{4,8},{8,4},{5,9},{9,5},{6,10},{10,6},{7,11},{11,7},{20,24},{24,20... | collective-permute-start | bytes 2211848 | tf_op jit(solution)/shard_map/ppermute | solution.py:725
  675.7 53.5 %collective-permute-start.56 = (bf16[1,2,1,1,24,6144]{5,4,3,2,1,0:T(8,128)(2,1)S(1)}, bf16[1,2,1,1,24,6144]{5,4,3,2,1,0:T(8,128)(2,1)}, u32[]{:S(2)}, u32[]{:S(2)}) collective-permute-start(bf16[1,2,1,1,24,6144]{5,4,3,2,1,0:T(8,128)(2,1)S(1)} %get-tuple-element.527), channel_id=1, source_target_pairs={{0,2},{2,0},{1,3},{3,1},{4,6},{6,4},{5,7},{7,5},{8,10},{10,8},{9,1... | collective-permute-start | bytes 1769480 | tf_op jit(solution)/shard_map/ppermute | solution.py:443
  677.5 51.7 %collective-permute-start.61 = (bf16[1,2,96,1152]{3,2,1,0:T(8,128)(2,1)S(1)}, bf16[1,2,96,1152]{3,2,1,0:T(8,128)(2,1)S(1)}, u32[]{:S(2)}, u32[]{:S(2)}) collective-permute-start(bf16[1,2,96,1152]{3,2,1,0:T(8,128)(2,1)S(1)} %get-tuple-element.537), channel_id=1, source_target_pairs={{0,2},{2,0},{1,3},{3,1},{4,6},{6,4},{5,7},{7,5},{8,10},{10,8},{9,1... | collective-permute-start | bytes 1327112 | tf_op jit(solution)/shard_map/ppermute | solution.py:443
  679.2 50.0 %collective-permute-start.63 = (bf16[1,2,2,1,32,768]{5,4,3,2,1,0:T(8,128)(2,1)S(1)}, bf16[1,2,2,1,32,768]{5,4,3,2,1,0:T(8,128)(2,1)S(1)}, u32[]{:S(2)}, u32[]{:S(2)}) collective-permute-start(bf16[1,2,2,1,32,768]{5,4,3,2,1,0:T(8,128)(2,1)S(1)} %get-tuple-element.561), channel_id=1, source_target_pairs={{0,1},{1,0},{2,3},{3,2},{4,5},{5,4},{6,7},{7,6},{8,9},{9,8},{10,11... | collective-permute-start | bytes 589832 | tf_op jit(solution)/shard_map/ppermute | solution.py:443
  755.8 30.6 %collective-permute-start.70 = (bf16[1,1,112,1152]{3,2,1,0:T(8,128)(2,1)S(1)}, bf16[1,1,112,1152]{3,2,1,0:T(8,128)(2,1)}, u32[]{:S(2)}, u32[]{:S(2)}) collective-permute-start(bf16[1,1,112,1152]{3,2,1,0:T(8,128)(2,1)S(1)} %add_convert_fusion.25), channel_id=1, source_target_pairs={{4,8},{8,4},{5,9},{9,5},{6,10},{10,6},{7,11},{11,7},{20,24},{24,20... | collective-permute-start | bytes 774152 | tf_op jit(solution)/shard_map/ppermute | solution.py:725
  (246 other events, 2934.6 us)
Sparse Core Ops, SparseCore 0:
  34.5 66.9 all-gather.1

commit v4 on v3

--- a/solution.py
+++ b/solution.py
@@ -634,7 +634,7 @@
         inputs, weights_p, vect_p, my_len, ([private_two, private_three, shared_one, shared_two], [shared_three])
     )
     second_out, second_saved, weights_s = layer_forward(
-        first_out, weights_s, vect_s[: 8 * D + FF], my_len, ([shared_two], [])
+        first_out, weights_s, vect_s[: 8 * D + FF], my_len, ([shared_two, shared_three], [])
     )
 
     final_scale = vect_s[8 * D + FF : 9 * D + FF]

time: 844 us -> 841 us (level)
  starting transfers between devices: 141 us -> 126 us
  waiting for transfers between devices: 164 us -> 179 us
    ppermute x65, waiting for transfers between devices: 155 us -> 170 us  [across(): return lax.ppermute(x, name, FLIP)]
    ppermute x65, starting transfers between devices: 91.9 us -> 79.7 us  [across(): return lax.ppermute(x, name, FLIP)]
    select_n x30 -> x29, other arithmetic: 65.7 us -> 62.8 us  [advance(): jnp.where(low_side, jnp.concatenate([self.held, self.other], dim), jnp.co...]
    unnamed x405 -> x411, local copies, waits for them, and re-layouts: 18.7 us -> 18.7 us
  transfers between devices with their start and end apart: 78 -> 78, of which waited for: 17 -> 18; matrix products, arithmetic and copies ran while one was open for 42% -> 41% of each run, Pallas kernels for 6% -> 6%
where the time goes in v4:
time: 841 us; the launch traced here: 830 us
  other arithmetic  215 us (26%)
  waiting for transfers between devices  179 us (21%)
  matrix products  144 us (17%)
  starting transfers between devices  126 us (15%)
  local copies, waits for them, and re-layouts  80.1 us (10%)
  Pallas kernels  48.4 us (6%)
  between operations  27.8 us (3%)
  blocking collectives  8.81 us (1%)
    ppermute x65, waiting for transfers between devices, across(): return lax.ppermute(x, name, FLIP)  170 us
    ppermute x65, starting transfers between devices, across(): return lax.ppermute(x, name, FLIP)  79.7 us
    select_n x29, other arithmetic, advance(): jnp.where(low_side, jnp.concatenate([self.held, self.other], dim), jnp.co...  62.8 us
    dot_general x11, matrix products, dot_plain(): return jnp.dot(former, latter, preferred_element_type=jnp.float32)  51.3 us
    dot_general x18, matrix products, dot_inner(): lax.dot_general(former, latter, (((0,), (0,)), ((), ())), preferred_eleme...  47.1 us
    dot_general x9, matrix products, dot_outer(): lax.dot_general(former, latter, (((1,), (1,)), ((), ())), preferred_eleme...  45.6 us
    dynamic_slice x25, local copies, waits for them, and re-layouts, send(): lax.dynamic_index_in_dim(self.held, 1 - side, dim, True)  27.2 us
    pallas_call x2, Pallas kernels, attend(): pl.pallas_call(attend_kernel, grid_spec=pltpu.PrefetchScalarGridSpec(num_...  25.2 us
  transfers between devices with their start and end apart: 78, of which 18 were waited for; matrix products, arithmetic and copies ran while one was open for 41% of the time, Pallas kernels for 6%

profile of v4, /device:TPU:0, one launch (start us, length us, event | category | flops | bytes accessed | tf_op | source)
XLA Modules:
  0.0 829.8 jit_solution(560729424960023085)
XLA Ops:
  39.1 8.0 all-to-all-done.2
  87.1 16.7 %all-to-all-start.3 = ((bf16[32,32,768]{2,1,0:T(8,128)(2,1)}), bf16[32,32,768]{2,1,0:T(8,128)(2,1)}, u32[]{:S(2)}, u32[]{:S(2)}) async-start(bf16[32,32,768]{2,1,0:T(8,128)(2,1)} %bitcast.348), calls=%async_computation.3 | async-start | bytes 3145728 | tf_op jit(solution)/shard_map/all_to_all | solution.py:617
  108.9 19.8 %collective-permute-done.15 = bf16[1,1,2,2,1,24,3072]{6,5,4,3,2,1,0:T(8,128)(2,1)S(1)} collective-permute-done((bf16[1,1,2,2,1,24,3072]{6,5,4,3,2,1,0:T(8,128)(2,1)S(1)}, bf16[1,1,2,2,1,24,3072]{6,5,4,3,2,1,0:T(8,128)(2,1)S(1)}, u32[]{:S(2)}, u32[]{:S(2)}) %collective-permute-start.15) | collective-permute-done | bytes 589856 | tf_op jit(solution)/shard_map/ppermute | solution.py:443
  144.7 7.1 collective-permute-done.11
  195.0 12.6 %shard_map.475 = (bf16[512,768]{1,0:T(8,128)(2,1)S(1)}, f32[6,2,512]{2,1,0:T(2,128)S(1)}) custom-call(s32[1]{0:T(128)} %bitcast.32.live_ref, bf16[512,2304]{1,0:T(8,128)(2,1)S(1)} %fusion.26.q_ref.k_ref.v_ref, bf16[512,2304]{1,0:T(8,128)(2,1)S(1)} %fusion.26.q_ref.k_ref.v_ref, bf16[512,2304]{1,0:T(8,128)(2,1)S(1)} %fusion.26.q_ref.k_ref.v_ref), custom_call_target="tpu_custom_call" | custom-call | tf_op jit(solution)/shard_map/pallas_call | solution.py:151
  239.1 12.6 %shard_map.476 = (bf16[512,768]{1,0:T(8,128)(2,1)S(1)}, f32[6,2,512]{2,1,0:T(2,128)S(1)}) custom-call(s32[1]{0:T(128)} %bitcast.32.live_ref, bf16[512,2304]{1,0:T(8,128)(2,1)S(1)} %fusion.27.q_ref.k_ref.v_ref, bf16[512,2304]{1,0:T(8,128)(2,1)S(1)} %fusion.27.q_ref.k_ref.v_ref, bf16[512,2304]{1,0:T(8,128)(2,1)S(1)} %fusion.27.q_ref.k_ref.v_ref), custom_call_target="tpu_custom_call" | custom-call | tf_op jit(solution)/shard_map/pallas_call | solution.py:151
  251.7 16.1 %collective-permute-done.25 = bf16[1,1,2,2,2,96,768]{6,5,4,3,2,1,0:T(8,128)(2,1)S(1)} collective-permute-done((bf16[1,1,2,2,2,96,768]{6,5,4,3,2,1,0:T(8,128)(2,1)S(1)}, bf16[1,1,2,2,2,96,768]{6,5,4,3,2,1,0:T(8,128)(2,1)S(1)}, u32[]{:S(2)}, u32[]{:S(2)}) %collective-permute-start.25) | collective-permute-done | bytes 1179680 | tf_op jit(solution)/shard_map/ppermute | solution.py:443
  269.7 7.6 maximum_select_fusion.1
  303.3 11.2 %collective-permute-done.28 = bf16[1,1,1,128,768]{4,3,2,1,0:T(8,128)(2,1)S(1)} collective-permute-done((bf16[1,1,1,128,768]{4,3,2,1,0:T(8,128)(2,1)S(1)}, bf16[1,1,1,128,768]{4,3,2,1,0:T(8,128)(2,1)S(1)}, u32[]{:S(2)}, u32[]{:S(2)}) %collective-permute-start.28) | collective-permute-done | bytes 196640 | tf_op jit(solution)/shard_map/ppermute | solution.py:443
  317.0 8.7 %collective-permute-done.29 = bf16[2,1,1,128,768]{4,3,2,1,0:T(8,128)(2,1)S(1)} collective-permute-done((bf16[2,1,1,128,768]{4,3,2,1,0:T(8,128)(2,1)S(1)}, bf16[2,1,1,128,768]{4,3,2,1,0:T(8,128)(2,1)S(1)}, u32[]{:S(2)}, u32[]{:S(2)}) %collective-permute-start.29) | collective-permute-done | bytes 393248 | tf_op jit(solution)/shard_map/ppermute | solution.py:443
  326.2 8.0 maximum_select_fusion
  334.2 10.3 %collective-permute-done.30 = bf16[2,2,1,128,768]{4,3,2,1,0:T(8,128)(2,1)S(1)} collective-permute-done((bf16[2,2,1,128,768]{4,3,2,1,0:T(8,128)(2,1)S(1)}, bf16[2,2,1,128,768]{4,3,2,1,0:T(8,128)(2,1)S(1)}, u32[]{:S(2)}, u32[]{:S(2)}) %collective-permute-start.30) | collective-permute-done | bytes 786464 | tf_op jit(solution)/shard_map/ppermute | solution.py:443
  344.8 14.2 %add_reduce_fusion = (f32[1024]{0:T(1024)S(1)}, f32[1024,6336]{0,1:T(8,128)}) fusion(f32[6336]{0:T(1024)S(1)} %copy-done.120, bf16[1024,768]{1,0:T(8,128)(2,1)S(1)} %bitcast.398, bf16[6336,768]{1,0:T(8,128)(2,1)S(1)} %bitcast.345), kind=kOutput, calls=%fused_computation.32 | convolution fusion | flops 9978641408 | bytes 37286656 | tf_op jit(solution)/shard_map/dot_general | solution.py:39
  359.0 16.6 %select_reduce_fusion.2 = (f32[1024]{0:T(1024)S(1)}, f32[1024]{0:T(1024)S(1)}, bf16[1024,6336]{0,1:T(8,128)(2,1)}) fusion(f32[1024,6336]{0,1:T(8,128)} %get-tuple-element.611, s32[1024]{0:T(1024)S(1)} %copy-done.132, f32[6336]{0:T(1024)S(1)} %copy-done.120, f32[1024]{0:T(1024)S(1)} %get-tuple-element.610), kind=kLoop, calls=%fused_computation.27 | loop fusion | flops 45414400 | bytes 38970112 | tf_op jit(solution)/shard_map/reduce_sum | solution.py:673
  379.9 17.4 %fusion.193 = f32[1024,768]{1,0:T(8,128)} fusion(bf16[1024,6336]{0,1:T(8,128)(2,1)} %get-tuple-element.314, bf16[6336,768]{1,0:T(8,128)(2,1)} %bitcast.346), kind=kOutput, calls=%fused_computation.580 | convolution fusion | flops 9965666304 | bytes 25853952 | tf_op jit(solution)/shard_map/dot_general | solution.py:29
  402.5 9.3 %subtract_convert_fusion = bf16[1024,6336]{0,1:T(8,128)(2,1)S(1)} fusion(bf16[1024,6336]{0,1:T(8,128)(2,1)} %get-tuple-element.314, f32[1024]{0:T(1024)S(1)} %get-tuple-element.591, f32[1024]{0:T(1024)S(1)} %get-tuple-element.590, s32[1024]{0:T(1024)S(1)} %copy-done.132), kind=kLoop, calls=%fused_computation.26 | loop fusion | flops 38928384 | bytes 25964544 | tf_op jit(solution)/shard_map/convert_element_type | solution.py:690
  411.8 6.9 convolution_convert_fusion
  420.6 7.3 convolution_convert_fusion.1
  452.6 6.5 fusion.24
  491.5 11.7 %shard_map.477 = bf16[512,2304]{1,0:T(8,128)(2,1)S(1)} custom-call(s32[1]{0:T(128)} %bitcast.32.live_ref, bf16[512,2304]{1,0:T(8,128)(2,1)S(1)} %copy-done.3, bf16[512,2304]{1,0:T(8,128)(2,1)S(1)} %copy-done.3, bf16[512,2304]{1,0:T(8,128)(2,1)S(1)} %copy-done.3, bf16[512,768]{1,0:T(8,128)(2,1)S(1)} %convolution_convert_fusion.9.grad_ref, ...), custom_call_target="tpu_custom_call" | custom-call | tf_op jit(solution)/shard_map/pallas_call | solution.py:180
  520.0 9.3 %collective-permute-done.42 = bf16[1,2,2,1,96,768]{5,4,3,2,1,0:T(8,128)(2,1)S(1)} collective-permute-done((bf16[1,2,2,1,96,768]{5,4,3,2,1,0:T(8,128)(2,1)S(1)}, bf16[1,2,2,1,96,768]{5,4,3,2,1,0:T(8,128)(2,1)S(1)}, u32[]{:S(2)}, u32[]{:S(2)}) %collective-permute-start.42) | collective-permute-done | bytes 589856 | tf_op jit(solution)/shard_map/ppermute | solution.py:443
  537.3 8.6 %fusion.17 = bf16[512,3072]{1,0:T(8,128)(2,1)S(1)} fusion(f32[512,3072]{1,0:T(8,128)} %get-tuple-element.603, f32[3072]{0:T(1024)S(1)} %bitcast.435, bf16[512,768]{1,0:T(8,128)(2,1)S(1)} %get-tuple-element.483, bf16[3072,768]{1,0:T(8,128)(2,1)S(1)} %bitcast.368), kind=kOutput, calls=%fused_computation.52 | convolution fusion | flops 2448949248 | bytes 14954496 | tf_op jit(solution)/shard_map/dot_general | solution.py:39
  579.5 11.5 %shard_map.478 = bf16[512,2304]{1,0:T(8,128)(2,1)S(1)} custom-call(s32[1]{0:T(128)} %bitcast.32.live_ref, bf16[512,2304]{1,0:T(8,128)(2,1)S(1)} %copy-done.1, bf16[512,2304]{1,0:T(8,128)(2,1)S(1)} %copy-done.1, bf16[512,2304]{1,0:T(8,128)(2,1)S(1)} %copy-done.1, bf16[512,768]{1,0:T(8,128)(2,1)S(1)} %convolution_convert_fusion.8.grad_ref, ...), custom_call_target="tpu_custom_call" | custom-call | tf_op jit(solution)/shard_map/pallas_call | solution.py:180
  612.2 12.9 %collective-permute-done.50 = bf16[1,1,384,768]{3,2,1,0:T(8,128)(2,1)S(1)} collective-permute-done((bf16[1,1,384,768]{3,2,1,0:T(8,128)(2,1)}, bf16[1,1,384,768]{3,2,1,0:T(8,128)(2,1)S(1)}, u32[]{:S(2)}, u32[]{:S(2)}) %collective-permute-start.50) | collective-permute-done | bytes 589856 | tf_op jit(solution)/shard_map/ppermute | solution.py:443
  641.0 6.3 collective-permute-done.55
  649.1 8.5 %collective-permute-start.62 = (bf16[1,2,2,2,32,768]{5,4,3,2,1,0:T(8,128)(2,1)}, bf16[1,2,2,2,32,768]{5,4,3,2,1,0:T(8,128)(2,1)}, u32[]{:S(2)}, u32[]{:S(2)}) collective-permute-start(bf16[1,2,2,2,32,768]{5,4,3,2,1,0:T(8,128)(2,1)} %constant_dynamic-slice_fusion.12), channel_id=1, source_target_pairs={{0,8},{8,0},{1,9},{9,1},{2,10},{10,2},{3,11},{11,3},{4,12},{12,4},... | collective-permute-start | bytes 1179656 | tf_op jit(solution)/shard_map/ppermute | solution.py:443
  680.3 45.5 %collective-permute-done.61 = bf16[1,2,96,1152]{3,2,1,0:T(8,128)(2,1)S(1)} collective-permute-done((bf16[1,2,96,1152]{3,2,1,0:T(8,128)(2,1)S(1)}, bf16[1,2,96,1152]{3,2,1,0:T(8,128)(2,1)S(1)}, u32[]{:S(2)}, u32[]{:S(2)}) %collective-permute-start.61) | collective-permute-done | bytes 442400 | tf_op jit(solution)/shard_map/ppermute | solution.py:443
  735.9 6.5 bitcast_add_fusion
  758.0 15.9 %collective-permute-done.67 = bf16[1,1,1,1,32,768]{5,4,3,2,1,0:T(8,128)(2,1)S(1)} collective-permute-done((bf16[1,1,1,1,32,768]{5,4,3,2,1,0:T(8,128)(2,1)S(1)}, bf16[1,1,1,1,32,768]{5,4,3,2,1,0:T(8,128)(2,1)S(1)}, u32[]{:S(2)}, u32[]{:S(2)}) %collective-permute-start.67) | collective-permute-done | bytes 49184 | tf_op jit(solution)/shard_map/ppermute | solution.py:443
  787.7 8.8 %all_to_all.68 = f32[32,1,128]{2,1,0:T(1,128)S(1)} all-to-all(f32[32,1,128]{2,1,0:T(1,128)S(1)} %broadcast_in_dim.311), channel_id=1, replica_groups=mesh['pair'=2,'core'=2,'s0'=2,'s1'=2,'s2'=2] {'pair','core','s0','s1','s2'}, dimensions={0} | all-to-all | bytes 32768 | tf_op jit(solution)/shard_map/all_to_all | solution.py:840
  799.1 6.9 multiply_subtract_fusion.1
  807.8 8.6 %multiply_subtract_fusion = (f32[1572,768]{1,0:T(8,128)}, f32[1572,768]{1,0:T(8,128)}, f32[1572,768]{1,0:T(8,128)}) fusion(f32[1572,768]{1,0:T(8,128)S(1)} %bitcast.340, f32[1572,768]{1,0:T(8,128)S(1)} %bitcast.342, f32[]{:T(128)S(6)} %min.3, f32[1572,768]{1,0:T(8,128)S(1)} %bitcast.356, f32[1572,768]{1,0:T(8,128)} %param.38), kind=kLoop, calls=%fused_computation.70 | loop fusion | flops 18109440 | bytes 33804292 | tf_op jit(solution)/shard_map/sub | solution.py:435
  (906 shorter events, 424.0 us)
Async XLA Ops:
  9.1 38.3 %collective-permute-start.1 = (bf16[1,1,1,1,1,24,3072]{6,5,4,3,2,1,0:T(8,128)(2,1)}, bf16[1,1,1,1,1,24,3072]{6,5,4,3,2,1,0:T(8,128)(2,1)}, u32[]{:S(2)}, u32[]{:S(2)}) collective-permute-start(bf16[1,1,1,1,1,24,3072]{6,5,4,3,2,1,0:T(8,128)(2,1)} %slice_bitcast_fusion.3), channel_id=1, source_target_pairs={{0,4},{4,0},{1,5},{5,1},{2,6},{6,2},{3,7},{7,3},{8,12},{12,8},{9,1... | collective-permute-start | bytes 442376 | tf_op jit(solution)/shard_map/ppermute | solution.py:443
  16.9 30.6 %collective-permute-start = (bf16[96,3072]{1,0:T(8,128)(2,1)}, bf16[96,3072]{1,0:T(8,128)(2,1)}, u32[]{:S(2)}, u32[]{:S(2)}) collective-permute-start(bf16[96,3072]{1,0:T(8,128)(2,1)} %slice.336), channel_id=1, source_target_pairs={{4,8},{8,4},{5,9},{9,5},{6,10},{10,6},{7,11},{11,7},{20,24},{24,20... | collective-permute-start | bytes 1769480 | tf_op jit(solution)/shard_map/ppermute | solution.py:539
  30.2 153.9 %all-gather.2.cloned.1.call-start = ((), (), s32[]{:S(2)}) async-start(), calls=%async_computation.8 | async-start | bytes 1622016 | tf_op jit(solution)/shard_map/all_gather | solution.py:551
  31.8 145.9 %collective-permute-start.2 = (bf16[1,1,1584,768]{3,2,1,0:T(8,128)(2,1)}, bf16[1,1,1584,768]{3,2,1,0:T(8,128)(2,1)}, u32[]{:S(2)}, u32[]{:S(2)}) collective-permute-start(bf16[1,1,1584,768]{3,2,1,0:T(8,128)(2,1)} %pad_bitcast_fusion), channel_id=1, source_target_pairs={{0,16},{16,0},{1,17},{17,1},{2,18},{18,2},{3,19},{19,3},{4,20},{20... | collective-permute-start | bytes 7299080 | tf_op jit(solution)/shard_map/ppermute | solution.py:443
  52.5 28.8 %collective-permute-start.5 = (bf16[1,1,1,96,3072]{4,3,2,1,0:T(8,128)(2,1)}, bf16[1,1,1,96,3072]{4,3,2,1,0:T(8,128)(2,1)}, u32[]{:S(2)}, u32[]{:S(2)}) collective-permute-start(bf16[1,1,1,96,3072]{4,3,2,1,0:T(8,128)(2,1)} %get-tuple-element.267), channel_id=1, source_target_pairs={{0,1},{1,0},{2,3},{3,2},{4,5},{5,4},{6,7},{7,6},{8,9},{9,8},{10,11... | collective-permute-start | bytes 1769480 | tf_op jit(solution)/shard_map/ppermute | solution.py:443
  76.1 63.6 %collective-permute-start.10 = (bf16[1,1,1,1,1,24,3072]{6,5,4,3,2,1,0:T(8,128)(2,1)}, bf16[1,1,1,1,1,24,3072]{6,5,4,3,2,1,0:T(8,128)(2,1)}, u32[]{:S(2)}, u32[]{:S(2)}) collective-permute-start(bf16[1,1,1,1,1,24,3072]{6,5,4,3,2,1,0:T(8,128)(2,1)} %slice_bitcast_fusion.4), channel_id=1, source_target_pairs={{0,4},{4,0},{1,5},{5,1},{2,6},{6,2},{3,7},{7,3},{8,12},{12,8},{9,1... | collective-permute-start | bytes 442376 | tf_op jit(solution)/shard_map/ppermute | solution.py:443
  82.2 71.9 %collective-permute-start.9 = (bf16[1,1,1,384,768]{4,3,2,1,0:T(8,128)(2,1)}, bf16[1,1,1,384,768]{4,3,2,1,0:T(8,128)(2,1)}, u32[]{:S(2)}, u32[]{:S(2)}) collective-permute-start(bf16[1,1,1,384,768]{4,3,2,1,0:T(8,128)(2,1)} %select_bitcast_fusion), channel_id=1, source_target_pairs={{0,2},{2,0},{1,3},{3,1},{4,6},{6,4},{5,7},{7,5},{8,10},{10,8},{9,1... | collective-permute-start | bytes 1769480 | tf_op jit(solution)/shard_map/ppermute | solution.py:443
  85.9 68.3 %collective-permute-start.7 = (bf16[1,1,2,96,3072]{4,3,2,1,0:T(8,128)(2,1)}, bf16[1,1,2,96,3072]{4,3,2,1,0:T(8,128)(2,1)}, u32[]{:S(2)}, u32[]{:S(2)}) collective-permute-start(bf16[1,1,2,96,3072]{4,3,2,1,0:T(8,128)(2,1)} %maximum_select_fusion.15), channel_id=1, source_target_pairs={{0,2},{2,0},{1,3},{3,1},{4,6},{6,4},{5,7},{7,5},{8,10},{10,8},{9,1... | collective-permute-start | bytes 3538952 | tf_op jit(solution)/shard_map/ppermute | solution.py:443
  87.1 91.0 %all-to-all-start.3 = ((bf16[32,32,768]{2,1,0:T(8,128)(2,1)}), bf16[32,32,768]{2,1,0:T(8,128)(2,1)}, u32[]{:S(2)}, u32[]{:S(2)}) async-start(bf16[32,32,768]{2,1,0:T(8,128)(2,1)} %bitcast.348), calls=%async_computation.3 | async-start | bytes 3145728 | tf_op jit(solution)/shard_map/all_to_all | solution.py:617
  151.8 55.9 %collective-permute-start.16 = (bf16[1,1,2,2,2,24,3072]{6,5,4,3,2,1,0:T(8,128)(2,1)}, bf16[1,1,2,2,2,24,3072]{6,5,4,3,2,1,0:T(8,128)(2,1)}, u32[]{:S(2)}, u32[]{:S(2)}) collective-permute-start(bf16[1,1,2,2,2,24,3072]{6,5,4,3,2,1,0:T(8,128)(2,1)} %maximum_select_fusion.18), channel_id=1, source_target_pairs={{0,16},{16,0},{1,17},{17,1},{2,18},{18,2},{3,19},{19,3},{4,20},{20... | collective-permute-start | bytes 3538952 | tf_op jit(solution)/shard_map/ppermute | solution.py:443
  162.6 45.1 %collective-permute-start.14 = (bf16[1,2,1,384,768]{4,3,2,1,0:T(8,128)(2,1)}, bf16[1,2,1,384,768]{4,3,2,1,0:T(8,128)(2,1)}, u32[]{:S(2)}, u32[]{:S(2)}) collective-permute-start(bf16[1,2,1,384,768]{4,3,2,1,0:T(8,128)(2,1)} %maximum_select_fusion.17), channel_id=1, source_target_pairs={{0,1},{1,0},{2,3},{3,2},{4,5},{5,4},{6,7},{7,6},{8,9},{9,8},{10,11... | collective-permute-start | bytes 3538952 | tf_op jit(solution)/shard_map/ppermute | solution.py:443
  173.1 34.6 %collective-permute-start.13 = (bf16[1,1,2,96,3072]{4,3,2,1,0:T(8,128)(2,1)}, bf16[1,1,2,96,3072]{4,3,2,1,0:T(8,128)(2,1)}, u32[]{:S(2)}, u32[]{:S(2)}) collective-permute-start(bf16[1,1,2,96,3072]{4,3,2,1,0:T(8,128)(2,1)} %maximum_select_fusion.16), channel_id=1, source_target_pairs={{0,2},{2,0},{1,3},{3,1},{4,6},{6,4},{5,7},{7,5},{8,10},{10,8},{9,1... | collective-permute-start | bytes 3538952 | tf_op jit(solution)/shard_map/ppermute | solution.py:443
  177.7 30.0 %collective-permute-start.19 = (bf16[1,1,2,2,1,24,3072]{6,5,4,3,2,1,0:T(8,128)(2,1)}, bf16[1,1,2,2,1,24,3072]{6,5,4,3,2,1,0:T(8,128)(2,1)}, u32[]{:S(2)}, u32[]{:S(2)}) collective-permute-start(bf16[1,1,2,2,1,24,3072]{6,5,4,3,2,1,0:T(8,128)(2,1)} %maximum_select_fusion.23), channel_id=1, source_target_pairs={{0,1},{1,0},{2,3},{3,2},{4,5},{5,4},{6,7},{7,6},{8,9},{9,8},{10,11... | collective-permute-start | bytes 1769480 | tf_op jit(solution)/shard_map/ppermute | solution.py:443
  214.5 37.3 %collective-permute-start.24 = (bf16[1,1,2,2,2,24,3072]{6,5,4,3,2,1,0:T(8,128)(2,1)S(1)}, bf16[1,1,2,2,2,24,3072]{6,5,4,3,2,1,0:T(8,128)(2,1)S(1)}, u32[]{:S(2)}, u32[]{:S(2)}) collective-permute-start(bf16[1,1,2,2,2,24,3072]{6,5,4,3,2,1,0:T(8,128)(2,1)S(1)} %maximum_select_fusion.19), channel_id=1, source_target_pairs={{0,16},{16,0},{1,17},{17,1},{2,18},{18,2},{3,19},{19,3},{4,20},{20... | collective-permute-start | bytes 3538952 | tf_op jit(solution)/shard_map/ppermute | solution.py:443
  229.5 38.4 %collective-permute-start.25 = (bf16[1,1,2,2,2,96,768]{6,5,4,3,2,1,0:T(8,128)(2,1)S(1)}, bf16[1,1,2,2,2,96,768]{6,5,4,3,2,1,0:T(8,128)(2,1)S(1)}, u32[]{:S(2)}, u32[]{:S(2)}) collective-permute-start(bf16[1,1,2,2,2,96,768]{6,5,4,3,2,1,0:T(8,128)(2,1)S(1)} %maximum_select_fusion.20), channel_id=1, source_target_pairs={{0,16},{16,0},{1,17},{17,1},{2,18},{18,2},{3,19},{19,3},{4,20},{20... | collective-permute-start | bytes 3538952 | tf_op jit(solution)/shard_map/ppermute | solution.py:443
  277.3 48.9 %collective-permute-start.31 = (bf16[2,1,1584,768]{3,2,1,0:T(8,128)(2,1)}, bf16[2,1,1584,768]{3,2,1,0:T(8,128)(2,1)}, u32[]{:S(2)}, u32[]{:S(2)}) collective-permute-start(bf16[2,1,1584,768]{3,2,1,0:T(8,128)(2,1)} %maximum_select_fusion.1), channel_id=1, source_target_pairs={{0,8},{8,0},{1,9},{9,1},{2,10},{10,2},{3,11},{11,3},{4,12},{12,4},... | collective-permute-start | bytes 14598152 | tf_op jit(solution)/shard_map/ppermute | solution.py:443
  447.6 32.7 %collective-permute-start.37 = (bf16[1,1584,768]{2,1,0:T(8,128)(2,1)}, bf16[1,1584,768]{2,1,0:T(8,128)(2,1)}, u32[]{:S(2)}, u32[]{:S(2)}) collective-permute-start(bf16[1,1584,768]{2,1,0:T(8,128)(2,1)} %get-tuple-element.509), channel_id=1, source_target_pairs={{0,8},{8,0},{1,9},{9,1},{2,10},{10,2},{3,11},{11,3},{4,12},{12,4},... | collective-permute-start | bytes 7299080 | tf_op jit(solution)/shard_map/ppermute | solution.py:443
  465.6 37.7 %collective-permute-start.40 = (bf16[1,2,2,2,96,768]{5,4,3,2,1,0:T(8,128)(2,1)}, bf16[1,2,2,2,96,768]{5,4,3,2,1,0:T(8,128)(2,1)}, u32[]{:S(2)}, u32[]{:S(2)}) collective-permute-start(bf16[1,2,2,2,96,768]{5,4,3,2,1,0:T(8,128)(2,1)} %get-tuple-element.523), channel_id=1, source_target_pairs={{0,16},{16,0},{1,17},{17,1},{2,18},{18,2},{3,19},{19,3},{4,20},{20... | collective-permute-start | bytes 3538952 | tf_op jit(solution)/shard_map/ppermute | solution.py:443
  536.2 55.0 %collective-permute-start.48 = (bf16[1,2,2,2,24,6144]{5,4,3,2,1,0:T(8,128)(2,1)}, bf16[1,2,2,2,24,6144]{5,4,3,2,1,0:T(8,128)(2,1)}, u32[]{:S(2)}, u32[]{:S(2)}) collective-permute-start(bf16[1,2,2,2,24,6144]{5,4,3,2,1,0:T(8,128)(2,1)} %get-tuple-element.511), channel_id=1, source_target_pairs={{0,16},{16,0},{1,17},{17,1},{2,18},{18,2},{3,19},{19,3},{4,20},{20... | collective-permute-start | bytes 7077896 | tf_op jit(solution)/shard_map/ppermute | solution.py:443
  562.4 30.0 %collective-permute-start.49 = (bf16[2,1,384,768]{3,2,1,0:T(8,128)(2,1)}, bf16[2,1,384,768]{3,2,1,0:T(8,128)(2,1)}, u32[]{:S(2)}, u32[]{:S(2)}) collective-permute-start(bf16[2,1,384,768]{3,2,1,0:T(8,128)(2,1)} %get-tuple-element.521), channel_id=1, source_target_pairs={{0,1},{1,0},{2,3},{3,2},{4,5},{5,4},{6,7},{7,6},{8,9},{9,8},{10,11... | collective-permute-start | bytes 3538952 | tf_op jit(solution)/shard_map/ppermute | solution.py:443
  577.6 47.4 %collective-permute-start.51 = (bf16[1,2,96,3840]{3,2,1,0:T(8,128)(2,1)}, bf16[1,2,96,3840]{3,2,1,0:T(8,128)(2,1)}, u32[]{:S(2)}, u32[]{:S(2)}) collective-permute-start(bf16[1,2,96,3840]{3,2,1,0:T(8,128)(2,1)} %get-tuple-element.517), channel_id=1, source_target_pairs={{0,2},{2,0},{1,3},{3,1},{4,6},{6,4},{5,7},{7,5},{8,10},{10,8},{9,1... | collective-permute-start | bytes 4423688 | tf_op jit(solution)/shard_map/ppermute | solution.py:443
  595.6 29.5 %collective-permute-start.50 = (bf16[1,1,384,768]{3,2,1,0:T(8,128)(2,1)}, bf16[1,1,384,768]{3,2,1,0:T(8,128)(2,1)S(1)}, u32[]{:S(2)}, u32[]{:S(2)}) collective-permute-start(bf16[1,1,384,768]{3,2,1,0:T(8,128)(2,1)} %get-tuple-element.533), channel_id=1, source_target_pairs={{0,2},{2,0},{1,3},{3,1},{4,6},{6,4},{5,7},{7,5},{8,10},{10,8},{9,1... | collective-permute-start | bytes 1769480 | tf_op jit(solution)/shard_map/ppermute | solution.py:443
  600.6 40.4 %collective-permute-start.53 = (bf16[1,2,2,1,24,6144]{5,4,3,2,1,0:T(8,128)(2,1)}, bf16[1,2,2,1,24,6144]{5,4,3,2,1,0:T(8,128)(2,1)}, u32[]{:S(2)}, u32[]{:S(2)}) collective-permute-start(bf16[1,2,2,1,24,6144]{5,4,3,2,1,0:T(8,128)(2,1)} %get-tuple-element.519), channel_id=1, source_target_pairs={{0,1},{1,0},{2,3},{3,2},{4,5},{5,4},{6,7},{7,6},{8,9},{9,8},{10,11... | collective-permute-start | bytes 3538952 | tf_op jit(solution)/shard_map/ppermute | solution.py:443
  603.5 34.9 %collective-permute-start.52 = (bf16[384,2304]{1,0:T(8,128)(2,1)}, bf16[384,2304]{1,0:T(8,128)(2,1)}, u32[]{:S(2)}, u32[]{:S(2)}) collective-permute-start(bf16[384,2304]{1,0:T(8,128)(2,1)} %convolution_convert_fusion.2), channel_id=1, source_target_pairs={{0,8},{8,0},{1,9},{9,1},{2,10},{10,2},{3,11},{11,3},{4,12},{12,4},... | collective-permute-start | bytes 5308424 | tf_op jit(solution)/shard_map/ppermute | solution.py:443
  606.1 69.7 %collective-permute-start.57 = (bf16[1,1584,768]{2,1,0:T(8,128)(2,1)}, bf16[1,1584,768]{2,1,0:T(8,128)(2,1)}, u32[]{:S(2)}, u32[]{:S(2)}) collective-permute-start(bf16[1,1584,768]{2,1,0:T(8,128)(2,1)} %get-tuple-element.505), channel_id=1, source_target_pairs={{0,16},{16,0},{1,17},{17,1},{2,18},{18,2},{3,19},{19,3},{4,20},{20... | collective-permute-start | bytes 7299080 | tf_op jit(solution)/shard_map/ppermute | solution.py:443
  658.8 67.0 %collective-permute-start.60 = (bf16[2,1,112,1152]{3,2,1,0:T(8,128)(2,1)}, bf16[2,1,112,1152]{3,2,1,0:T(8,128)(2,1)}, u32[]{:S(2)}, u32[]{:S(2)}) collective-permute-start(bf16[2,1,112,1152]{3,2,1,0:T(8,128)(2,1)} %get-tuple-element.539), channel_id=1, source_target_pairs={{0,1},{1,0},{2,3},{3,2},{4,5},{5,4},{6,7},{7,6},{8,9},{9,8},{10,11... | collective-permute-start | bytes 1548296 | tf_op jit(solution)/shard_map/ppermute | solution.py:443
  663.0 62.9 %all-to-all-start.6 = ((bf16[32,32,768]{2,1,0:T(8,128)(2,1)}), bf16[32,32,768]{2,1,0:T(8,128)(2,1)}, u32[]{:S(2)}, u32[]{:S(2)}) async-start(bf16[32,32,768]{2,1,0:T(8,128)(2,1)} %bitcast.397), calls=%async_computation.6 | async-start | bytes 3145728 | tf_op jit(solution)/shard_map/all_to_all | solution.py:801
  669.1 56.8 %collective-permute-start.58 = (bf16[1,1,96,3840]{3,2,1,0:T(8,128)(2,1)S(1)}, bf16[1,1,96,3840]{3,2,1,0:T(8,128)(2,1)}, u32[]{:S(2)}, u32[]{:S(2)}) collective-permute-start(bf16[1,1,96,3840]{3,2,1,0:T(8,128)(2,1)S(1)} %add_convert_fusion.16), channel_id=1, source_target_pairs={{4,8},{8,4},{5,9},{9,5},{6,10},{10,6},{7,11},{11,7},{20,24},{24,20... | collective-permute-start | bytes 2211848 | tf_op jit(solution)/shard_map/ppermute | solution.py:725
  672.3 53.5 %collective-permute-start.56 = (bf16[1,2,1,1,24,6144]{5,4,3,2,1,0:T(8,128)(2,1)S(1)}, bf16[1,2,1,1,24,6144]{5,4,3,2,1,0:T(8,128)(2,1)}, u32[]{:S(2)}, u32[]{:S(2)}) collective-permute-start(bf16[1,2,1,1,24,6144]{5,4,3,2,1,0:T(8,128)(2,1)S(1)} %get-tuple-element.531), channel_id=1, source_target_pairs={{0,2},{2,0},{1,3},{3,1},{4,6},{6,4},{5,7},{7,5},{8,10},{10,8},{9,1... | collective-permute-start | bytes 1769480 | tf_op jit(solution)/shard_map/ppermute | solution.py:443
  674.2 51.7 %collective-permute-start.61 = (bf16[1,2,96,1152]{3,2,1,0:T(8,128)(2,1)S(1)}, bf16[1,2,96,1152]{3,2,1,0:T(8,128)(2,1)S(1)}, u32[]{:S(2)}, u32[]{:S(2)}) collective-permute-start(bf16[1,2,96,1152]{3,2,1,0:T(8,128)(2,1)S(1)} %get-tuple-element.541), channel_id=1, source_target_pairs={{0,2},{2,0},{1,3},{3,1},{4,6},{6,4},{5,7},{7,5},{8,10},{10,8},{9,1... | collective-permute-start | bytes 1327112 | tf_op jit(solution)/shard_map/ppermute | solution.py:443
  675.8 50.0 %collective-permute-start.63 = (bf16[1,2,2,1,32,768]{5,4,3,2,1,0:T(8,128)(2,1)S(1)}, bf16[1,2,2,1,32,768]{5,4,3,2,1,0:T(8,128)(2,1)S(1)}, u32[]{:S(2)}, u32[]{:S(2)}) collective-permute-start(bf16[1,2,2,1,32,768]{5,4,3,2,1,0:T(8,128)(2,1)S(1)} %get-tuple-element.565), channel_id=1, source_target_pairs={{0,1},{1,0},{2,3},{3,2},{4,5},{5,4},{6,7},{7,6},{8,9},{9,8},{10,11... | collective-permute-start | bytes 589832 | tf_op jit(solution)/shard_map/ppermute | solution.py:443
  752.4 30.6 %collective-permute-start.70 = (bf16[1,1,112,1152]{3,2,1,0:T(8,128)(2,1)S(1)}, bf16[1,1,112,1152]{3,2,1,0:T(8,128)(2,1)}, u32[]{:S(2)}, u32[]{:S(2)}) collective-permute-start(bf16[1,1,112,1152]{3,2,1,0:T(8,128)(2,1)S(1)} %add_convert_fusion.25), channel_id=1, source_target_pairs={{4,8},{8,4},{5,9},{9,5},{6,10},{10,6},{7,11},{11,7},{20,24},{24,20... | collective-permute-start | bytes 774152 | tf_op jit(solution)/shard_map/ppermute | solution.py:725
  (249 other events, 2795.0 us)
Sparse Core Ops, SparseCore 0:
  34.5 66.7 all-gather.1
